TPU v7x, 32 devices: a whole 2x2x4 slice. The times are simulated.
32 devices in a mesh: ctx: 4 (over y, x), fsdp: 8 (over z, core).
Axes of the slice: x: 2, y: 2, z: 4, core: 2. Of those that a mesh axis runs over, the one named last changes fastest.
Arguments:
- tokens: bfloat16 [1024, 16, 768], P('ctx', 'fsdp'), may hold values from -6 to 6
- norm1_gain: bfloat16 [768], P('fsdp'), may hold values from 0.5 to 1.5
- norm1_bias: bfloat16 [768], P('fsdp'), may hold values from -4 to 4
- norm2_gain: bfloat16 [768], P('fsdp'), may hold values from 0.5 to 1.5
- norm2_bias: bfloat16 [768], P('fsdp'), may hold values from -4 to 4
- qkv_weight: bfloat16 [768, 2304], P('fsdp'), may hold values from -0.3125 to 0.3125
- qkv_bias: bfloat16 [2304], P('fsdp'), may hold values from -6 to 6
- out_weight: bfloat16 [768, 768], P('fsdp'), may hold values from -0.4375 to 0.4375
- out_bias: bfloat16 [768], P('fsdp'), may hold values from -6 to 6
- up_weight: bfloat16 [768, 3072], P('fsdp'), may hold values from -0.21875 to 0.21875
- up_bias: bfloat16 [3072], P('fsdp'), may hold values from -6 to 6
- down_weight: bfloat16 [3072, 768], P('fsdp'), may hold values from -0.15625 to 0.15625
- down_bias: bfloat16 [768], P('fsdp'), may hold values from -6 to 6
- cotangent: bfloat16 [1024, 16, 768], P('ctx', 'fsdp'), may hold values from -6 to 6
Outputs:
- layer_out: bfloat16 [1024, 16, 768], P('ctx', 'fsdp')
- tokens_grad: bfloat16 [1024, 16, 768], P('ctx', 'fsdp')
- norm1_gain_grad: float32 [768], P('fsdp')
- norm1_bias_grad: float32 [768], P('fsdp')
- norm2_gain_grad: float32 [768], P('fsdp')
- norm2_bias_grad: float32 [768], P('fsdp')
- qkv_weight_grad: float32 [768, 2304], P('fsdp')
- qkv_bias_grad: float32 [2304], P('fsdp')
- out_weight_grad: float32 [768, 768], P('fsdp')
- out_bias_grad: float32 [768], P('fsdp')
- up_weight_grad: float32 [768, 3072], P('fsdp')
- up_bias_grad: float32 [3072], P('fsdp')
- down_weight_grad: float32 [3072, 768], P('fsdp')
- down_bias_grad: float32 [768], P('fsdp')
All inputs are finite; a program needn't handle non-finite values.
Results may differ from a plain program's by a relative error of at most 0.012.
The roundings to bfloat16 on the way count: a program that leaves them out, or rounds other values in their place, can miss the bound.
Values may be sent and summed in bfloat16 or wider, within the bound.
No kernel may reach another device: no remote copies, remote signals or barrier semaphores. Data moves between devices by JAX's collectives and lax.ppermute only.
A program may use at most 256 MiB of HBM per device.

v0:
```python
import jax
import jax.numpy as jnp
from jax import lax
from jax.sharding import PartitionSpec as P

H = 12
HD = 64
ROT = 16


epsilon = 1e-05
masked_score = -1e30


def layer_norm(inputs, gain_vec, bias_vec):
    center = inputs - jnp.mean(inputs, axis=-1, keepdims=True)
    spread = jnp.mean(center * center, axis=-1, keepdims=True)
    return center * lax.rsqrt(spread + epsilon) * gain_vec + bias_vec


def exact_gelu(values_in):
    return jax.nn.gelu(values_in, approximate=False)


def angles(positions):
    inverse = 10000.0 ** (-jnp.arange(0, ROT, 2, dtype=jnp.float32) / ROT)
    phase = positions[:, None] * inverse[None, :]
    phase = jnp.concatenate([phase, phase], axis=-1)
    return (jnp.cos(phase), jnp.sin(phase))


def rotate(values_in, cosine_table, sine_table):
    half_rot = ROT // 2
    part = values_in[..., :ROT]
    turned = jnp.concatenate([-part[..., half_rot:], part[..., :half_rot]], axis=-1)
    return jnp.concatenate(
        [part * cosine_table + turned * sine_table, values_in[..., ROT:]], axis=-1
    )


def unrotate(grads_in, cosine_table, sine_table):
    half_rot = ROT // 2
    part = grads_in[..., :ROT]
    weighted = part * sine_table
    turned_back = jnp.concatenate([weighted[..., half_rot:], -weighted[..., :half_rot]], axis=-1)
    return jnp.concatenate([part * cosine_table + turned_back, grads_in[..., ROT:]], axis=-1)


def back_dot(left, right):
    return lax.dot_general(
        left, right, (((1,), (1,)), ((), ())), preferred_element_type=jnp.float32
    )


def outer_sum(left, right):
    return lax.dot_general(
        left, right, (((0,), (0,)), ((), ())), preferred_element_type=jnp.float32
    )


def body(
    tokens,
    norm1_gain,
    norm1_bias,
    norm2_gain,
    norm2_bias,
    qkv_weight,
    qkv_bias,
    out_weight,
    out_bias,
    up_weight,
    up_bias,
    down_weight,
    down_bias,
    cotangent,
):
    block_len, seq_count, model_width = tokens.shape
    head_count = H
    head_size = HD
    row_count = block_len * seq_count
    score_scale = head_size ** (-0.5)
    gathered = (
        lax.all_gather(norm1_gain, "fsdp", axis=0, tiled=True),
        lax.all_gather(norm1_bias, "fsdp", axis=0, tiled=True),
        lax.all_gather(norm2_gain, "fsdp", axis=0, tiled=True),
        lax.all_gather(norm2_bias, "fsdp", axis=0, tiled=True),
        lax.all_gather(qkv_weight, "fsdp", axis=0, tiled=True),
        lax.all_gather(qkv_bias, "fsdp", axis=0, tiled=True),
        lax.all_gather(out_weight, "fsdp", axis=0, tiled=True),
        lax.all_gather(out_bias, "fsdp", axis=0, tiled=True),
        lax.all_gather(up_weight, "fsdp", axis=0, tiled=True),
        lax.all_gather(up_bias, "fsdp", axis=0, tiled=True),
        lax.all_gather(down_weight, "fsdp", axis=0, tiled=True),
        lax.all_gather(down_bias, "fsdp", axis=0, tiled=True),
    )
    (
        gain_one,
        bias_one,
        gain_two,
        bias_two,
        weight_qkv,
        bias_qkv,
        weight_out,
        bias_out,
        weight_up,
        bias_up,
        weight_down,
        bias_down,
    ) = gathered
    gain_one = gain_one.astype(jnp.float32)
    bias_one = bias_one.astype(jnp.float32)
    gain_two = gain_two.astype(jnp.float32)
    bias_two = bias_two.astype(jnp.float32)
    own_start = lax.axis_index("ctx") * block_len
    positions = own_start + jnp.arange(block_len, dtype=jnp.int32)
    cosine_table, sine_table = angles(positions.astype(jnp.float32))
    cosine_table = cosine_table[:, None, None, :]
    sine_table = sine_table[:, None, None, :]
    inputs = tokens.astype(jnp.float32).reshape(row_count, model_width)
    normed_one = layer_norm(inputs, gain_one, bias_one).astype(jnp.bfloat16)
    normed_two = layer_norm(inputs, gain_two, bias_two).astype(jnp.bfloat16)
    projected = jnp.dot(
        normed_one, weight_qkv, preferred_element_type=jnp.float32
    ) + bias_qkv.astype(jnp.float32)
    split = projected.reshape(block_len, seq_count, 3, head_count, head_size)
    query_rot = rotate(split[:, :, 0], cosine_table, sine_table).astype(jnp.bfloat16)
    key_rot = rotate(split[:, :, 1], cosine_table, sine_table).astype(jnp.bfloat16)
    value_low = split[:, :, 2].astype(jnp.bfloat16)
    key_flat = key_rot.reshape(block_len, seq_count, model_width)
    value_flat = value_low.reshape(block_len, seq_count, model_width)

    def key_blocks(piece_rows):
        block_total = piece_rows.shape[0] // block_len
        return (
            block_total,
            piece_rows.reshape(block_total, block_len, seq_count, head_count, head_size),
        )

    zero_heads = jnp.zeros((seq_count, head_count, block_len, head_size), jnp.float32)
    start_max = jnp.full((seq_count, head_count, block_len), masked_score, jnp.float32)
    start_sum = jnp.zeros((seq_count, head_count, block_len), jnp.float32)
    piece_rows = (
        lax.all_gather(key_flat, "ctx", axis=0, tiled=True),
        lax.all_gather(value_flat, "ctx", axis=0, tiled=True),
    )
    block_total, key_parts = key_blocks(piece_rows[0])
    _, value_parts = key_blocks(piece_rows[1])
    offsets = jnp.arange(block_total, dtype=jnp.int32) * block_len

    def attend_visit(current, block_item):
        key_blk, value_blk, offset = block_item

        def attend_update(running):
            accumulated, running_max, running_sum = running
            scores = (
                jnp.einsum(
                    "qshd,kshd->shqk", query_rot, key_blk, preferred_element_type=jnp.float32
                )
                * score_scale
            )
            allowed = (offset + jnp.arange(block_len, dtype=jnp.int32))[None, :] <= positions[
                :, None
            ]
            scores = jnp.where(allowed, scores, masked_score)
            new_max = jnp.maximum(running_max, jnp.max(scores, axis=-1))
            exps = jnp.exp(scores - new_max[..., None])
            fading = jnp.exp(running_max - new_max)
            running_sum = running_sum * fading + jnp.sum(exps, axis=-1)
            accumulated = accumulated * fading[..., None] + jnp.einsum(
                "shqk,kshd->shqd",
                exps.astype(jnp.bfloat16),
                value_blk,
                preferred_element_type=jnp.float32,
            )
            return (accumulated, new_max, running_sum)

        def attend_unchanged(running):
            return running

        return (lax.cond(offset <= own_start, attend_update, attend_unchanged, current), None)

    result, _ = lax.scan(
        attend_visit, (zero_heads, start_max, start_sum), (key_parts, value_parts, offsets)
    )
    accumulated, running_max, running_sum = result
    attended = accumulated / running_sum[..., None]
    log_total = running_max + jnp.log(running_sum)
    mixed_heads = (
        attended.transpose(2, 0, 1, 3).reshape(row_count, model_width).astype(jnp.bfloat16)
    )
    attn_branch = jnp.dot(
        mixed_heads, weight_out, preferred_element_type=jnp.float32
    ) + bias_out.astype(jnp.float32)
    hidden_pre = jnp.dot(
        normed_two, weight_up, preferred_element_type=jnp.float32
    ) + bias_up.astype(jnp.float32)
    activated = exact_gelu(hidden_pre).astype(jnp.bfloat16)
    mlp_branch = jnp.dot(
        activated, weight_down, preferred_element_type=jnp.float32
    ) + bias_down.astype(jnp.float32)
    layer_out = (
        (inputs + attn_branch + mlp_branch)
        .astype(jnp.bfloat16)
        .reshape(block_len, seq_count, model_width)
    )
    upstream = cotangent.reshape(row_count, model_width)
    upstream_f = upstream.astype(jnp.float32)
    column_sums = jnp.sum(upstream_f, axis=0)
    grad_out_w = outer_sum(mixed_heads, upstream)
    grad_down_w = outer_sum(activated, upstream)
    grad_heads = (
        back_dot(upstream, weight_out)
        .astype(jnp.bfloat16)
        .reshape(block_len, seq_count, head_count, head_size)
    )
    head_delta = jnp.einsum("qshd,shqd->shq", grad_heads.astype(jnp.float32), attended)
    piece_rows = (
        lax.all_gather(key_flat, "ctx", axis=0, tiled=True),
        lax.all_gather(value_flat, "ctx", axis=0, tiled=True),
    )
    block_total, key_parts = key_blocks(piece_rows[0])
    _, value_parts = key_blocks(piece_rows[1])
    offsets = jnp.arange(block_total, dtype=jnp.int32) * block_len

    def query_visit(current, block_item):
        key_blk, value_blk, offset = block_item

        def query_update(running):
            scores = (
                jnp.einsum(
                    "qshd,kshd->shqk", query_rot, key_blk, preferred_element_type=jnp.float32
                )
                * score_scale
            )
            allowed = (offset + jnp.arange(block_len, dtype=jnp.int32))[None, :] <= positions[
                :, None
            ]
            scores = jnp.where(allowed, scores, masked_score)
            probs_f = jnp.where(allowed, jnp.exp(scores - log_total[..., None]), 0.0)
            grad_probs = jnp.einsum(
                "qshd,kshd->shqk", grad_heads, value_blk, preferred_element_type=jnp.float32
            )
            grad_scores = (probs_f * (grad_probs - head_delta[..., None])).astype(jnp.bfloat16)
            return running + jnp.einsum(
                "shqk,kshd->shqd", grad_scores, key_blk, preferred_element_type=jnp.float32
            )

        def query_unchanged(running):
            return running

        return (lax.cond(offset <= own_start, query_update, query_unchanged, current), None)

    result, _ = lax.scan(query_visit, zero_heads, (key_parts, value_parts, offsets))
    grad_query_acc = result
    query_send = query_rot.reshape(block_len, seq_count, model_width)
    grad_send = grad_heads.reshape(block_len, seq_count, model_width)
    total_send = log_total.transpose(2, 0, 1)
    delta_send = head_delta.transpose(2, 0, 1)
    total_every, delta_every = (
        lax.all_gather(total_send, "ctx", axis=0, tiled=True),
        lax.all_gather(delta_send, "ctx", axis=0, tiled=True),
    )
    query_all = lax.all_gather(query_send, "ctx", axis=0, tiled=True)
    grad_all_rows = lax.all_gather(grad_send, "ctx", axis=0, tiled=True)
    piece_len = query_all.shape[0]
    block_total = piece_len // block_len
    query_parts = query_all.reshape(block_total, block_len, seq_count, head_count, head_size)
    grad_parts = grad_all_rows.reshape(block_total, block_len, seq_count, head_count, head_size)
    total_parts = total_every.reshape(block_total, block_len, seq_count, head_count)
    delta_parts = delta_every.reshape(block_total, block_len, seq_count, head_count)
    offsets = jnp.arange(block_total, dtype=jnp.int32) * block_len

    def key_visit(current, block_item):
        query_blk, grad_blk, total_blk, delta_blk, offset = block_item

        def key_update(running):
            grad_key_run, grad_value_run = running
            total_rows = total_blk.transpose(1, 2, 0)
            delta_rows = delta_blk.transpose(1, 2, 0)
            scores = (
                jnp.einsum(
                    "qshd,kshd->shqk", query_blk, key_rot, preferred_element_type=jnp.float32
                )
                * score_scale
            )
            allowed = (
                positions[None, :] <= (offset + jnp.arange(block_len, dtype=jnp.int32))[:, None]
            )
            scores = jnp.where(allowed, scores, masked_score)
            probs_f = jnp.where(allowed, jnp.exp(scores - total_rows[..., None]), 0.0)
            grad_probs = jnp.einsum(
                "qshd,kshd->shqk", grad_blk, value_low, preferred_element_type=jnp.float32
            )
            grad_scores = (probs_f * (grad_probs - delta_rows[..., None])).astype(jnp.bfloat16)
            grad_key_run = grad_key_run + jnp.einsum(
                "shqk,qshd->shkd", grad_scores, query_blk, preferred_element_type=jnp.float32
            )
            grad_value_run = grad_value_run + jnp.einsum(
                "shqk,qshd->shkd",
                probs_f.astype(jnp.bfloat16),
                grad_blk,
                preferred_element_type=jnp.float32,
            )
            return (grad_key_run, grad_value_run)

        def key_unchanged(running):
            return running

        return (lax.cond(offset >= own_start, key_update, key_unchanged, current), None)

    result, _ = lax.scan(
        key_visit,
        (zero_heads, zero_heads),
        (query_parts, grad_parts, total_parts, delta_parts, offsets),
    )
    grad_key_acc, grad_value_acc = result
    grad_query = unrotate(
        grad_query_acc.transpose(2, 0, 1, 3) * score_scale, cosine_table, sine_table
    )
    grad_key = unrotate(grad_key_acc.transpose(2, 0, 1, 3) * score_scale, cosine_table, sine_table)
    grad_value = grad_value_acc.transpose(2, 0, 1, 3)
    grad_proj = (
        jnp.stack([grad_query, grad_key, grad_value], axis=2)
        .reshape(row_count, 3 * model_width)
        .astype(jnp.bfloat16)
    )
    grad_qkv_w = outer_sum(normed_one, grad_proj)
    grad_qkv_b = jnp.sum(grad_proj.astype(jnp.float32), axis=0)
    grad_normed_one = back_dot(grad_proj, weight_qkv)
    grad_act = back_dot(upstream, weight_down)
    _, gelu_back = jax.vjp(exact_gelu, hidden_pre)
    grad_hidden = gelu_back(grad_act)[0].astype(jnp.bfloat16)
    grad_up_w = outer_sum(normed_two, grad_hidden)
    grad_up_b = jnp.sum(grad_hidden.astype(jnp.float32), axis=0)
    grad_normed_two = back_dot(grad_hidden, weight_up)
    _, norm_back_one = jax.vjp(layer_norm, inputs, gain_one, bias_one)
    grad_in_one, grad_gain_one, grad_bias_one = norm_back_one(grad_normed_one)
    _, norm_back_two = jax.vjp(layer_norm, inputs, gain_two, bias_two)
    grad_in_two, grad_gain_two, grad_bias_two = norm_back_two(grad_normed_two)
    tokens_grad = (
        (upstream_f + grad_in_one + grad_in_two)
        .astype(jnp.bfloat16)
        .reshape(block_len, seq_count, model_width)
    )
    summed_rows = (
        lax.psum_scatter(grad_gain_one, "fsdp", scatter_dimension=0, tiled=True),
        lax.psum_scatter(grad_bias_one, "fsdp", scatter_dimension=0, tiled=True),
        lax.psum_scatter(grad_gain_two, "fsdp", scatter_dimension=0, tiled=True),
        lax.psum_scatter(grad_bias_two, "fsdp", scatter_dimension=0, tiled=True),
        lax.psum_scatter(grad_qkv_w, "fsdp", scatter_dimension=0, tiled=True),
        lax.psum_scatter(grad_qkv_b, "fsdp", scatter_dimension=0, tiled=True),
        lax.psum_scatter(grad_out_w, "fsdp", scatter_dimension=0, tiled=True),
        lax.psum_scatter(column_sums, "fsdp", scatter_dimension=0, tiled=True),
        lax.psum_scatter(grad_up_w, "fsdp", scatter_dimension=0, tiled=True),
        lax.psum_scatter(grad_up_b, "fsdp", scatter_dimension=0, tiled=True),
        lax.psum_scatter(grad_down_w, "fsdp", scatter_dimension=0, tiled=True),
        lax.psum_scatter(column_sums, "fsdp", scatter_dimension=0, tiled=True),
    )
    (
        part_gain_one,
        part_bias_one,
        part_gain_two,
        part_bias_two,
        part_qkv_w,
        part_qkv_b,
        part_out_w,
        part_out_b,
        part_up_w,
        part_up_b,
        part_down_w,
        part_down_b,
    ) = summed_rows
    finished = lax.psum(
        (
            part_gain_one,
            part_bias_one,
            part_gain_two,
            part_bias_two,
            part_qkv_w,
            part_qkv_b,
            part_out_w,
            part_out_b,
            part_up_w,
            part_up_b,
            part_down_w,
            part_down_b,
        ),
        "ctx",
    )
    return (
        layer_out,
        tokens_grad,
        finished[0],
        finished[1],
        finished[2],
        finished[3],
        finished[4],
        finished[5],
        finished[6],
        finished[7],
        finished[8],
        finished[9],
        finished[10],
        finished[11],
    )


def solution(mesh):
    placed = (
        P("ctx", "fsdp", None),
        P("fsdp"),
        P("fsdp"),
        P("fsdp"),
        P("fsdp"),
        P("fsdp", None),
        P("fsdp"),
        P("fsdp", None),
        P("fsdp"),
        P("fsdp", None),
        P("fsdp"),
        P("fsdp", None),
        P("fsdp"),
        P("ctx", "fsdp", None),
    )
    return jax.shard_map(
        body,
        mesh=mesh,
        in_specs=placed,
        out_specs=(
            P("ctx", "fsdp", None),
            P("ctx", "fsdp", None),
            P("fsdp"),
            P("fsdp"),
            P("fsdp"),
            P("fsdp"),
            P("fsdp", None),
            P("fsdp"),
            P("fsdp", None),
            P("fsdp"),
            P("fsdp", None),
            P("fsdp"),
            P("fsdp", None),
            P("fsdp"),
        ),
        check_vma=False,
    )
```

profile of v0, /device:TPU:0, one launch (start us, length us, event | category | flops | bytes accessed | tf_op | source)
XLA Modules:
  0.0 806.5 jit_solution(3832058901322340197)
XLA Ops:
  17.5 32.2 %all-reduce.17 = (bf16[768]{0:T(1024)(128)(2,1)}, bf16[768]{0:T(1024)(128)(2,1)}, bf16[2304]{0:T(1024)(128)(2,1)S(1)}, bf16[768]{0:T(1024)(128)(2,1)S(1)}, bf16[...) all-reduce(bf16[768]{0:T(1024)(128)(2,1)S(1)} %dynamic-update-slice, ...), channel_id=1, replica_groups=mesh['ctx'=4,'fsdp'=8] {'fsdp'}, use_global_device_ids=true, to_apply=%add.5 | all-reduce | flops 6912 | bytes 27648
  51.2 3.5 all-gather.10.cloned.1.call-done
  54.6 6.2 convolution_add_fusion
  60.9 9.5 %reshape.266 = f32[256,2,3,12,64]{4,3,2,1,0:T(8,128)} reshape(f32[512,2304]{1,0:T(8,128)} %convolution_add_fusion) | data formatting | bytes 9437184 | tf_op jit(solution)/shard_map/reshape | solution.py:125
  70.4 7.8 fusion.106
  78.2 3.1 copy.205
  81.3 3.1 copy.206
  104.0 4.1 copy.200
  108.0 20.6 %all-gather.12.cloned.1.call-done = bf16[1024,2,768]{0,2,1:T(8,128)(2,1)} async-done(((bf16[256,2,768]{0,2,1:T(8,128)(2,1)}), bf16[1024,2,768]{0,2,1:T(8,128)(2,1)}) %all-gather.12.cloned.1.call-update) | async-done | bytes 3145744 | tf_op jit(solution)/shard_map/all_gather | solution.py:143
  128.7 4.8 reshape.267
  135.7 39.1 %all-gather.14.cloned.1.call-done = bf16[1024,2,768]{0,2,1:T(8,128)(2,1)} async-done(((bf16[256,2,768]{0,2,1:T(8,128)(2,1)}), bf16[1024,2,768]{0,2,1:T(8,128)(2,1)}) %all-gather.14.cloned.1.call-update) | async-done | bytes 3145744 | tf_op jit(solution)/shard_map/all_gather | solution.py:144
  174.8 6.2 reshape.268
  181.0 4.2 copy.178
  185.4 12.4 %while.45 = (s32[]{:T(128)}, f32[2,12,256,64]{2,3,1,0:T(8,128)S(1)}, f32[2,12,256]{2,1,0:T(8,128)S(1)}, f32[2,12,256]{2,1,0:T(8,128)S(1)}, s32[4]{0:T(128)S(1)},...) while((s32[]{:T(128)}, ...), condition=%wide.region_7.8_spmd.clone.clone, body=%wide.region_2.7_spmd.clone.clone.sunk | while | flops 420819456 | bytes 25042192 | solution.py:182
  186.7 7.3 conditional.12
  200.5 3.9 copy.179
  206.4 3.7 fusion.113
  210.1 12.2 %reduce-scatter.5.cloned.1.call-start = ((), (), s32[]{:S(2)}) async-start(), calls=%async_computation.12 | async-start | bytes 7962624 | tf_op jit(solution)/shard_map/reduce_scatter | solution.py:350
  222.3 3.1 add_convert_fusion.1
  225.4 3.0 convert_element_type.183
  235.6 6.2 reshape.274
  241.8 4.2 copy.188
  245.9 28.7 %all_gather.71 = f32[1024,2,12]{0,2,1:T(8,128)S(1)} all-gather(f32[256,2,12]{0,2,1:T(8,128)S(1)} %bitcast.157), channel_id=1, replica_groups=mesh['ctx'=4,'fsdp'=8] {'ctx'}, dimensions={0}, use_global_device_ids=true | all-gather | bytes 122880 | tf_op jit(solution)/shard_map/all_gather | solution.py:260
  274.7 9.2 %all_gather.73 = f32[1024,2,12]{0,2,1:T(8,128)S(1)} all-gather(f32[256,2,12]{0,2,1:T(8,128)S(1)} %bitcast.156), channel_id=1, replica_groups=mesh['ctx'=4,'fsdp'=8] {'ctx'}, dimensions={0}, use_global_device_ids=true | all-gather | bytes 122880 | tf_op jit(solution)/shard_map/all_gather | solution.py:261
  284.0 6.2 reshape.272
  290.2 4.3 copy.186
  294.7 16.9 %while.46 = (s32[]{:T(128)}, f32[2,12,256,64]{2,3,1,0:T(8,128)S(1)}, s32[4]{0:T(128)S(1)}, s32[]{:T(128)}, bf16[4,256,2,12,64]{1,4,3,2,0:T(8,128)(2,1)}, /*index...) while((s32[]{:T(128)}, ...), condition=%wide.region_11.12_spmd.clone.clone, body=%wide.region_8.11_spmd.clone.clone.sunk | while | flops 615449088 | bytes 19848944 | solution.py:253
  295.9 11.8 %conditional.13 = (f32[2,12,256,64]{2,3,1,0:T(8,128)S(1)}) conditional(s32[]{:T(128)} %convert_element_type.239, f32[2,12,256,64]{2,3,1,0:T(8,128)S(1)} %get-tuple-element.1229, (s32[]{:T(128)}, s32[]{:T(128)}, bf16[4,256,2,12,64]{1,4,3,2,0:T(8,128)(2,1)}, s32[]{:T(128)}, bf16[256,2,12,64]{0,3,2,1:T(8,128)(2,1)S(1)}, ...), branch_computations={%region_9.9_spmd, %region_10.10_spmd} | conditional | flops 615449088 | bytes 19847696 | solution.py:251
  296.0 4.9 fusion.41
  301.6 6.2 fusion.35
  314.6 79.8 %while.47 = (s32[]{:T(128)}, f32[2,12,256,64]{2,3,1,0:T(8,128)S(1)}, f32[2,12,256,64]{2,3,1,0:T(8,128)}, s32[4]{0:T(128)S(1)}, s32[]{:T(128)}, /*index=5*/bf16[4...) while((s32[]{:T(128)}, ...), condition=%wide.region_15.16_spmd.clone.clone, body=%wide.region_12.0_spmd.clone.clone.sunk | while | flops 825033216 | bytes 30261540 | solution.py:311
  315.8 18.9 %conditional.14 = ((f32[2,12,256,64]{2,3,1,0:T(8,128)S(1)}, f32[2,12,256,64]{2,3,1,0:T(8,128)})) conditional(s32[]{:T(128)} %convert_element_type.240, (f32[2,12,256,64]{2,3,1,0:T(8,128)S(1)}, f32[2,12,256,64]{2,3,1,0:T(8,128)}) %tuple.168, (s32[]{:T(128)}, s32[]{:T(128)}, bf16[4,256,2,12,64]{1,4,3,2,0:T(8,128)(2,1)}, s32[]{:T(128)}, ...), branch_computations={%region_13.13_spmd, %region_14.14_spmd} | conditional | flops 825033216 | bytes 30260260 | solution.py:309
  315.8 4.9 fusion.69
  321.5 6.7 fusion.61
  328.2 6.6 fusion.62
  336.0 18.8 %conditional.14 = ((f32[2,12,256,64]{2,3,1,0:T(8,128)S(1)}, f32[2,12,256,64]{2,3,1,0:T(8,128)})) conditional(s32[]{:T(128)} %convert_element_type.240, (f32[2,12,256,64]{2,3,1,0:T(8,128)S(1)}, f32[2,12,256,64]{2,3,1,0:T(8,128)}) %tuple.168, (s32[]{:T(128)}, s32[]{:T(128)}, bf16[4,256,2,12,64]{1,4,3,2,0:T(8,128)(2,1)}, s32[]{:T(128)}, ...), branch_computations={%region_13.13_spmd, %region_14.14_spmd} | conditional | flops 825033216 | bytes 30260260 | solution.py:309
  336.0 4.9 fusion.69
  341.6 6.8 fusion.61
  348.4 6.3 fusion.62
  356.0 18.6 %conditional.14 = ((f32[2,12,256,64]{2,3,1,0:T(8,128)S(1)}, f32[2,12,256,64]{2,3,1,0:T(8,128)})) conditional(s32[]{:T(128)} %convert_element_type.240, (f32[2,12,256,64]{2,3,1,0:T(8,128)S(1)}, f32[2,12,256,64]{2,3,1,0:T(8,128)}) %tuple.168, (s32[]{:T(128)}, s32[]{:T(128)}, bf16[4,256,2,12,64]{1,4,3,2,0:T(8,128)(2,1)}, s32[]{:T(128)}, ...), branch_computations={%region_13.13_spmd, %region_14.14_spmd} | conditional | flops 825033216 | bytes 30260260 | solution.py:309
  356.0 4.9 fusion.69
  361.6 6.7 fusion.61
  368.3 6.2 fusion.62
  375.8 18.6 %conditional.14 = ((f32[2,12,256,64]{2,3,1,0:T(8,128)S(1)}, f32[2,12,256,64]{2,3,1,0:T(8,128)})) conditional(s32[]{:T(128)} %convert_element_type.240, (f32[2,12,256,64]{2,3,1,0:T(8,128)S(1)}, f32[2,12,256,64]{2,3,1,0:T(8,128)}) %tuple.168, (s32[]{:T(128)}, s32[]{:T(128)}, bf16[4,256,2,12,64]{1,4,3,2,0:T(8,128)(2,1)}, s32[]{:T(128)}, ...), branch_computations={%region_13.13_spmd, %region_14.14_spmd} | conditional | flops 825033216 | bytes 30260260 | solution.py:309
  375.8 4.9 fusion.69
  381.4 6.7 fusion.61
  388.1 6.3 fusion.62
  397.8 10.0 %copy.193 = bf16[256,2,3,12,64]{4,3,2,1,0:T(8,128)(2,1)} copy(bf16[256,2,3,12,64]{0,4,3,2,1:T(8,128)(2,1)S(1)} %get-tuple-element.902) | data formatting | bytes 4718592 | tf_op jit(solution)/shard_map/convert_element_type | solution.py:325
  407.8 7.3 convert_element_type.179
  415.1 5.0 fusion.112
  420.8 12.7 %all-gather = bf16[8,1,384]{2,1,0:T(2,128)(2,1)S(1)} all-gather(bf16[1,1,384]{2,1,0:T(2,128)(2,1)S(1)} %reshape.298), channel_id=1, replica_groups=mesh['ctx'=4,'fsdp'=8] {'fsdp'}, dimensions={0}, use_global_device_ids=true | all-gather | bytes 6912 | tf_op jit(solution)/shard_map/all_gather | solution.py:92
  433.6 8.4 %fusion.102 = f32[512,3072]{1,0:T(8,128)} fusion(bf16[768,3072]{1,0:T(8,128)(2,1)} %all-gather.18.cloned.1.call-done, f32[512,768]{1,0:T(8,128)} %copy-done.7, f32[768]{0:T(1024)S(1)} %convert_element_type.168, f32[768]{0:T(1024)S(1)} %convert_element_type.167, f32[512]{0:T(512)S(1)} %copy-done.35, f32[512]{0:T(512)S(1)} %copy-done.33), kind=kOutput, calls=%fused_computation.168 | convolution fusion | flops 2417885184 | bytes 12593152 | tf_op jit(solution)/shard_map/dot_general | solution.py:194
  441.9 19.6 %convert_reduce_fusion = (f32[3072]{0:T(1024)S(1)}, bf16[512,3072]{1,0:T(8,128)(2,1)}, f32[512,3072]{1,0:T(8,128)S(1)}) fusion(f32[512,3072]{1,0:T(8,128)} %fusion.102, f32[3072]{0:T(1024)S(1)} %bitcast.158, bf16[512,768]{1,0:T(8,128)(2,1)S(1)} %copy-done.6, bf16[3072,768]{1,0:T(8,128)(2,1)} %all-gather.20.cloned.1.call-done), kind=kOutput, calls=%fused_computation.88 | convolution fusion | flops 2533880832 | bytes 21258240 | tf_op jit(solution)/shard_map/dot_general | solution.py:50
  464.7 5.2 fusion.114
  469.9 9.0 %fusion.101 = f32[768,3072]{1,0:T(8,128)} fusion(bf16[512,3072]{1,0:T(8,128)(2,1)} %get-tuple-element.899, f32[512,768]{1,0:T(8,128)} %copy-done.7, f32[768]{0:T(1024)S(1)} %convert_element_type.168, f32[768]{0:T(1024)S(1)} %convert_element_type.167, f32[512]{0:T(512)S(1)} %copy-done.35, f32[512]{0:T(512)S(1)} %copy-done.33), kind=kOutput, calls=%fused_computation.167 | convolution fusion | flops 2417885184 | bytes 14166016 | tf_op jit(solution)/shard_map/dot_general | solution.py:56
  483.0 13.8 %reduce-scatter.5.cloned.1.call-done = f32[96,2304]{1,0:T(8,128)} async-done(((f32[768,2304]{1,0:T(8,128)}), f32[96,2304]{1,0:T(8,128)}) %reduce-scatter.5.cloned.1.call-update) | async-done | bytes 884752 | tf_op jit(solution)/shard_map/reduce_scatter | solution.py:350
  496.8 100.2 %reduce-scatter.11.cloned.1.call-done = f32[384,768]{1,0:T(8,128)} async-done(((f32[3072,768]{1,0:T(8,128)}), f32[384,768]{1,0:T(8,128)}) %reduce-scatter.11.cloned.1.call-update) | async-done | bytes 1179664 | tf_op jit(solution)/shard_map/reduce_scatter | solution.py:356
  596.9 100.1 %reduce-scatter.9.cloned.1.call-done = f32[96,3072]{1,0:T(8,128)} async-done(((f32[768,3072]{1,0:T(8,128)}), f32[96,3072]{1,0:T(8,128)}) %reduce-scatter.9.cloned.1.call-update) | async-done | bytes 1179664 | tf_op jit(solution)/shard_map/reduce_scatter | solution.py:354
  697.0 7.1 fusion.110
  704.1 4.6 fusion.111
  708.8 7.3 multiply_reduce_fusion.1
  716.1 26.5 %all-reduce.14 = (f32[768]{0:T(1024)S(1)}, f32[768]{0:T(1024)S(1)}, f32[768]{0:T(1024)S(1)}, f32[768]{0:T(1024)S(1)}, f32[2304]{0:T(1024)S(1)}, /*index=5*/f32[768]{0:T(1024)S(1)}, f32[3072]{0:T(1024)S(1)}) all-reduce(f32[768]{0:T(1024)S(1)} %get-tuple-element.808, ...), channel_id=2, replica_groups=mesh['ctx'=4,'fsdp'=8] {'fsdp'}, use_global_device_ids=true, to_apply=%region_21.22.clone | all-reduce | flops 9216 | bytes 73728
  743.1 10.8 %all-reduce.15 = (f32[96]{0:T(128)}, f32[96]{0:T(128)}, f32[96]{0:T(128)}, f32[96]{0:T(128)}, f32[288]{0:T(512)}, /*index=5*/f32[96]{0:T(128)S(1)}, f32[384]{0:T(512)}) all-reduce(f32[96]{0:T(128)S(1)} %dynamic-slice.8, f32[96]{0:T(128)S(1)} %dynamic-slice.10, f32[96]{0:T(128)S(1)} %dynamic-slice.12, ...), channel_id=1, replica_groups=mesh['ctx'=4,'fsdp'=8] {'ctx'}, use_global_device_ids=true, to_apply=%region_22.23 | all-reduce | flops 1152 | bytes 9216 | tf_op jit(solution)/shard_map/psum | solution.py:373
  764.7 28.4 %all-reduce.20.cloned.1.call-done = (f32[96,2304]{1,0:T(8,128)}, f32[96,768]{1,0:T(8,128)}, f32[96,3072]{1,0:T(8,128)}, f32[384,768]{1,0:T(8,128)}) async-done(((f32[96,2304]{1,0:T(8,128)}, f32[96,768]{1,0:T(8,128)}, f32[96,3072]{1,0:T(8,128)}, f32[384,768]{1,0:T(8,128)}), (f32[96,2304]{1,0:T(8,128)}, f32[96,768]{1,0:T(8,128)}, f32[96,3072]{1,0:T(8,128)}, ...) | async-done | bytes 3538960 | tf_op jit(solution)/shard_map/psum | solution.py:373
  (287 shorter events, 92.5 us)
Async XLA Ops:
  7.2 6.6 copy-start.40
  7.2 6.3 copy-start.4
  7.2 8.6 %copy-start.43 = (bf16[96]{0:T(256)(128)(2,1)S(1)}, bf16[96]{0:T(256)(128)(2,1)}, u32[]{:S(2)}) copy-start(bf16[96]{0:T(256)(128)(2,1)} %param.27) | copy-start | bytes 580
  7.2 8.8 %copy-start.44 = (bf16[96]{0:T(256)(128)(2,1)S(1)}, bf16[96]{0:T(256)(128)(2,1)}, u32[]{:S(2)}) copy-start(bf16[96]{0:T(256)(128)(2,1)} %param.28) | copy-start | bytes 580
  7.2 9.0 %copy-start.45 = (bf16[96]{0:T(256)(128)(2,1)S(1)}, bf16[96]{0:T(256)(128)(2,1)}, u32[]{:S(2)}) copy-start(bf16[96]{0:T(256)(128)(2,1)} %param.34) | copy-start | bytes 580
  7.2 9.3 %copy-start.46 = (bf16[96]{0:T(256)(128)(2,1)S(1)}, bf16[96]{0:T(256)(128)(2,1)}, u32[]{:S(2)}) copy-start(bf16[96]{0:T(256)(128)(2,1)} %param.29) | copy-start | bytes 580
  7.2 9.5 %copy-start.47 = (bf16[96]{0:T(256)(128)(2,1)S(1)}, bf16[96]{0:T(256)(128)(2,1)}, u32[]{:S(2)}) copy-start(bf16[96]{0:T(256)(128)(2,1)} %param.30) | copy-start | bytes 580
  7.3 9.7 %copy-start.48 = (bf16[96]{0:T(256)(128)(2,1)S(1)}, bf16[96]{0:T(256)(128)(2,1)}, u32[]{:S(2)}) copy-start(bf16[96]{0:T(256)(128)(2,1)} %param.38) | copy-start | bytes 580
  7.3 9.9 %copy-start.41 = (bf16[288]{0:T(512)(128)(2,1)S(1)}, bf16[288]{0:T(512)(128)(2,1)}, u32[]{:S(2)}) copy-start(bf16[288]{0:T(512)(128)(2,1)} %param.32) | copy-start | bytes 1732
  7.3 47.4 %all-gather.10.cloned.1.call-start = ((), (), s32[]{:S(2)}) async-start(), calls=%async_computation.4 | async-start | bytes 3981312 | tf_op jit(solution)/shard_map/all_gather | solution.py:87
  8.0 83.4 %all-gather.16.cloned.1.call-start = ((), (), s32[]{:S(2)}) async-start(), calls=%async_computation.7 | async-start | bytes 1327104 | tf_op jit(solution)/shard_map/all_gather | solution.py:89
  8.8 119.9 %all-gather.12.cloned.1.call-start = ((), (), s32[]{:S(2)}) async-start(), calls=%async_computation.5 | async-start | bytes 3932160 | tf_op jit(solution)/shard_map/all_gather | solution.py:143
  13.5 47.4 %copy-start.32 = (f32[512]{0:T(512)}, f32[512]{0:T(512)S(1)}, u32[]{:S(2)}) copy-start(f32[512]{0:T(512)S(1)} %div.47) | copy-start | bytes 6148
  13.7 47.2 %copy-start.7 = (f32[512,768]{1,0:T(8,128)}, f32[512,768]{1,0:T(8,128)S(1)}, u32[]{:S(2)}) copy-start(f32[512,768]{1,0:T(8,128)S(1)} %reshape.265) | copy-start | bytes 4718596
  49.6 172.6 %copy-start.28 = (f32[768]{0:T(1024)}, f32[768]{0:T(1024)S(1)}, u32[]{:S(2)}) copy-start(f32[768]{0:T(1024)S(1)} %convert_element_type.153) | copy-start | bytes 9220
  50.5 0.5 copy-start.30
  50.5 10.4 %copy-start.34 = (f32[512]{0:T(512)}, f32[512]{0:T(512)S(1)}, u32[]{:S(2)}) copy-start(f32[512]{0:T(512)S(1)} %rsqrt.18) | copy-start | bytes 6148
  51.1 33.4 %copy-start.24 = (f32[256,16]{0,1:T(8,128)}, f32[256,16]{0,1:T(8,128)S(1)}, u32[]{:S(2)}) copy-start(f32[256,16]{0,1:T(8,128)S(1)} %get-tuple-element.939) | copy-start | bytes 49156
  51.2 33.4 %copy-start.26 = (f32[256,16]{0,1:T(8,128)}, f32[256,16]{0,1:T(8,128)S(1)}, u32[]{:S(2)}) copy-start(f32[256,16]{0,1:T(8,128)S(1)} %get-tuple-element.940) | copy-start | bytes 49156
  84.4 1.4 copy-start.15
  85.8 5.3 copy-start.17
  85.8 89.0 %all-gather.14.cloned.1.call-start = ((), (), s32[]{:S(2)}) async-start(), calls=%async_computation.6 | async-start | bytes 3932160 | tf_op jit(solution)/shard_map/all_gather | solution.py:144
  91.0 144.6 %all-gather.24.cloned.1.call-start = ((), (), s32[]{:S(2)}) async-start(), calls=%async_computation.11 | async-start | bytes 3932160 | tf_op jit(solution)/shard_map/all_gather | solution.py:264
  91.4 4.8 copy-start.5
  96.2 187.8 %all-gather.22.cloned.1.call-start = ((), (), s32[]{:S(2)}) async-start(), calls=%async_computation.10 | async-start | bytes 3932160 | tf_op jit(solution)/shard_map/all_gather | solution.py:263
  98.6 335.0 %all-gather.18.cloned.1.call-start = ((), (), s32[]{:S(2)}) async-start(), calls=%async_computation.8 | async-start | bytes 5308416 | tf_op jit(solution)/shard_map/all_gather | solution.py:91
  99.3 342.6 %all-gather.20.cloned.1.call-start = ((), (), s32[]{:S(2)}) async-start(), calls=%async_computation.9 | async-start | bytes 5308416 | tf_op jit(solution)/shard_map/all_gather | solution.py:93
  100.1 382.9 %reduce-scatter.7.cloned.1.call-start = ((), (), s32[]{:S(2)}) async-start(), calls=%async_computation.13 | async-start | bytes 2654208 | tf_op jit(solution)/shard_map/reduce_scatter | solution.py:352
  101.4 2.6 copy-start.2
  181.0 4.4 copy-start
  206.4 15.9 %copy-start.23 = (f32[256,2]{1,0:T(8,128)S(1)}, f32[256,2]{1,0:T(8,128)}, u32[]{:S(2)}) copy-start(f32[256,2]{1,0:T(8,128)} %get-tuple-element.931) | copy-start | bytes 6148
  210.1 18.3 %copy-start.3 = (bf16[256,2,12,64]{3,2,1,0:T(8,128)(2,1)S(1)}, bf16[256,2,12,64]{3,2,1,0:T(8,128)(2,1)}, u32[]{:S(2)}) copy-start(bf16[256,2,12,64]{3,2,1,0:T(8,128)(2,1)} %copy-done.2) | copy-start | bytes 2359300
  210.1 286.7 %reduce-scatter.5.cloned.1.call-start = ((), (), s32[]{:S(2)}) async-start(), calls=%async_computation.12 | async-start | bytes 7962624 | tf_op jit(solution)/shard_map/reduce_scatter | solution.py:350
  290.2 4.5 copy-start.22
  311.6 2.9 copy-start.1
  311.8 1.2 copy-start.13
  394.4 1.4 copy-start.14
  394.4 1.4 copy-start.27
  394.4 1.6 copy-start.25
  395.9 1.4 copy-start.10
  407.8 7.3 copy-start.16
  420.1 0.7 copy-start.39
  420.1 0.7 copy-start.38
  420.1 0.7 copy-start.42
  420.1 13.5 %copy-start.33 = (f32[512]{0:T(512)S(1)}, f32[512]{0:T(512)}, u32[]{:S(2)}) copy-start(f32[512]{0:T(512)} %copy-done.32) | copy-start | bytes 6148
  420.1 13.5 %copy-start.35 = (f32[512]{0:T(512)S(1)}, f32[512]{0:T(512)}, u32[]{:S(2)}) copy-start(f32[512]{0:T(512)} %copy-done.34) | copy-start | bytes 6148
  420.1 176.8 %reduce-scatter.11.cloned.1.call-start = ((), (), s32[]{:S(2)}) async-start(), calls=%async_computation.15 | async-start | bytes 10616832 | tf_op jit(solution)/shard_map/reduce_scatter | solution.py:356
  433.5 8.4 %copy-start.6 = (bf16[512,768]{1,0:T(8,128)(2,1)S(1)}, bf16[512,768]{1,0:T(8,128)(2,1)}, u32[]{:S(2)}) copy-start(bf16[512,768]{1,0:T(8,128)(2,1)} %copy-done.5) | copy-start | bytes 2359300
  441.9 19.6 %copy-start.11 = (f32[512,3072]{1,0:T(8,128)S(1)}, f32[512,3072]{1,0:T(8,128)}, u32[]{:S(2)}) copy-start(f32[512,3072]{1,0:T(8,128)} %fusion.102) | copy-start | bytes 18874372
  463.1 1.6 copy-start.18
  469.9 227.1 %reduce-scatter.9.cloned.1.call-start = ((), (), s32[]{:S(2)}) async-start(), calls=%async_computation.14 | async-start | bytes 10616832 | tf_op jit(solution)/shard_map/reduce_scatter | solution.py:354
  478.9 2.2 copy-start.37
  478.9 2.2 copy-start.36
  478.9 314.2 %all-reduce.20.cloned.1.call-start = ((), (), s32[]{:S(2)}) async-start(), calls=%async_computation.16 | async-start | bytes 7077888 | tf_op jit(solution)/shard_map/psum | solution.py:373
  704.1 4.6 copy-start.8
  704.1 4.6 copy-start.29
  704.1 4.6 copy-start.50
  708.8 7.3 copy-start.19
  708.8 45.1 %copy-start.31 = (f32[512]{0:T(512)S(1)}, f32[512]{0:T(512)}, u32[]{:S(2)}) copy-start(f32[512]{0:T(512)} %copy-done.30) | copy-start | bytes 6148
  708.8 45.1 %copy-start.9 = (f32[512,768]{1,0:T(8,128)S(1)}, f32[512,768]{1,0:T(8,128)}, u32[]{:S(2)}) copy-start(f32[512,768]{1,0:T(8,128)} %copy-done.7) | copy-start | bytes 4718596
  753.9 39.2 %copy-start.49 = (f32[96]{0:T(128)}, f32[96]{0:T(128)S(1)}, u32[]{:S(2)}) copy-start(f32[96]{0:T(128)S(1)} %get-tuple-element.1287) | copy-start | bytes 1156
  756.9 4.1 copy-start.12
  793.2 4.5 copy-start.21
  793.2 5.6 copy-start.20
Sparse Core Ops, SparseCore 0:
  9.8 44.8 all-gather.9
  56.3 21.4 all-gather.15
  85.9 42.7 all-gather.11
  130.9 43.8 all-gather.13
  176.5 43.8 all-gather.23
  222.6 43.8 all-gather.21
  268.1 51.7 all-gather.17
  321.5 50.5 all-gather.19
  374.4 35.0 reduce-scatter.6
  420.2 76.4 reduce-scatter.4
  499.1 97.7 reduce-scatter.10
  599.1 97.8 reduce-scatter.8
  700.4 92.6 all-reduce.19
where the time goes:
time: 813 us; the launch traced here: 806 us
  waiting for transfers between devices  309 us (38%)
  matrix products  169 us (21%)
  local copies, waits for them, and re-layouts  139 us (17%)
  blocking collectives  120 us (15%)
  other arithmetic  30.5 us (4%)
  between operations  18.3 us (2%)
  starting transfers between devices  13.1 us (2%)
  loops' own time  8.38 us (1%)
    reduce_scatter x1, waiting for transfers between devices, body(): lax.psum_scatter(grad_down_w, 'fsdp', scatter_dimension=0, tiled=True)  100 us
    reduce_scatter x1, waiting for transfers between devices, body(): lax.psum_scatter(grad_up_w, 'fsdp', scatter_dimension=0, tiled=True)  100 us
    unnamed x2, blocking collectives  58.7 us
    unnamed x141, local copies, waits for them, and re-layouts  45.2 us
    all_gather x1, waiting for transfers between devices, body(): lax.all_gather(value_flat, 'ctx', axis=0, tiled=True)  39.1 us
    dot_general x4, matrix products, back_dot(): lax.dot_general(left, right, (((1,), (1,)), ((), ())), preferred_element_...  33.9 us
    all_gather x1, blocking collectives, body(): lax.all_gather(total_send, 'ctx', axis=0, tiled=True)  28.7 us
    psum x1, waiting for transfers between devices, body(): lax.psum((part_gain_one, part_bias_one, part_gain_two, part_bias_two, par...  28.4 us
  transfers between devices with their start and end apart: 13, of which 7 were waited for; matrix products, arithmetic and copies ran while one was open for 40% of the time, Pallas kernels for 0%

commit v1 on v0

v1 whole, which is shorter than its diff:
```python
import functools

import jax
import jax.numpy as jnp
import numpy as np
from jax import lax
from jax.experimental import pallas as pl
from jax.experimental.pallas import tpu as pltpu
from jax.sharding import PartitionSpec as P

H = 12
HD = 64
ROT = 16
LANES = 128
EPS = 1e-05
MASKED = -1e30
VMEM = 56 * 1024 * 1024
BF = jnp.bfloat16
F32 = jnp.float32


def dot(left, right, dims=((1,), (0,))):
    return lax.dot_general(left, right, (dims, ((), ())), preferred_element_type=F32)


def back_dot(left, right):
    return dot(left, right, ((1,), (1,)))


def outer_sum(left, right):
    return dot(left, right, ((0,), (0,)))


def layer_norm(inputs, gain_vec, bias_vec):
    center = inputs - jnp.mean(inputs, axis=-1, keepdims=True)
    spread = jnp.mean(center * center, axis=-1, keepdims=True)
    return center * lax.rsqrt(spread + EPS) * gain_vec + bias_vec


def rotary_tables(length):
    half = ROT // 2
    inverse = np.float32(10000.0) ** (-np.arange(0, ROT, 2, dtype=np.float32) / np.float32(ROT))
    phase = np.arange(length, dtype=np.float32)[:, None] * inverse[None, :].astype(np.float32)
    cosine, sine = np.cos(phase), np.sin(phase)
    c = np.ones((length, HD), np.float32)
    s1 = np.zeros((length, HD), np.float32)
    s2 = np.zeros((length, HD), np.float32)
    c[:, :half] = cosine
    c[:, half:ROT] = cosine
    s1[:, :half] = -sine
    s2[:, half:ROT] = sine
    return tuple(np.concatenate([t, t], axis=1) for t in (c, s1, s2))


def turn(values, c, s1, s2):
    half = ROT // 2
    return (
        values * c
        + pltpu.roll(values, LANES - half, 1) * s1
        + pltpu.roll(values, half, 1) * s2
    )


def project_kernel(
    me, normed, cot, w_qkv, b_qkv, w_out, c_ref, s1_ref, s2_ref, out
):
    kind = pl.program_id(0)
    width = out.shape[-1]

    @pl.when(kind < 2)
    def _():
        full = dot(normed[...], w_qkv[...]) + b_qkv[...]
        c, s1, s2 = c_ref[...], s1_ref[...], s2_ref[...]
        for j in range(width // LANES):
            cols = slice(j * LANES, (j + 1) * LANES)
            out[0, :, cols] = turn(full[:, cols], c, s1, s2).astype(BF)

    @pl.when(kind == 2)
    def _():
        out[0] = (dot(normed[...], w_qkv[...]) + b_qkv[...]).astype(BF)

    @pl.when(kind == 3)
    def _():
        out[0] = back_dot(cot[...], w_out[...]).astype(BF)


def project(shift, me, normed, cot, w_qkv, b_qkv, w_out, tables, block_len, width, used):
    model = normed.shape[1]
    per = model // width

    def group(me_ref):
        return jnp.minimum(me_ref[0] ^ shift, used - 1)

    def rows(kind, me_ref):
        return (group(me_ref) // per, 0)

    def qkv_cols(kind, me_ref):
        return (0, jnp.minimum(kind, 2) * per + group(me_ref) % per)

    def own(kind, me_ref):
        return (0, 0)

    flops = 2 * 4 * block_len * model * width
    return pl.pallas_call(
        project_kernel,
        grid_spec=pltpu.PrefetchScalarGridSpec(
            num_scalar_prefetch=1,
            grid=(4,),
            in_specs=[
                pl.BlockSpec((block_len, model), rows),
                pl.BlockSpec((block_len, model), rows),
                pl.BlockSpec((model, width), qkv_cols),
                pl.BlockSpec((1, width), qkv_cols),
                pl.BlockSpec((width, model), lambda kind, me_ref: (group(me_ref) % per, 0)),
                pl.BlockSpec((block_len, LANES), own),
                pl.BlockSpec((block_len, LANES), own),
                pl.BlockSpec((block_len, LANES), own),
            ],
            out_specs=pl.BlockSpec((1, block_len, width), lambda kind, me_ref: (kind, 0, 0)),
        ),
        out_shape=jax.ShapeDtypeStruct((4, block_len, width), BF),
        compiler_params=pltpu.CompilerParams(vmem_limit_bytes=VMEM),
        cost_estimate=pl.CostEstimate(
            flops=flops, bytes_accessed=2 * (4 * model * width + 8 * block_len * width), transcendentals=0
        ),
        name="project",
    )(me, normed, cot, w_qkv, b_qkv, w_out, *tables)


def attend_kernel(n, block, me, *refs):
    ins = refs[:n]
    c_ref, s1_ref, s2_ref = refs[n : n + 3]
    outs = refs[n + 3 : 2 * n + 3]
    (q_s, k_s, v_s, g_s, qt_s, kt_s, vt_s, gt_s, sc, pb, dk, dv, o_s, dq_s) = refs[2 * n + 3 :]
    two = 2 * block
    scale = HD**-0.5

    for shift in range(n):
        at = ins[shift]
        place = me[0] ^ shift
        for kind, plain, flipped in ((0, q_s, qt_s), (1, k_s, kt_s), (2, v_s, vt_s), (3, g_s, gt_s)):
            piece = at[kind].astype(F32)
            if kind == 0:
                piece = piece * scale
            plain[place] = piece.astype(BF)
            flipped[place] = piece.T.astype(BF)

    lane = lax.broadcasted_iota(jnp.int32, (block, LANES), 1) < HD
    row = lax.broadcasted_iota(jnp.int32, (LANES, block), 0) < HD
    key_at = lax.broadcasted_iota(jnp.int32, (block, two), 0)
    query_at = lax.broadcasted_iota(jnp.int32, (block, two), 1)
    query_at = jnp.where(query_at >= block, query_at - block, query_at)
    allowed = key_at <= query_at

    def beside(flipped):
        zero = jnp.zeros_like(flipped)
        return jnp.concatenate([jnp.where(row, flipped, zero), jnp.where(row, zero, flipped)], axis=1)

    def below(plain):
        zero = jnp.zeros_like(plain)
        return jnp.concatenate([jnp.where(lane, plain, zero), jnp.where(lane, zero, plain)], axis=0)

    def loop(upto, body, init):
        if isinstance(upto, int):
            for j in range(upto):
                init = body(j, init)
            return init
        return lax.fori_loop(0, upto, body, init)

    def query_block(i, _):
        queries_t = beside(qt_s[i].astype(F32)).astype(BF)
        grads_t = beside(gt_s[i].astype(F32)).astype(BF)
        queries = below(q_s[i].astype(F32)).astype(BF)
        grads = below(g_s[i].astype(F32)).astype(BF)

        def score(j, top):
            found = dot(k_s[j], queries_t)
            sc[j] = found
            return jnp.maximum(top, jnp.max(found, axis=0, keepdims=True))

        diagonal = jnp.where(allowed, dot(k_s[i], queries_t), MASKED)
        sc[i] = diagonal
        top = loop(i, score, jnp.max(diagonal, axis=0, keepdims=True))

        def weigh(j, total):
            exps = jnp.exp(sc[j] - top)
            sc[j] = exps
            return total + jnp.sum(exps, axis=0, keepdims=True)

        total = loop(i + 1, weigh, jnp.zeros((1, two), F32))
        inverse = 1.0 / total

        def mix(j, heads):
            probs = sc[j] * inverse
            sc[j] = probs
            low = probs.astype(BF)
            pb[j] = low
            return tuple(
                heads[h] + dot(vt_s[j, h * HD : (h + 1) * HD], low[:, h * block : (h + 1) * block])
                for h in range(2)
            )

        none = jnp.zeros((HD, block), F32)
        heads = loop(i + 1, mix, (none, none))
        delta = jnp.concatenate(
            [
                jnp.sum(heads[h] * gt_s[i, h * HD : (h + 1) * HD].astype(F32), axis=0, keepdims=True)
                for h in range(2)
            ],
            axis=1,
        )
        o_s[i] = jnp.concatenate(heads, axis=0).T.astype(BF)

        def back(j, found, first):
            grad_scores = (sc[j] * (dot(v_s[j], grads_t) - delta)).astype(BF)
            key_part = dot(grad_scores, queries)
            value_part = dot(pb[j], grads)
            if first:
                dk[j] = key_part
                dv[j] = value_part
            else:
                dk[j] = dk[j] + key_part
                dv[j] = dv[j] + value_part
            return tuple(
                found[h]
                + dot(kt_s[j, h * HD : (h + 1) * HD], grad_scores[:, h * block : (h + 1) * block])
                for h in range(2)
            )

        found = back(i, (none, none), True)
        found = loop(i, lambda j, kept: back(j, kept, False), found)
        grad_query = jnp.concatenate(found, axis=0).T * scale
        dq_s[i] = turn(grad_query, c_ref[i], -s1_ref[i], -s2_ref[i]).astype(BF)
        return 0

    if n <= 4:
        for i in range(n):
            query_block(i, 0)
    else:
        lax.fori_loop(0, n, query_block, 0)

    for shift in range(n):
        place = me[0] ^ shift
        c, s1, s2 = c_ref[place], -s1_ref[place], -s2_ref[place]
        outs[shift][0] = o_s[place]
        outs[shift][1] = dq_s[place]
        outs[shift][2] = turn(dk[place], c, s1, s2).astype(BF)
        outs[shift][3] = dv[place].astype(BF)


def attend(n, me, pieces, tables):
    _, block, width = pieces[0].shape
    length = n * block
    spec = pl.BlockSpec((4, block, LANES), lambda j, me_ref: (0, 0, j))
    table_spec = pl.BlockSpec((n, block, LANES), lambda j, me_ref: (0, 0, 0))
    plain = pltpu.VMEM((n, block, LANES), BF)
    flipped = pltpu.VMEM((n, LANES, block), BF)
    total = pltpu.VMEM((n, block, LANES), F32)
    work = width // HD * length * (length + block) // 2
    return pl.pallas_call(
        functools.partial(attend_kernel, n, block),
        grid_spec=pltpu.PrefetchScalarGridSpec(
            num_scalar_prefetch=1,
            grid=(width // LANES,),
            in_specs=[spec] * n + [table_spec] * 3,
            out_specs=[spec] * n,
            scratch_shapes=[
                plain, plain, plain, plain,
                flipped, flipped, flipped, flipped,
                pltpu.VMEM((n, block, 2 * block), F32),
                pltpu.VMEM((n, block, 2 * block), BF),
                total, total, plain, plain,
            ],
        ),
        out_shape=[jax.ShapeDtypeStruct((4, block, width), BF)] * n,
        compiler_params=pltpu.CompilerParams(vmem_limit_bytes=VMEM),
        cost_estimate=pl.CostEstimate(
            flops=12 * work * 4 * HD, bytes_accessed=2 * 8 * length * width, transcendentals=work
        ),
        name="attend",
    )(me, *pieces, *(jnp.asarray(t).reshape(n, block, LANES) for t in tables))


def mlp_kernel(normed, cot, w_up, b_up, w_down, out, grad_in, grad_up, grad_down, grad_b):
    step = pl.program_id(0)
    hidden = dot(normed[...], w_up[...]) + b_up[...]
    share = 0.5 + 0.5 * lax.erf(hidden * (0.5**0.5))
    slope = share + hidden * (jnp.exp(-0.5 * hidden * hidden) * ((2.0 * np.pi) ** -0.5))
    active = (hidden * share).astype(BF)
    grad_hidden_f = back_dot(cot[...], w_down[...]) * slope
    grad_hidden = grad_hidden_f.astype(BF)
    grad_b[...] = jnp.sum(grad_hidden.astype(F32), axis=0, keepdims=True)
    mixed = dot(active, w_down[...])
    back = back_dot(grad_hidden, w_up[...])

    @pl.when(step == 0)
    def _():
        out[...] = mixed
        grad_in[...] = back

    @pl.when(step > 0)
    def _():
        out[...] = out[...] + mixed
        grad_in[...] = grad_in[...] + back

    grad_down[...] = outer_sum(active, cot[...]).astype(BF)
    grad_up[...] = outer_sum(normed[...], grad_hidden).astype(BF)


def mlp(normed, cot, w_up, b_up, w_down):
    rows, model = normed.shape
    hidden = w_up.shape[1]
    chunk = 384
    whole = pl.BlockSpec((rows, model), lambda j: (0, 0))
    tall = pl.BlockSpec((model, chunk), lambda j: (0, j))
    flat = pl.BlockSpec((chunk, model), lambda j: (j, 0))
    line = pl.BlockSpec((1, chunk), lambda j: (0, j))
    return pl.pallas_call(
        mlp_kernel,
        grid=(hidden // chunk,),
        in_specs=[whole, whole, tall, line, flat],
        out_specs=[whole, whole, tall, flat, line],
        out_shape=[
            jax.ShapeDtypeStruct((rows, model), F32),
            jax.ShapeDtypeStruct((rows, model), F32),
            jax.ShapeDtypeStruct((model, hidden), BF),
            jax.ShapeDtypeStruct((hidden, model), BF),
            jax.ShapeDtypeStruct((1, hidden), F32),
        ],
        compiler_params=pltpu.CompilerParams(vmem_limit_bytes=VMEM),
        cost_estimate=pl.CostEstimate(
            flops=12 * rows * model * hidden,
            bytes_accessed=8 * model * hidden + 12 * rows * model,
            transcendentals=2 * rows * hidden,
        ),
        name="mlp",
    )(normed, cot, w_up, b_up, w_down)


def swap(value, shift, n):
    return lax.ppermute(value, "ctx", [(i, i ^ shift) for i in range(n)])


def sum_over_ctx(shard, n):
    me = lax.axis_index("ctx")
    rows = shard.shape[0] // n
    parts = shard.reshape((n, rows) + shard.shape[1:])

    def part(at):
        return lax.dynamic_index_in_dim(parts, at, 0, keepdims=False)

    total = part(me).astype(F32)
    for shift in range(1, n):
        total = total + swap(part(me ^ shift), shift, n).astype(F32)
    own = total.astype(BF)
    gathered = jnp.stack([own] + [swap(own, shift, n) for shift in range(1, n)])
    return jnp.stack(
        [lax.dynamic_index_in_dim(gathered, me ^ at, 0, keepdims=False) for at in range(n)]
    ).reshape(shard.shape)


def body(
    tokens,
    norm1_gain,
    norm1_bias,
    norm2_gain,
    norm2_bias,
    qkv_weight,
    qkv_bias,
    out_weight,
    out_bias,
    up_weight,
    up_bias,
    down_weight,
    down_bias,
    cotangent,
):
    block_len, seq_count, model = tokens.shape
    n = lax.axis_size("ctx")
    shards = lax.axis_size("fsdp")
    rows = block_len * seq_count
    hidden = up_weight.shape[1]
    me = lax.axis_index("ctx")
    me_arr = me.astype(jnp.int32).reshape(1)
    width = -(-seq_count * model // (n * LANES)) * LANES
    used = seq_count * model // width
    per = model // width

    vectors = (
        norm1_gain, norm1_bias, norm2_gain, norm2_bias, qkv_bias, out_bias, up_bias, down_bias,
    )
    sizes = [v.shape[0] for v in vectors]
    packed = jnp.concatenate(vectors)
    lines = 16
    packed = jnp.pad(packed, (0, lines * model - packed.shape[0])).reshape(lines, model)
    own_rows = out_weight.shape[0]
    out_every = lax.all_gather(
        jnp.concatenate([out_weight, packed], axis=0), "fsdp", axis=0, tiled=False
    )
    w_qkv = lax.all_gather(qkv_weight, "fsdp", axis=0, tiled=True)
    w_up = lax.all_gather(up_weight, "fsdp", axis=0, tiled=True)
    w_down = lax.all_gather(down_weight, "fsdp", axis=0, tiled=True)
    w_out = out_every[:, :own_rows].reshape(model, model)
    flat = out_every[:, own_rows:].reshape(shards, lines * model)
    whole, start = [], 0
    for size in sizes:
        whole.append(flat[:, start : start + size].reshape(shards * size).astype(F32))
        start += size
    gain_one, bias_one, gain_two, bias_two, b_qkv, b_out, b_up, b_down = whole

    inputs_low = tokens.transpose(1, 0, 2).reshape(rows, model)
    inputs = inputs_low.astype(F32)
    cot = cotangent.transpose(1, 0, 2).reshape(rows, model)
    cot_f = cot.astype(F32)
    normed_one = layer_norm(inputs, gain_one, bias_one).astype(BF)
    normed_two = layer_norm(inputs, gain_two, bias_two).astype(BF)

    tables = rotary_tables(n * block_len)
    own_tables = tuple(
        lax.dynamic_slice_in_dim(jnp.asarray(t), me * block_len, block_len, 0) for t in tables
    )

    def made(shift):
        return project(
            shift, me_arr, normed_one, cot, w_qkv, b_qkv.reshape(1, -1), w_out, own_tables,
            block_len, width, used,
        )

    pieces = [None] * n
    for shift in list(range(1, n)) + [0]:
        pieces[shift] = made(shift) if shift == 0 else swap(made(shift), shift, n)
    answers = attend(n, me_arr, pieces, tables)
    answers = jnp.stack(
        [answers[0]] + [swap(answers[shift], shift, n) for shift in range(1, n)]
    )
    by_group = jnp.stack(
        [lax.dynamic_index_in_dim(answers, me ^ at, 0, keepdims=False) for at in range(used)]
    )
    by_kind = (
        by_group.reshape(seq_count, per, 4, block_len, width)
        .transpose(2, 0, 3, 1, 4)
        .reshape(4, rows, model)
    )
    mixed_heads = by_kind[0]

    mlp_out, grad_two, grad_up, grad_down, grad_up_b = mlp(
        normed_two, cot, w_up, b_up.reshape(1, -1), w_down
    )
    attn_branch = jnp.dot(mixed_heads, w_out, preferred_element_type=F32) + b_out
    layer_out = (
        (inputs + attn_branch + mlp_out + b_down)
        .astype(BF)
        .reshape(seq_count, block_len, model)
        .transpose(1, 0, 2)
    )
    column_sums = jnp.sum(cot_f, axis=0)
    grad_out = outer_sum(mixed_heads, cot)
    grad_kinds = [outer_sum(normed_one, by_kind[t]) for t in (1, 2, 3)]
    grad_qkv_b = jnp.concatenate([jnp.sum(by_kind[t].astype(F32), axis=0) for t in (1, 2, 3)])
    grad_one = sum(
        back_dot(by_kind[t], w_qkv[:, (t - 1) * model : t * model]) for t in (1, 2, 3)
    )
    _, norm_back_one = jax.vjp(layer_norm, inputs, gain_one, bias_one)
    grad_in_one, grad_gain_one, grad_bias_one = norm_back_one(grad_one)
    _, norm_back_two = jax.vjp(layer_norm, inputs, gain_two, bias_two)
    grad_in_two, grad_gain_two, grad_bias_two = norm_back_two(grad_two)
    tokens_grad = (
        (cot_f + grad_in_one + grad_in_two)
        .astype(BF)
        .reshape(seq_count, block_len, model)
        .transpose(1, 0, 2)
    )

    grad_vectors = (
        grad_gain_one, grad_bias_one, grad_gain_two, grad_bias_two, grad_qkv_b, column_sums,
        grad_up_b.reshape(-1),
    )
    grad_sizes = [v.shape[0] // shards for v in grad_vectors]
    grad_lines = 32
    packed_grads = jnp.concatenate([v.reshape(shards, -1) for v in grad_vectors], axis=1)
    packed_grads = jnp.pad(
        packed_grads, ((0, 0), (0, grad_lines * model - packed_grads.shape[1]))
    ).reshape(shards, grad_lines, model)
    last = jnp.concatenate(
        [g.astype(BF).reshape(shards, own_rows, model) for g in grad_kinds + [grad_out]]
        + [packed_grads.astype(BF)],
        axis=1,
    ).reshape(-1, model)

    def shard_sum(value):
        return lax.psum_scatter(value, "fsdp", scatter_dimension=0, tiled=True)

    part_down = sum_over_ctx(shard_sum(grad_down), n).astype(F32)
    part_up = sum_over_ctx(shard_sum(grad_up), n).astype(F32)
    part_last = sum_over_ctx(shard_sum(last), n).astype(F32)
    part_qkv = jnp.concatenate(
        [part_last[t * own_rows : (t + 1) * own_rows] for t in range(3)], axis=1
    )
    part_out = part_last[3 * own_rows : 4 * own_rows]
    line_sums = part_last[4 * own_rows :].reshape(-1)
    found, start = [], 0
    for size in grad_sizes:
        found.append(line_sums[start : start + size])
        start += size
    gain1, bias1, gain2, bias2, qkv_b, columns, up_b = found
    return (
        layer_out, tokens_grad, gain1, bias1, gain2, bias2, part_qkv, qkv_b, part_out, columns,
        part_up, up_b, part_down, columns,
    )


def solution(mesh):
    blocks = P("ctx", "fsdp", None)
    line, matrix = P("fsdp"), P("fsdp", None)
    return jax.shard_map(
        body,
        mesh=mesh,
        in_specs=(
            blocks, line, line, line, line, matrix, line, matrix, line, matrix, line, matrix, line,
            blocks,
        ),
        out_specs=(
            blocks, blocks, line, line, line, line, matrix, line, matrix, line, matrix, line,
            matrix, line,
        ),
        check_vma=False,
    )
```

time: 813 us -> 415 us (0.51)
  matrix products: 169 us -> 8.51 us
  blocking collectives: 120 us -> 0 us
  local copies, waits for them, and re-layouts: 139 us -> 38.9 us
  waiting for transfers between devices: 309 us -> 224 us
  Pallas kernels: 0 us -> 70.2 us
  starting transfers between devices: 13.1 us -> 28.7 us
  loops' own time: 8.38 us -> 0 us
    reduce_scatter x4 -> x3, waiting for transfers between devices: 214 us -> 21.5 us  [shard_sum(): return lax.psum_scatter(value, 'fsdp', scatter_dimension=0, tiled=True)]
    dot_general x28 -> x8, matrix products: 169 us -> 8.51 us  [the longest x7 6.2 us: dot(): lax.dot_general(left, right, (dims, ((), ())), preferred_element_type=F32)]
    pallas_call x0 -> x6, Pallas kernels: none -> 70.2 us  [the longest x1 28.9 us: mlp(): pl.pallas_call(mlp_kernel, grid=(hidden // chunk,), in_specs=[whole, whol...]
    ppermute x0 -> x24, waiting for transfers between devices: none -> 69.4 us  [swap(): return lax.ppermute(value, 'ctx', [(i, i ^ shift) for i in range(n)])]
    all_gather x8 -> x4, waiting for transfers between devices: 63.3 us -> 131 us  [the longest x1 52.2 us: body(): w_up = lax.all_gather(up_weight, 'fsdp', axis=0, tiled=True)]
    unnamed x2 -> x0, blocking collectives: 58.7 us -> none
    all_gather x3 -> x0, blocking collectives: 50.6 us -> none  [the longest x1 28.7 us: body(): lax.all_gather(total_send, 'ctx', axis=0, tiled=True)]
    unnamed x141 -> x55, local copies, waits for them, and re-layouts: 45.2 us -> 11.4 us
  transfers between devices with their start and end apart: 13 -> 31, of which waited for: 7 -> 19; matrix products, arithmetic and copies ran while one was open for 40% -> 12% of each run, Pallas kernels for 0% -> 17%
where the time goes in v1:
time: 415 us; the launch traced here: 409 us
  waiting for transfers between devices  224 us (54%)
  Pallas kernels  70.2 us (17%)
  local copies, waits for them, and re-layouts  38.9 us (9%)
  starting transfers between devices  28.7 us (7%)
  other arithmetic  23.4 us (6%)
  between operations  14.9 us (4%)
  matrix products  8.51 us (2%)
    ppermute x24, waiting for transfers between devices, swap(): return lax.ppermute(value, 'ctx', [(i, i ^ shift) for i in range(n)])  69.4 us
    all_gather x1, waiting for transfers between devices, body(): w_up = lax.all_gather(up_weight, 'fsdp', axis=0, tiled=True)  52.2 us
    all_gather x1, waiting for transfers between devices, body(): w_down = lax.all_gather(down_weight, 'fsdp', axis=0, tiled=True)  49 us
    pallas_call x1, Pallas kernels, mlp(): pl.pallas_call(mlp_kernel, grid=(hidden // chunk,), in_specs=[whole, whol...  28.9 us
    ppermute x24, starting transfers between devices, swap(): return lax.ppermute(value, 'ctx', [(i, i ^ shift) for i in range(n)])  27.9 us
    all_gather x1, waiting for transfers between devices, body(): lax.all_gather(jnp.concatenate([out_weight, packed], axis=0), 'fsdp', axi...  23.2 us
    pallas_call x1, Pallas kernels, attend(): pl.pallas_call(functools.partial(attend_kernel, n, block), grid_spec=pltp...  21.6 us
    reduce_scatter x3, waiting for transfers between devices, shard_sum(): return lax.psum_scatter(value, 'fsdp', scatter_dimension=0, tiled=True)  21.5 us
  transfers between devices with their start and end apart: 31, of which 19 were waited for; matrix products, arithmetic and copies ran while one was open for 12% of the time, Pallas kernels for 17%

profile of v1, /device:TPU:0, one launch (start us, length us, event | category | flops | bytes accessed | tf_op | source)
XLA Modules:
  0.0 409.0 jit_solution(854814523649172466)
XLA Ops:
  7.2 5.5 %concatenate.20 = bf16[1248]{0:T(1024)(128)(2,1)S(1)} concatenate(bf16[96]{0:T(256)(128)(2,1)} %param.18, bf16[96]{0:T(256)(128)(2,1)} %param.19, bf16[96]{0:T(256)(128)(2,1)} %param.20, bf16[96]{0:T(256)(128)(2,1)} %param.21, bf16[288]{0:T(512)(128)(2,1)} %param.23, bf16[96]{0:T(256)(128)(2,1)} %param.25, bf16[384]{0:T(512)(128)(2,1)} %param.27, bf16[96]{0:T(256)(128)(2,1)} %param.29), dimensions={0} | concatenate | bytes 4992 | tf_op jit(solution)/shard_map/concatenate | solution.py:393
  12.8 1.6 pad_maximum_fusion.9
  18.1 23.2 %all-gather.12.cloned.1.call-done = bf16[896,768]{1,0:T(8,128)(2,1)} async-done(((bf16[112,768]{1,0:T(8,128)(2,1)}), bf16[896,768]{1,0:T(8,128)(2,1)}) %all-gather.12.cloned.1.call-update) | async-done | bytes 1376272 | tf_op jit(solution)/shard_map/all_gather | solution.py:397
  43.3 1.6 fusion.18
  44.9 49.0 %all-gather.10.cloned.1.call-done.w_down = bf16[3072,768]{1,0:T(8,128)(2,1)} async-done(((bf16[384,768]{1,0:T(8,128)(2,1)}), bf16[3072,768]{1,0:T(8,128)(2,1)}) %all-gather.10.cloned.1.call-update) | async-done | bytes 4718608 | tf_op jit(solution)/shard_map/all_gather | solution.py:402
  94.0 52.2 %all-gather.8.cloned.1.call-done.w_up = bf16[768,3072]{1,0:T(8,128)(2,1)} async-done(((bf16[96,3072]{1,0:T(8,128)(2,1)}), bf16[768,3072]{1,0:T(8,128)(2,1)}) %all-gather.8.cloned.1.call-update) | async-done | bytes 4718608 | tf_op jit(solution)/shard_map/all_gather | solution.py:401
  146.2 28.9 %mlp.1 = (f32[512,768]{1,0:T(8,128)}, f32[512,768]{1,0:T(8,128)}, bf16[768,3072]{1,0:T(8,128)(2,1)}, bf16[3072,768]{1,0:T(8,128)(2,1)}, f32[1,3072]{1,0:T(1,128)}) custom-call(bf16[512,768]{1,0:T(8,128)(2,1)} %get-tuple-element.58.normed, bf16[512,768]{1,0:T(8,128)(2,1)} %bitcast.197, bf16[768,3072]{1,0:T(8,128)(2,1)} %all-gather.8.cloned.1.call-done.w_up, ...), custom_call_target="tpu_custom_call" | custom-call | flops 14495514624 | bytes 23592960 | tf_op jit(solution)/shard_map/mlp/pallas_call | solution.py:318
  176.3 1.6 constant_dynamic-slice_fusion.18.c_ref
  177.8 1.7 constant_dynamic-slice_fusion.16
  179.5 1.1 slice.130
  181.3 6.7 %all-gather.6.cloned.1.call-done.w_qkv = bf16[768,2304]{1,0:T(8,128)(2,1)} async-done(((bf16[96,2304]{1,0:T(8,128)(2,1)}), bf16[768,2304]{1,0:T(8,128)(2,1)}) %all-gather.6.cloned.1.call-update) | async-done | bytes 3538960 | tf_op jit(solution)/shard_map/all_gather | solution.py:400
  188.0 4.8 %project.5 = bf16[4,256,384]{2,1,0:T(8,128)(2,1)} custom-call(s32[1]{0:T(128)} %bitcast.2.me, bf16[512,768]{1,0:T(8,128)(2,1)} %get-tuple-element.57.normed, bf16[512,768]{1,0:T(8,128)(2,1)} %bitcast.198, bf16[768,2304]{1,0:T(8,128)(2,1)} %all-gather.6.cloned.1.call-done.w_qkv, f32[1,2304]{1,0:T(1,128)} %reshape.387.b_qkv, bf16[768,768]{1,0:T(8,128)(2,1)} %bitcast.192, ...), custom_call_target="tpu_custom_call" | custom-call | flops 603979776 | bytes 3932160 | tf_op jit(solution)/shard_map/project/pallas_call | solution.py:104
  192.8 1.5 collective-permute-start
  194.3 5.1 %project.6 = bf16[4,256,384]{2,1,0:T(8,128)(2,1)} custom-call(s32[1]{0:T(128)} %bitcast.2.me, bf16[512,768]{1,0:T(8,128)(2,1)} %get-tuple-element.57.normed, bf16[512,768]{1,0:T(8,128)(2,1)} %bitcast.199, bf16[768,2304]{1,0:T(8,128)(2,1)} %all-gather.6.cloned.1.call-done.w_qkv, f32[1,2304]{1,0:T(1,128)} %reshape.387.b_qkv, bf16[768,768]{1,0:T(8,128)(2,1)} %bitcast.193, ...), custom_call_target="tpu_custom_call" | custom-call | flops 603979776 | bytes 3932160 | tf_op jit(solution)/shard_map/project/pallas_call | solution.py:104
  199.4 1.6 collective-permute-start.1
  201.0 4.9 %project.7 = bf16[4,256,384]{2,1,0:T(8,128)(2,1)} custom-call(s32[1]{0:T(128)} %bitcast.2.me, bf16[512,768]{1,0:T(8,128)(2,1)} %get-tuple-element.57.normed, bf16[512,768]{1,0:T(8,128)(2,1)} %bitcast.200, bf16[768,2304]{1,0:T(8,128)(2,1)} %all-gather.6.cloned.1.call-done.w_qkv, f32[1,2304]{1,0:T(1,128)} %reshape.387.b_qkv, bf16[768,768]{1,0:T(8,128)(2,1)} %bitcast.194, ...), custom_call_target="tpu_custom_call" | custom-call | flops 603979776 | bytes 3932160 | tf_op jit(solution)/shard_map/project/pallas_call | solution.py:104
  206.1 4.8 %project.4.refs_0_ = bf16[4,256,384]{2,1,0:T(8,128)(2,1)} custom-call(s32[1]{0:T(128)} %bitcast.2.me, bf16[512,768]{1,0:T(8,128)(2,1)} %get-tuple-element.57.normed, bf16[512,768]{1,0:T(8,128)(2,1)} %bitcast.201, bf16[768,2304]{1,0:T(8,128)(2,1)} %all-gather.6.cloned.1.call-done.w_qkv, f32[1,2304]{1,0:T(1,128)} %reshape.387.b_qkv, ...), custom_call_target="tpu_custom_call" | custom-call | flops 603979776 | bytes 3932160 | tf_op jit(solution)/shard_map/project/pallas_call | solution.py:104
  210.9 2.5 collective-permute-done.refs_1_
  213.4 22.6 %collective-permute-done.1.refs_2_ = bf16[4,256,384]{2,1,0:T(8,128)(2,1)S(1)} collective-permute-done((bf16[4,256,384]{2,1,0:T(8,128)(2,1)}, bf16[4,256,384]{2,1,0:T(8,128)(2,1)S(1)}, u32[]{:S(2)}, u32[]{:S(2)}) %collective-permute-start.1) | collective-permute-done | bytes 786464 | tf_op jit(solution)/shard_map/ppermute | solution.py:341
  237.8 21.6 %attend.1 = (bf16[4,256,384]{2,1,0:T(8,128)(2,1)}, bf16[4,256,384]{2,1,0:T(8,128)(2,1)}, bf16[4,256,384]{2,1,0:T(8,128)(2,1)}, bf16[4,256,384]{2,1,0:T(8,128)(2,1)}) custom-call(s32[1]{0:T(128)} %bitcast.2.me, bf16[4,256,384]{2,1,0:T(8,128)(2,1)} %project.4.refs_0_, bf16[4,256,384]{2,1,0:T(8,128)(2,1)} %copy-done.17, bf16[4,256,384]{2,1,0:T(8,128)(2,1)} %copy-done.18, ...), custom_call_target="tpu_custom_call" | custom-call | flops 12079595520 | bytes 6291456 | tf_op jit(solution)/shard_map/attend/pallas_call | solution.py:260
  259.4 1.5 collective-permute-start.4
  261.1 1.9 collective-permute-start.3
  263.8 1.2 fusion.16
  265.0 30.4 %collective-permute-done.4 = bf16[4,256,384]{2,1,0:T(8,128)(2,1)S(1)} collective-permute-done((bf16[4,256,384]{2,1,0:T(8,128)(2,1)}, bf16[4,256,384]{2,1,0:T(8,128)(2,1)S(1)}, u32[]{:S(2)}, u32[]{:S(2)}) %collective-permute-start.4) | collective-permute-done | bytes 786464 | tf_op jit(solution)/shard_map/ppermute | solution.py:341
  295.4 1.3 collective-permute-done.3
  296.7 1.6 pad_maximum_fusion
  299.4 3.2 copy.73
  302.6 3.8 slice_reduce_fusion.2
  306.6 1.3 copy.48
  311.8 1.0 copy-done.3
  313.8 1.1 copy-done
  318.1 1.3 fusion.48
  319.4 1.5 fusion.22
  323.3 3.2 add_convert_fusion
  326.7 1.9 dynamic-slice_bitcast_fusion.5
  328.9 1.5 collective-permute-start.19
  330.3 1.8 collective-permute-start.20
  332.1 1.1 dynamic-slice_bitcast_fusion.8
  333.5 1.5 collective-permute-start.13
  335.2 1.6 collective-permute-start.14
  336.8 2.2 collective-permute-done.20
  338.9 1.1 fusion.38
  340.0 1.3 collective-permute-start.21
  341.3 2.1 collective-permute-start.22
  343.6 1.5 collective-permute-done.14
  345.1 1.0 fusion.41
  346.1 1.8 collective-permute-start.15
  347.9 1.8 collective-permute-start.16
  349.7 2.3 fusion.27
  352.0 1.7 copy.74
  353.7 1.7 copy.75
  355.9 1.2 bitcast_convert_fusion.2
  357.0 21.5 %reduce-scatter.4.cloned.1.call-done = bf16[416,768]{1,0:T(8,128)(2,1)} async-done(((bf16[3328,768]{1,0:T(8,128)(2,1)}), bf16[416,768]{1,0:T(8,128)(2,1)}) %reduce-scatter.4.cloned.1.call-update) | async-done | bytes 638992 | tf_op jit(solution)/shard_map/reduce_scatter | solution.py:491
  378.5 1.1 dynamic-slice_bitcast_fusion.2
  379.6 1.5 collective-permute-start.6
  381.2 1.5 collective-permute-start.7
  383.3 2.5 collective-permute-done.6
  385.8 1.5 collective-permute-done.7
  387.3 1.6 collective-permute-done.8
  388.8 1.0 fusion.35
  391.3 2.1 collective-permute-start.11
  393.4 1.1 bitcast_convert_fusion.1
  395.7 1.7 collective-permute-done.11
  400.4 1.0 pad_maximum_fusion.2
  (152 shorter events, 30.2 us)
Async XLA Ops:
  7.2 9.4 %copy-start.1 = (bf16[256,2,768]{2,1,0:T(2,128)(2,1)S(1)}, bf16[256,2,768]{2,1,0:T(2,128)(2,1)}, u32[]{:S(2)}) copy-start(bf16[256,2,768]{2,1,0:T(2,128)(2,1)} %param.17) | copy-start | bytes 2359300
  7.2 34.1 %all-gather.12.cloned.1.call-start = ((), (), s32[]{:S(2)}) async-start(), calls=%async_computation.9 | async-start | bytes 1548288 | tf_op jit(solution)/shard_map/all_gather | solution.py:397
  14.4 2.7 copy-start.8
  14.5 79.5 %all-gather.10.cloned.1.call-start = ((), (), s32[]{:S(2)}) async-start(), calls=%async_computation.5 | async-start | bytes 5308416 | tf_op jit(solution)/shard_map/all_gather | solution.py:402
  15.2 130.9 %all-gather.8.cloned.1.call-start = ((), (), s32[]{:S(2)}) async-start(), calls=%async_computation.4 | async-start | bytes 5308416 | tf_op jit(solution)/shard_map/all_gather | solution.py:401
  15.9 172.1 %all-gather.6.cloned.1.call-start = ((), (), s32[]{:S(2)}) async-start(), calls=%async_computation.3 | async-start | bytes 3981312 | tf_op jit(solution)/shard_map/all_gather | solution.py:400
  16.5 310.1 %reduce-scatter.8.cloned.1.call-start = ((), (), s32[]{:S(2)}) async-start(), calls=%async_computation.8 | async-start | bytes 5308416 | tf_op jit(solution)/shard_map/reduce_scatter | solution.py:491
  175.1 157.0 %reduce-scatter.6.cloned.1.call-start = ((), (), s32[]{:S(2)}) async-start(), calls=%async_computation.7 | async-start | bytes 5308416 | tf_op jit(solution)/shard_map/reduce_scatter | solution.py:491
  175.2 4.4 %copy-start.9 = (bf16[896,768]{1,0:T(8,128)(2,1)S(1)}, bf16[896,768]{1,0:T(8,128)(2,1)}, u32[]{:S(2)}) copy-start(bf16[896,768]{1,0:T(8,128)(2,1)} %all-gather.12.cloned.1.call-done) | copy-start | bytes 4128772
  175.7 202.8 %reduce-scatter.4.cloned.1.call-start = ((), (), s32[]{:S(2)}) async-start(), calls=%async_computation.6 | async-start | bytes 5750784 | tf_op jit(solution)/shard_map/reduce_scatter | solution.py:491
  192.8 20.6 %collective-permute-start = (bf16[4,256,384]{2,1,0:T(8,128)(2,1)}, bf16[4,256,384]{2,1,0:T(8,128)(2,1)S(1)}, u32[]{:S(2)}, u32[]{:S(2)}) collective-permute-start(bf16[4,256,384]{2,1,0:T(8,128)(2,1)} %project.5), channel_id=1, source_target_pairs={{0,8},{8,0},{16,24},{24,16},{1,9},{9,1},{17,25},{25,17},{2,10},{10... | collective-permute-start | bytes 2359304 | tf_op jit(solution)/shard_map/ppermute | solution.py:341
  199.4 36.6 %collective-permute-start.1 = (bf16[4,256,384]{2,1,0:T(8,128)(2,1)}, bf16[4,256,384]{2,1,0:T(8,128)(2,1)S(1)}, u32[]{:S(2)}, u32[]{:S(2)}) collective-permute-start(bf16[4,256,384]{2,1,0:T(8,128)(2,1)} %project.6), channel_id=1, source_target_pairs={{0,16},{8,24},{16,0},{24,8},{1,17},{9,25},{17,1},{25,9},{2,18},{10... | collective-permute-start | bytes 2359304 | tf_op jit(solution)/shard_map/ppermute | solution.py:341
  205.9 30.1 %collective-permute-start.2 = (bf16[4,256,384]{2,1,0:T(8,128)(2,1)}, bf16[4,256,384]{2,1,0:T(8,128)(2,1)S(1)}, u32[]{:S(2)}, u32[]{:S(2)}) collective-permute-start(bf16[4,256,384]{2,1,0:T(8,128)(2,1)} %project.7), channel_id=1, source_target_pairs={{0,24},{8,16},{16,8},{24,0},{1,25},{9,17},{17,9},{25,1},{2,26},{10... | collective-permute-start | bytes 2359304 | tf_op jit(solution)/shard_map/ppermute | solution.py:341
  213.4 22.6 %copy-start.17 = (bf16[4,256,384]{2,1,0:T(8,128)(2,1)}, bf16[4,256,384]{2,1,0:T(8,128)(2,1)S(1)}, u32[]{:S(2)}) copy-start(bf16[4,256,384]{2,1,0:T(8,128)(2,1)S(1)} %collective-permute-done.refs_1_) | copy-start | bytes 2359300
  236.0 0.9 copy-start.18
  236.9 0.9 copy-start.19
  259.4 37.3 %copy-start.10 = (bf16[4,256,384]{2,1,0:T(8,128)(2,1)S(1)}, bf16[4,256,384]{2,1,0:T(8,128)(2,1)}, u32[]{:S(2)}) copy-start(bf16[4,256,384]{2,1,0:T(8,128)(2,1)} %get-tuple-element.23) | copy-start | bytes 2359300
  259.4 36.0 %collective-permute-start.4 = (bf16[4,256,384]{2,1,0:T(8,128)(2,1)}, bf16[4,256,384]{2,1,0:T(8,128)(2,1)S(1)}, u32[]{:S(2)}, u32[]{:S(2)}) collective-permute-start(bf16[4,256,384]{2,1,0:T(8,128)(2,1)} %get-tuple-element.25), channel_id=1, source_target_pairs={{0,16},{8,24},{16,0},{24,8},{1,17},{9,25},{17,1},{25,9},{2,18},{10... | collective-permute-start | bytes 2359304 | tf_op jit(solution)/shard_map/ppermute | solution.py:341
  260.9 34.5 %collective-permute-start.5 = (bf16[4,256,384]{2,1,0:T(8,128)(2,1)}, bf16[4,256,384]{2,1,0:T(8,128)(2,1)}, u32[]{:S(2)}, u32[]{:S(2)}) collective-permute-start(bf16[4,256,384]{2,1,0:T(8,128)(2,1)} %get-tuple-element.26), channel_id=1, source_target_pairs={{0,24},{8,16},{16,8},{24,0},{1,25},{9,17},{17,9},{25,1},{2,26},{10... | collective-permute-start | bytes 2359304 | tf_op jit(solution)/shard_map/ppermute | solution.py:341
  261.1 35.6 %collective-permute-start.3 = (bf16[4,256,384]{2,1,0:T(8,128)(2,1)}, bf16[4,256,384]{2,1,0:T(8,128)(2,1)}, u32[]{:S(2)}, u32[]{:S(2)}) collective-permute-start(bf16[4,256,384]{2,1,0:T(8,128)(2,1)} %get-tuple-element.24), channel_id=1, source_target_pairs={{0,8},{8,0},{16,24},{24,16},{1,9},{9,1},{17,25},{25,17},{2,10},{10... | collective-permute-start | bytes 2359304 | tf_op jit(solution)/shard_map/ppermute | solution.py:341
  308.0 1.1 copy-start.14
  308.2 3.6 copy-start.11
  311.7 1.1 copy-start.3
  312.9 2.0 copy-start
  314.9 2.3 copy-start.6
  315.7 2.4 copy-start.4
  319.4 1.5 copy-start.5
  319.4 1.8 copy-start.15
  326.6 23.0 %copy-start.2 = (bf16[8,96,768]{2,1,0:T(8,128)(2,1)S(1)}, bf16[8,96,768]{2,1,0:T(8,128)(2,1)}, u32[]{:S(2)}) copy-start(bf16[8,96,768]{2,1,0:T(8,128)(2,1)} %slice.130) | copy-start | bytes 3538948
  326.6 23.0 %copy-start.12 = (bf16[64,8,2,384]{3,1,2,0:T(8,128)(2,1)S(1)}, bf16[64,8,2,384]{3,1,2,0:T(8,128)(2,1)}, u32[]{:S(2)}) copy-start(bf16[64,8,2,384]{3,1,2,0:T(8,128)(2,1)} %copy-done.11) | copy-start | bytes 2359300
  326.7 23.0 %copy-start.13 = (bf16[256,2,768]{2,0,1:T(8,128)(2,1)S(1)}, bf16[256,2,768]{2,0,1:T(8,128)(2,1)}, u32[]{:S(2)}) copy-start(bf16[256,2,768]{2,0,1:T(8,128)(2,1)} %copy.36) | copy-start | bytes 2359300
  328.6 6.6 %collective-permute-start.18 = (bf16[96,768]{1,0:T(8,128)(2,1)S(1)}, bf16[96,768]{1,0:T(8,128)(2,1)S(1)}, u32[]{:S(2)}, u32[]{:S(2)}) collective-permute-start(bf16[96,768]{1,0:T(8,128)(2,1)S(1)} %get-tuple-element.72), channel_id=1, source_target_pairs={{0,8},{8,0},{16,24},{24,16},{1,9},{9,1},{17,25},{25,17},{2,10},{10... | collective-permute-start | bytes 442376 | tf_op jit(solution)/shard_map/ppermute | solution.py:341
  328.9 7.9 %collective-permute-start.19 = (bf16[96,768]{1,0:T(8,128)(2,1)}, bf16[96,768]{1,0:T(8,128)(2,1)S(1)}, u32[]{:S(2)}, u32[]{:S(2)}) collective-permute-start(bf16[96,768]{1,0:T(8,128)(2,1)} %get-tuple-element.74), channel_id=1, source_target_pairs={{0,16},{8,24},{16,0},{24,8},{1,17},{9,25},{17,1},{25,9},{2,18},{10... | collective-permute-start | bytes 442376 | tf_op jit(solution)/shard_map/ppermute | solution.py:341
  330.3 8.6 %collective-permute-start.20 = (bf16[96,768]{1,0:T(8,128)(2,1)}, bf16[96,768]{1,0:T(8,128)(2,1)}, u32[]{:S(2)}, u32[]{:S(2)}) collective-permute-start(bf16[96,768]{1,0:T(8,128)(2,1)} %get-tuple-element.73), channel_id=1, source_target_pairs={{0,24},{8,16},{16,8},{24,0},{1,25},{9,17},{17,9},{25,1},{2,26},{10... | collective-permute-start | bytes 442376 | tf_op jit(solution)/shard_map/ppermute | solution.py:341
  333.2 10.2 %collective-permute-start.12 = (bf16[24,3072]{1,0:T(8,128)(2,1)S(1)}, bf16[24,3072]{1,0:T(8,128)(2,1)S(1)}, u32[]{:S(2)}, u32[]{:S(2)}) collective-permute-start(bf16[24,3072]{1,0:T(8,128)(2,1)S(1)} %get-tuple-element.79), channel_id=1, source_target_pairs={{0,8},{8,0},{16,24},{24,16},{1,9},{9,1},{17,25},{25,17},{2,10},{10... | collective-permute-start | bytes 442376 | tf_op jit(solution)/shard_map/ppermute | solution.py:341
  333.5 10.1 %collective-permute-start.13 = (bf16[24,3072]{1,0:T(8,128)(2,1)S(1)}, bf16[24,3072]{1,0:T(8,128)(2,1)S(1)}, u32[]{:S(2)}, u32[]{:S(2)}) collective-permute-start(bf16[24,3072]{1,0:T(8,128)(2,1)S(1)} %get-tuple-element.81), channel_id=1, source_target_pairs={{0,16},{8,24},{16,0},{24,8},{1,17},{9,25},{17,1},{25,9},{2,18},{10... | collective-permute-start | bytes 442376 | tf_op jit(solution)/shard_map/ppermute | solution.py:341
  335.2 9.9 %collective-permute-start.14 = (bf16[24,3072]{1,0:T(8,128)(2,1)S(1)}, bf16[24,3072]{1,0:T(8,128)(2,1)S(1)}, u32[]{:S(2)}, u32[]{:S(2)}) collective-permute-start(bf16[24,3072]{1,0:T(8,128)(2,1)S(1)} %get-tuple-element.80), channel_id=1, source_target_pairs={{0,24},{8,16},{16,8},{24,0},{1,25},{9,17},{17,9},{25,1},{2,26},{10... | collective-permute-start | bytes 442376 | tf_op jit(solution)/shard_map/ppermute | solution.py:341
  340.0 9.6 %collective-permute-start.21 = (bf16[96,768]{1,0:T(8,128)(2,1)S(1)}, bf16[96,768]{1,0:T(8,128)(2,1)S(1)}, u32[]{:S(2)}, u32[]{:S(2)}) collective-permute-start(bf16[96,768]{1,0:T(8,128)(2,1)S(1)} %fusion.38), channel_id=1, source_target_pairs={{0,8},{8,0},{16,24},{24,16},{1,9},{9,1},{17,25},{25,17},{2,10},{10... | collective-permute-start | bytes 442376 | tf_op jit(solution)/shard_map/ppermute | solution.py:341
  341.3 14.1 %collective-permute-start.22 = (bf16[96,768]{1,0:T(8,128)(2,1)S(1)}, bf16[96,768]{1,0:T(8,128)(2,1)S(1)}, u32[]{:S(2)}, u32[]{:S(2)}) collective-permute-start(bf16[96,768]{1,0:T(8,128)(2,1)S(1)} %fusion.38), channel_id=1, source_target_pairs={{0,16},{8,24},{16,0},{24,8},{1,17},{9,25},{17,1},{25,9},{2,18},{10... | collective-permute-start | bytes 442376 | tf_op jit(solution)/shard_map/ppermute | solution.py:341
  343.4 12.0 %collective-permute-start.23 = (bf16[96,768]{1,0:T(8,128)(2,1)S(1)}, bf16[96,768]{1,0:T(8,128)(2,1)S(1)}, u32[]{:S(2)}, u32[]{:S(2)}) collective-permute-start(bf16[96,768]{1,0:T(8,128)(2,1)S(1)} %fusion.38), channel_id=1, source_target_pairs={{0,24},{8,16},{16,8},{24,0},{1,25},{9,17},{17,9},{25,1},{2,26},{10... | collective-permute-start | bytes 442376 | tf_op jit(solution)/shard_map/ppermute | solution.py:341
  346.1 9.4 %collective-permute-start.15 = (bf16[24,3072]{1,0:T(8,128)(2,1)S(1)}, bf16[24,3072]{1,0:T(8,128)(2,1)S(1)}, u32[]{:S(2)}, u32[]{:S(2)}) collective-permute-start(bf16[24,3072]{1,0:T(8,128)(2,1)S(1)} %fusion.41), channel_id=1, source_target_pairs={{0,8},{8,0},{16,24},{24,16},{1,9},{9,1},{17,25},{25,17},{2,10},{10... | collective-permute-start | bytes 442376 | tf_op jit(solution)/shard_map/ppermute | solution.py:341
  347.9 7.6 %collective-permute-start.16 = (bf16[24,3072]{1,0:T(8,128)(2,1)S(1)}, bf16[24,3072]{1,0:T(8,128)(2,1)S(1)}, u32[]{:S(2)}, u32[]{:S(2)}) collective-permute-start(bf16[24,3072]{1,0:T(8,128)(2,1)S(1)} %fusion.41), channel_id=1, source_target_pairs={{0,16},{8,24},{16,0},{24,8},{1,17},{9,25},{17,1},{25,9},{2,18},{10... | collective-permute-start | bytes 442376 | tf_op jit(solution)/shard_map/ppermute | solution.py:341
  349.6 6.0 %collective-permute-start.17 = (bf16[24,3072]{1,0:T(8,128)(2,1)S(1)}, bf16[24,3072]{1,0:T(8,128)(2,1)S(1)}, u32[]{:S(2)}, u32[]{:S(2)}) collective-permute-start(bf16[24,3072]{1,0:T(8,128)(2,1)S(1)} %fusion.41), channel_id=1, source_target_pairs={{0,24},{8,16},{16,8},{24,0},{1,25},{9,17},{17,9},{25,1},{2,26},{10... | collective-permute-start | bytes 442376 | tf_op jit(solution)/shard_map/ppermute | solution.py:341
  349.7 2.3 copy-start.7
  379.6 6.2 %collective-permute-start.6 = (bf16[104,768]{1,0:T(8,128)(2,1)S(1)}, bf16[104,768]{1,0:T(8,128)(2,1)S(1)}, u32[]{:S(2)}, u32[]{:S(2)}) collective-permute-start(bf16[104,768]{1,0:T(8,128)(2,1)S(1)} %get-tuple-element.65), channel_id=1, source_target_pairs={{0,8},{8,0},{16,24},{24,16},{1,9},{9,1},{17,25},{25,17},{2,10},{10... | collective-permute-start | bytes 479240 | tf_op jit(solution)/shard_map/ppermute | solution.py:341
  381.2 6.1 %collective-permute-start.7 = (bf16[104,768]{1,0:T(8,128)(2,1)S(1)}, bf16[104,768]{1,0:T(8,128)(2,1)S(1)}, u32[]{:S(2)}, u32[]{:S(2)}) collective-permute-start(bf16[104,768]{1,0:T(8,128)(2,1)S(1)} %get-tuple-element.67), channel_id=1, source_target_pairs={{0,16},{8,24},{16,0},{24,8},{1,17},{9,25},{17,1},{25,9},{2,18},{10... | collective-permute-start | bytes 479240 | tf_op jit(solution)/shard_map/ppermute | solution.py:341
  382.7 6.2 %collective-permute-start.8 = (bf16[104,768]{1,0:T(8,128)(2,1)S(1)}, bf16[104,768]{1,0:T(8,128)(2,1)S(1)}, u32[]{:S(2)}, u32[]{:S(2)}) collective-permute-start(bf16[104,768]{1,0:T(8,128)(2,1)S(1)} %get-tuple-element.66), channel_id=1, source_target_pairs={{0,24},{8,16},{16,8},{24,0},{1,25},{9,17},{17,9},{25,1},{2,26},{10... | collective-permute-start | bytes 479240 | tf_op jit(solution)/shard_map/ppermute | solution.py:341
  389.8 5.3 %collective-permute-start.9 = (bf16[104,768]{1,0:T(8,128)(2,1)S(1)}, bf16[104,768]{1,0:T(8,128)(2,1)S(1)}, u32[]{:S(2)}, u32[]{:S(2)}) collective-permute-start(bf16[104,768]{1,0:T(8,128)(2,1)S(1)} %fusion.35), channel_id=1, source_target_pairs={{0,8},{8,0},{16,24},{24,16},{1,9},{9,1},{17,25},{25,17},{2,10},{10... | collective-permute-start | bytes 479240 | tf_op jit(solution)/shard_map/ppermute | solution.py:341
  390.5 5.3 %collective-permute-start.10 = (bf16[104,768]{1,0:T(8,128)(2,1)S(1)}, bf16[104,768]{1,0:T(8,128)(2,1)S(1)}, u32[]{:S(2)}, u32[]{:S(2)}) collective-permute-start(bf16[104,768]{1,0:T(8,128)(2,1)S(1)} %fusion.35), channel_id=1, source_target_pairs={{0,16},{8,24},{16,0},{24,8},{1,17},{9,25},{17,1},{25,9},{2,18},{10... | collective-permute-start | bytes 479240 | tf_op jit(solution)/shard_map/ppermute | solution.py:341
  391.3 6.2 %collective-permute-start.11 = (bf16[104,768]{1,0:T(8,128)(2,1)S(1)}, bf16[104,768]{1,0:T(8,128)(2,1)S(1)}, u32[]{:S(2)}, u32[]{:S(2)}) collective-permute-start(bf16[104,768]{1,0:T(8,128)(2,1)S(1)} %fusion.35), channel_id=1, source_target_pairs={{0,24},{8,16},{16,8},{24,0},{1,25},{9,17},{17,9},{25,1},{2,26},{10... | collective-permute-start | bytes 479240 | tf_op jit(solution)/shard_map/ppermute | solution.py:341
  399.2 2.6 copy-start.16
Sparse Core Ops, SparseCore 0:
  14.6 26.6 all-gather.11
  42.9 50.9 all-gather.9
  95.6 50.5 all-gather.7
  147.6 40.3 all-gather.5
  190.2 53.8 reduce-scatter.7
  246.2 53.3 reduce-scatter.5
  322.4 56.1 reduce-scatter.3

commit v2 on v1

--- a/solution.py
+++ b/solution.py
@@ -31,10 +31,22 @@
     return dot(left, right, ((0,), (0,)))
 
 
-def layer_norm(inputs, gain_vec, bias_vec):
-    center = inputs - jnp.mean(inputs, axis=-1, keepdims=True)
+def normalized(values):
+    center = values - jnp.mean(values, axis=-1, keepdims=True)
     spread = jnp.mean(center * center, axis=-1, keepdims=True)
-    return center * lax.rsqrt(spread + EPS) * gain_vec + bias_vec
+    inverse = lax.rsqrt(spread + EPS)
+    return center * inverse, inverse
+
+
+def norm_back(hat, inverse, gain, grad):
+    scaled = grad * gain
+    first = jnp.mean(scaled, axis=-1, keepdims=True)
+    second = jnp.mean(scaled * hat, axis=-1, keepdims=True)
+    return (
+        inverse * (scaled - first - hat * second),
+        jnp.sum(grad * hat, axis=0, keepdims=True),
+        jnp.sum(grad, axis=0, keepdims=True),
+    )
 
 
 def rotary_tables(length):
@@ -62,69 +74,81 @@
 
 
 def project_kernel(
-    me, normed, cot, w_qkv, b_qkv, w_out, c_ref, s1_ref, s2_ref, out
+    n, block_len, used, me, tokens, cot, gain, bias, w, b, c_ref, s1_ref, s2_ref, *rest
 ):
+    outs, normed = rest[:n], rest[n]
     kind = pl.program_id(0)
-    width = out.shape[-1]
+
+    @pl.when(kind == 0)
+    def _():
+        hat, _inverse = normalized(tokens[...].astype(F32))
+        normed[...] = (hat * gain[...] + bias[...]).astype(BF)
+
+    width = outs[0].shape[-1]
+    per = w.shape[-1] // width
+
+    def operands(shift, left):
+        group = jnp.minimum(me[0] ^ shift, used - 1)
+        rows = pl.multiple_of((group // per) * block_len, block_len)
+        cols = pl.multiple_of((group % per) * width, LANES)
+        return left[pl.ds(rows, block_len)], pl.ds(cols, width)
 
     @pl.when(kind < 2)
     def _():
-        full = dot(normed[...], w_qkv[...]) + b_qkv[...]
         c, s1, s2 = c_ref[...], s1_ref[...], s2_ref[...]
-        for j in range(width // LANES):
-            cols = slice(j * LANES, (j + 1) * LANES)
-            out[0, :, cols] = turn(full[:, cols], c, s1, s2).astype(BF)
+        for shift in range(n):
+            left, cols = operands(shift, normed)
+            full = dot(left, w[0, :, cols]) + b[0, :, cols]
+            for j in range(width // LANES):
+                at = slice(j * LANES, (j + 1) * LANES)
+                outs[shift][0, :, at] = turn(full[:, at], c, s1, s2).astype(BF)
 
     @pl.when(kind == 2)
     def _():
-        out[0] = (dot(normed[...], w_qkv[...]) + b_qkv[...]).astype(BF)
+        for shift in range(n):
+            left, cols = operands(shift, normed)
+            outs[shift][0] = (dot(left, w[0, :, cols]) + b[0, :, cols]).astype(BF)
 
     @pl.when(kind == 3)
     def _():
-        out[0] = back_dot(cot[...], w_out[...]).astype(BF)
-
-
-def project(shift, me, normed, cot, w_qkv, b_qkv, w_out, tables, block_len, width, used):
-    model = normed.shape[1]
-    per = model // width
-
-    def group(me_ref):
-        return jnp.minimum(me_ref[0] ^ shift, used - 1)
-
-    def rows(kind, me_ref):
-        return (group(me_ref) // per, 0)
-
-    def qkv_cols(kind, me_ref):
-        return (0, jnp.minimum(kind, 2) * per + group(me_ref) % per)
-
-    def own(kind, me_ref):
-        return (0, 0)
-
-    flops = 2 * 4 * block_len * model * width
+        for shift in range(n):
+            left, cols = operands(shift, cot)
+            outs[shift][0] = back_dot(left, w[0, cols]).astype(BF)
+
+
+def project(n, me, tokens, cot, gain, bias, w, b, tables, block_len, width, used):
+    rows, model = tokens.shape
+    whole = pl.BlockSpec((rows, model), lambda kind, me_ref: (0, 0))
+    line = pl.BlockSpec((1, model), lambda kind, me_ref: (0, 0))
+    own = pl.BlockSpec((block_len, LANES), lambda kind, me_ref: (0, 0))
     return pl.pallas_call(
-        project_kernel,
+        functools.partial(project_kernel, n, block_len, used),
         grid_spec=pltpu.PrefetchScalarGridSpec(
             num_scalar_prefetch=1,
             grid=(4,),
             in_specs=[
-                pl.BlockSpec((block_len, model), rows),
-                pl.BlockSpec((block_len, model), rows),
-                pl.BlockSpec((model, width), qkv_cols),
-                pl.BlockSpec((1, width), qkv_cols),
-                pl.BlockSpec((width, model), lambda kind, me_ref: (group(me_ref) % per, 0)),
-                pl.BlockSpec((block_len, LANES), own),
-                pl.BlockSpec((block_len, LANES), own),
-                pl.BlockSpec((block_len, LANES), own),
+                whole,
+                whole,
+                line,
+                line,
+                pl.BlockSpec((1, model, model), lambda kind, me_ref: (kind, 0, 0)),
+                pl.BlockSpec((1, 1, model), lambda kind, me_ref: (jnp.minimum(kind, 2), 0, 0)),
+                own,
+                own,
+                own,
             ],
-            out_specs=pl.BlockSpec((1, block_len, width), lambda kind, me_ref: (kind, 0, 0)),
-        ),
-        out_shape=jax.ShapeDtypeStruct((4, block_len, width), BF),
+            out_specs=[pl.BlockSpec((1, block_len, width), lambda kind, me_ref: (kind, 0, 0))] * n,
+            scratch_shapes=[pltpu.VMEM((rows, model), BF)],
+        ),
+        out_shape=[jax.ShapeDtypeStruct((4, block_len, width), BF)] * n,
         compiler_params=pltpu.CompilerParams(vmem_limit_bytes=VMEM),
         cost_estimate=pl.CostEstimate(
-            flops=flops, bytes_accessed=2 * (4 * model * width + 8 * block_len * width), transcendentals=0
+            flops=8 * rows * model * model,
+            bytes_accessed=2 * (4 * model * model + 6 * rows * model),
+            transcendentals=0,
         ),
         name="project",
-    )(me, normed, cot, w_qkv, b_qkv, w_out, *tables)
+    )(me, tokens, cot, gain, bias, w, b.reshape(3, 1, model), *tables)
 
 
 def attend_kernel(n, block, me, *refs):
@@ -281,52 +305,67 @@
     )(me, *pieces, *(jnp.asarray(t).reshape(n, block, LANES) for t in tables))
 
 
-def mlp_kernel(normed, cot, w_up, b_up, w_down, out, grad_in, grad_up, grad_down, grad_b):
+def mlp_kernel(
+    tokens, cot, gain, bias, b_sum, w_up, b_up, w_down,
+    out, grad_in, grad_up, grad_down, grad_b, sums,
+    normed,
+):
     step = pl.program_id(0)
+
+    @pl.when(step == 0)
+    def _():
+        values = tokens[...].astype(F32)
+        hat, _inverse = normalized(values)
+        normed[...] = (hat * gain[...] + bias[...]).astype(BF)
+        out[...] = values + b_sum[...]
+        grad_in[...] = jnp.zeros_like(grad_in)
+
     hidden = dot(normed[...], w_up[...]) + b_up[...]
     share = 0.5 + 0.5 * lax.erf(hidden * (0.5**0.5))
     slope = share + hidden * (jnp.exp(-0.5 * hidden * hidden) * ((2.0 * np.pi) ** -0.5))
     active = (hidden * share).astype(BF)
-    grad_hidden_f = back_dot(cot[...], w_down[...]) * slope
-    grad_hidden = grad_hidden_f.astype(BF)
+    grad_hidden = (back_dot(cot[...], w_down[...]) * slope).astype(BF)
     grad_b[...] = jnp.sum(grad_hidden.astype(F32), axis=0, keepdims=True)
-    mixed = dot(active, w_down[...])
-    back = back_dot(grad_hidden, w_up[...])
-
-    @pl.when(step == 0)
-    def _():
-        out[...] = mixed
-        grad_in[...] = back
-
-    @pl.when(step > 0)
-    def _():
-        out[...] = out[...] + mixed
-        grad_in[...] = grad_in[...] + back
-
+    out[...] = out[...] + dot(active, w_down[...])
+    grad_in[...] = grad_in[...] + back_dot(grad_hidden, w_up[...])
     grad_down[...] = outer_sum(active, cot[...]).astype(BF)
     grad_up[...] = outer_sum(normed[...], grad_hidden).astype(BF)
 
-
-def mlp(normed, cot, w_up, b_up, w_down):
-    rows, model = normed.shape
+    @pl.when(step == pl.num_programs(0) - 1)
+    def _():
+        hat, inverse = normalized(tokens[...].astype(F32))
+        upstream = cot[...].astype(F32)
+        back, grad_gain, grad_bias = norm_back(hat, inverse, gain[...], grad_in[...])
+        grad_in[...] = upstream + back
+        sums[0:1] = grad_gain
+        sums[1:2] = grad_bias
+        sums[2:3] = jnp.sum(upstream, axis=0, keepdims=True)
+        sums[3:8] = jnp.zeros((5, sums.shape[1]), F32)
+
+
+def mlp(tokens, cot, gain, bias, b_sum, w_up, b_up, w_down):
+    rows, model = tokens.shape
     hidden = w_up.shape[1]
     chunk = 384
     whole = pl.BlockSpec((rows, model), lambda j: (0, 0))
+    flat_line = pl.BlockSpec((1, model), lambda j: (0, 0))
     tall = pl.BlockSpec((model, chunk), lambda j: (0, j))
     flat = pl.BlockSpec((chunk, model), lambda j: (j, 0))
     line = pl.BlockSpec((1, chunk), lambda j: (0, j))
     return pl.pallas_call(
         mlp_kernel,
         grid=(hidden // chunk,),
-        in_specs=[whole, whole, tall, line, flat],
-        out_specs=[whole, whole, tall, flat, line],
+        in_specs=[whole, whole, flat_line, flat_line, flat_line, tall, line, flat],
+        out_specs=[whole, whole, tall, flat, line, pl.BlockSpec((8, model), lambda j: (0, 0))],
         out_shape=[
             jax.ShapeDtypeStruct((rows, model), F32),
             jax.ShapeDtypeStruct((rows, model), F32),
             jax.ShapeDtypeStruct((model, hidden), BF),
             jax.ShapeDtypeStruct((hidden, model), BF),
             jax.ShapeDtypeStruct((1, hidden), F32),
+            jax.ShapeDtypeStruct((8, model), F32),
         ],
+        scratch_shapes=[pltpu.VMEM((rows, model), BF)],
         compiler_params=pltpu.CompilerParams(vmem_limit_bytes=VMEM),
         cost_estimate=pl.CostEstimate(
             flops=12 * rows * model * hidden,
@@ -334,11 +373,198 @@
             transcendentals=2 * rows * hidden,
         ),
         name="mlp",
-    )(normed, cot, w_up, b_up, w_down)
+    )(tokens, cot, gain, bias, b_sum, w_up, b_up, w_down)
+
+
+def finish_kernel(n, block_len, used, shards, at, *refs):
+    answers = refs[:n]
+    (tokens, cot, gain, bias, base, grad_base, w, out, grad_out, own, other, sums, normed, grad_in, held, grads) = refs[n:]
+    kind = pl.program_id(0)
+    width = answers[0].shape[-1]
+    per = w.shape[-1] // width
+    own_rows = own.shape[-2]
+
+    for shift in range(n):
+        group = jnp.minimum(at[0] ^ shift, used - 1)
+        rows = pl.multiple_of((group // per) * block_len, block_len)
+        cols = pl.multiple_of((group % per) * width, LANES)
+        if used == n:
+            held[pl.ds(rows, block_len), pl.ds(cols, width)] = answers[shift][0]
+        else:
+            @pl.when((at[0] ^ shift) < used)
+            def _(rows=rows, cols=cols, shift=shift):
+                held[pl.ds(rows, block_len), pl.ds(cols, width)] = answers[shift][0]
+
+    @pl.when(kind == 0)
+    def _():
+        hat, _inverse = normalized(tokens[...].astype(F32))
+        normed[...] = (hat * gain[...] + bias[...]).astype(BF)
+        out[...] = (base[...] + dot(held[...], w[0])).astype(BF)
+        grad_in[...] = jnp.zeros_like(grad_in)
+        sums[...] = jnp.zeros_like(sums)
+        grads[...] = outer_sum(held[...], cot[...]).astype(BF).reshape(grads.shape)
+
+    @pl.when(kind > 0)
+    def _():
+        grads[...] = outer_sum(normed[...], held[...]).astype(BF).reshape(grads.shape)
+        grad_in[...] = grad_in[...] + back_dot(held[...], w[0])
+        sums[pl.ds(kind, 1)] = jnp.sum(held[...].astype(F32), axis=0, keepdims=True)
+
+    for z in range(shards // 2):
+        own[0, z] = grads[z, at[1]]
+        other[0, z] = grads[z, at[1] ^ 1]
+
+    @pl.when(kind == 3)
+    def _():
+        hat, inverse = normalized(tokens[...].astype(F32))
+        back, grad_gain, grad_bias = norm_back(hat, inverse, gain[...], grad_in[...])
+        grad_out[...] = (grad_base[...] + back).astype(BF)
+        sums[4:5] = grad_gain
+        sums[5:6] = grad_bias
+
+
+def finish(n, me, core, answers, tokens, cot, gain, bias, base, grad_base, w, shards, used):
+    rows, model = tokens.shape
+    block_len, width = answers[0].shape[1:]
+    whole = pl.BlockSpec((rows, model), lambda kind, at: (0, 0))
+    line = pl.BlockSpec((1, model), lambda kind, at: (0, 0))
+    own_rows = model // shards
+
+    def unit(kind, at):
+        return (lax.rem(kind + 3, 4), 0, 0)
+
+    half = pl.BlockSpec(
+        (1, shards // 2, own_rows, model), lambda kind, at: (lax.rem(kind + 3, 4), 0, 0, 0)
+    )
+    return pl.pallas_call(
+        functools.partial(finish_kernel, n, block_len, used, shards),
+        grid_spec=pltpu.PrefetchScalarGridSpec(
+            num_scalar_prefetch=1,
+            grid=(4,),
+            in_specs=[pl.BlockSpec((1, block_len, width), lambda kind, at: (kind, 0, 0))] * n
+            + [whole, whole, line, line, whole, whole, pl.BlockSpec((1, model, model), unit)],
+            out_specs=[
+                whole, whole, half, half, pl.BlockSpec((8, model), lambda kind, at: (0, 0)),
+            ],
+            scratch_shapes=[
+                pltpu.VMEM((rows, model), BF),
+                pltpu.VMEM((rows, model), F32),
+                pltpu.VMEM((rows, model), BF),
+                pltpu.VMEM((shards // 2, 2, own_rows, model), BF),
+            ],
+        ),
+        out_shape=[
+            jax.ShapeDtypeStruct((rows, model), BF),
+            jax.ShapeDtypeStruct((rows, model), BF),
+            jax.ShapeDtypeStruct((4, shards // 2, own_rows, model), BF),
+            jax.ShapeDtypeStruct((4, shards // 2, own_rows, model), BF),
+            jax.ShapeDtypeStruct((8, model), F32),
+        ],
+        compiler_params=pltpu.CompilerParams(vmem_limit_bytes=VMEM),
+        cost_estimate=pl.CostEstimate(
+            flops=16 * rows * model * model, bytes_accessed=40 * rows * model, transcendentals=0
+        ),
+        name="finish",
+    )(jnp.stack([me, core]).astype(jnp.int32), *answers, tokens, cot, gain, bias, base, grad_base, w)
 
 
 def swap(value, shift, n):
     return lax.ppermute(value, "ctx", [(i, i ^ shift) for i in range(n)])
+
+
+def swap_shard(value, shift, m):
+    return lax.ppermute(value, "fsdp", [(i, i ^ shift) for i in range(m)])
+
+
+def assemble_kernel(where, counted, shard_first, at, *refs):
+    ins, out = refs[:counted], refs[counted]
+    for piece, index, place in where:
+        unit, shard = place(at)
+        if shard_first:
+            out[shard, unit] = ins[piece][index]
+        else:
+            out[unit, shard] = ins[piece][index]
+
+
+def gather_units(units, n, m, shard_first=False):
+    q, f = lax.axis_index("ctx"), lax.axis_index("fsdp")
+    steps = list(range(2, m, 2))
+    mine = lax.dynamic_index_in_dim(units, q, 0, keepdims=False)
+    other = swap_shard(units, 1, m)
+    along = jnp.stack([swap_shard(mine, step, m) for step in steps])
+    columns = [along] + [swap(along, shift, n) for shift in range(1, n)]
+    crossed = [swap_shard(held, 1, m) for held in columns]
+    pieces = [units, other] + columns + crossed
+    where = []
+    for unit in range(n):
+        where.append((0, unit, lambda at, unit=unit: (unit, at[1])))
+        where.append((1, unit, lambda at, unit=unit: (unit, at[1] ^ 1)))
+    for core in range(2):
+        for shift in range(n):
+            for index, step in enumerate(steps):
+                where.append(
+                    (
+                        2 + core * n + shift,
+                        index,
+                        lambda at, shift=shift, step=step, core=core: (at[0] ^ shift, at[1] ^ step ^ core),
+                    )
+                )
+    full = ((m, n) if shard_first else (n, m)) + units.shape[1:]
+    return pl.pallas_call(
+        functools.partial(assemble_kernel, where, len(pieces), shard_first),
+        grid_spec=pltpu.PrefetchScalarGridSpec(
+            num_scalar_prefetch=1,
+            grid=(1,),
+            in_specs=[pl.BlockSpec(p.shape, lambda i, at, r=p.ndim: (0,) * r) for p in pieces],
+            out_specs=pl.BlockSpec(full, lambda i, at: (0, 0, 0, 0)),
+        ),
+        out_shape=jax.ShapeDtypeStruct(full, units.dtype),
+        compiler_params=pltpu.CompilerParams(vmem_limit_bytes=VMEM),
+        cost_estimate=pl.CostEstimate(
+            flops=0, bytes_accessed=4 * n * m * mine.size, transcendentals=0
+        ),
+        name="assemble",
+    )(jnp.stack([q, f]).astype(jnp.int32), *pieces)
+
+
+def add_up(*pieces):
+    return sum(p.astype(F32) for p in pieces).astype(BF)
+
+
+def sum_units(own, other, n, m):
+    q, z = lax.axis_index("ctx"), lax.axis_index("fsdp") // 2
+
+    def pick(value, at, axis):
+        return lax.dynamic_index_in_dim(value, at, axis, keepdims=False)
+
+    chip = add_up(own, swap_shard(other, 1, m))
+    unit = add_up(pick(chip, q, 0), *[swap(pick(chip, q ^ s, 0), s, n) for s in range(1, n)])
+    own = add_up(
+        pick(unit, z, 0), *[swap_shard(pick(unit, z ^ s, 0), 2 * s, m) for s in range(1, m // 2)]
+    )
+    gathered = jnp.stack([own] + [swap(own, s, n) for s in range(1, n)])
+    return jnp.stack([pick(gathered, q ^ at, 0) for at in range(n)])
+
+
+def sum_lines(lines, n, m):
+    step = 1
+    while step < m:
+        lines = lines + swap_shard(lines, step, m)
+        step *= 2
+    step = 1
+    while step < n:
+        lines = lines + swap(lines, step, n)
+        step *= 2
+    return lines
+
+
+def gather_lines(line, m):
+    f = lax.axis_index("fsdp")
+    step = 1
+    while step < m:
+        line = jnp.concatenate([line, swap_shard(line, step, m)], axis=0)
+        step *= 2
+    return jnp.take(line, f ^ jnp.arange(m), axis=0)
 
 
 def sum_over_ctx(shard, n):
@@ -386,126 +612,95 @@
     used = seq_count * model // width
     per = model // width
 
+    parts = n // 4
+    own_rows = out_weight.shape[0]
+
     vectors = (
         norm1_gain, norm1_bias, norm2_gain, norm2_bias, qkv_bias, out_bias, up_bias, down_bias,
     )
     sizes = [v.shape[0] for v in vectors]
     packed = jnp.concatenate(vectors)
-    lines = 16
-    packed = jnp.pad(packed, (0, lines * model - packed.shape[0])).reshape(lines, model)
-    own_rows = out_weight.shape[0]
-    out_every = lax.all_gather(
-        jnp.concatenate([out_weight, packed], axis=0), "fsdp", axis=0, tiled=False
-    )
-    w_qkv = lax.all_gather(qkv_weight, "fsdp", axis=0, tiled=True)
-    w_up = lax.all_gather(up_weight, "fsdp", axis=0, tiled=True)
-    w_down = lax.all_gather(down_weight, "fsdp", axis=0, tiled=True)
-    w_out = out_every[:, :own_rows].reshape(model, model)
-    flat = out_every[:, own_rows:].reshape(shards, lines * model)
+    lines = -(-packed.shape[0] // LANES)
+    packed = jnp.pad(packed, (0, lines * LANES - packed.shape[0])).reshape(lines, LANES)
+    flat = gather_lines(packed.reshape(1, lines * LANES), shards)
     whole, start = [], 0
     for size in sizes:
-        whole.append(flat[:, start : start + size].reshape(shards * size).astype(F32))
+        whole.append(flat[:, start : start + size].astype(F32).reshape(1, shards * size))
         start += size
     gain_one, bias_one, gain_two, bias_two, b_qkv, b_out, b_up, b_down = whole
 
-    inputs_low = tokens.transpose(1, 0, 2).reshape(rows, model)
-    inputs = inputs_low.astype(F32)
+    w_up = lax.all_gather(up_weight, "fsdp", axis=0, tiled=True)
+    units = jnp.concatenate(
+        [qkv_weight[None, :, t * model : (t + 1) * model] for t in range(3)] + [out_weight[None]]
+    )
+    w_units = gather_units(units.reshape(n, own_rows // parts, model), n, shards)
+    w_units = (
+        w_units.reshape(4, parts, shards, own_rows // parts, model)
+        .transpose(0, 2, 1, 3, 4)
+        .reshape(4, model, model)
+    )
+    w_out = w_units[3]
+    down_units, _ = lax.optimization_barrier(
+        (down_weight.reshape(n, down_weight.shape[0] // n, model), w_units)
+    )
+    w_down = gather_units(down_units, n, shards, True).reshape(hidden, model)
+
+    inputs = tokens.transpose(1, 0, 2).reshape(rows, model)
     cot = cotangent.transpose(1, 0, 2).reshape(rows, model)
-    cot_f = cot.astype(F32)
-    normed_one = layer_norm(inputs, gain_one, bias_one).astype(BF)
-    normed_two = layer_norm(inputs, gain_two, bias_two).astype(BF)
 
     tables = rotary_tables(n * block_len)
     own_tables = tuple(
         lax.dynamic_slice_in_dim(jnp.asarray(t), me * block_len, block_len, 0) for t in tables
     )
 
-    def made(shift):
-        return project(
-            shift, me_arr, normed_one, cot, w_qkv, b_qkv.reshape(1, -1), w_out, own_tables,
-            block_len, width, used,
+    sent = project(
+        n, me_arr, inputs, cot, gain_one, bias_one, w_units, b_qkv, own_tables, block_len, width, used
+    )
+    pieces = [sent[0]] + [swap(sent[shift], shift, n) for shift in range(1, n)]
+    answers = attend(n, me_arr, pieces, tables)
+    mlp_inputs, *answers = lax.optimization_barrier((inputs, *answers))
+    answers = [answers[0]] + [swap(answers[shift], shift, n) for shift in range(1, n)]
+
+    base, grad_base, grad_up, grad_down, grad_up_b, sums_two = mlp(
+        mlp_inputs, cot, gain_two, bias_two, b_out + b_down, w_up, b_up, w_down
+    )
+    core = lax.axis_index("fsdp") % 2
+    layer_out, tokens_grad, own, other, sums_one = finish(
+        n, me, core, answers, inputs, cot, gain_one, bias_one, base, grad_base, w_units, shards, used
+    )
+
+    def placed(value):
+        return value.reshape(seq_count, block_len, model).transpose(1, 0, 2)
+
+    def cut(value):
+        return (
+            value.reshape(4, shards // 2, parts, own_rows // parts, model)
+            .transpose(0, 2, 1, 3, 4)
+            .reshape(n, shards // 2, own_rows // parts, model)
         )
-
-    pieces = [None] * n
-    for shift in list(range(1, n)) + [0]:
-        pieces[shift] = made(shift) if shift == 0 else swap(made(shift), shift, n)
-    answers = attend(n, me_arr, pieces, tables)
-    answers = jnp.stack(
-        [answers[0]] + [swap(answers[shift], shift, n) for shift in range(1, n)]
-    )
-    by_group = jnp.stack(
-        [lax.dynamic_index_in_dim(answers, me ^ at, 0, keepdims=False) for at in range(used)]
-    )
-    by_kind = (
-        by_group.reshape(seq_count, per, 4, block_len, width)
-        .transpose(2, 0, 3, 1, 4)
-        .reshape(4, rows, model)
-    )
-    mixed_heads = by_kind[0]
-
-    mlp_out, grad_two, grad_up, grad_down, grad_up_b = mlp(
-        normed_two, cot, w_up, b_up.reshape(1, -1), w_down
-    )
-    attn_branch = jnp.dot(mixed_heads, w_out, preferred_element_type=F32) + b_out
-    layer_out = (
-        (inputs + attn_branch + mlp_out + b_down)
-        .astype(BF)
-        .reshape(seq_count, block_len, model)
-        .transpose(1, 0, 2)
-    )
-    column_sums = jnp.sum(cot_f, axis=0)
-    grad_out = outer_sum(mixed_heads, cot)
-    grad_kinds = [outer_sum(normed_one, by_kind[t]) for t in (1, 2, 3)]
-    grad_qkv_b = jnp.concatenate([jnp.sum(by_kind[t].astype(F32), axis=0) for t in (1, 2, 3)])
-    grad_one = sum(
-        back_dot(by_kind[t], w_qkv[:, (t - 1) * model : t * model]) for t in (1, 2, 3)
-    )
-    _, norm_back_one = jax.vjp(layer_norm, inputs, gain_one, bias_one)
-    grad_in_one, grad_gain_one, grad_bias_one = norm_back_one(grad_one)
-    _, norm_back_two = jax.vjp(layer_norm, inputs, gain_two, bias_two)
-    grad_in_two, grad_gain_two, grad_bias_two = norm_back_two(grad_two)
-    tokens_grad = (
-        (cot_f + grad_in_one + grad_in_two)
-        .astype(BF)
-        .reshape(seq_count, block_len, model)
-        .transpose(1, 0, 2)
-    )
-
-    grad_vectors = (
-        grad_gain_one, grad_bias_one, grad_gain_two, grad_bias_two, grad_qkv_b, column_sums,
-        grad_up_b.reshape(-1),
-    )
-    grad_sizes = [v.shape[0] // shards for v in grad_vectors]
-    grad_lines = 32
-    packed_grads = jnp.concatenate([v.reshape(shards, -1) for v in grad_vectors], axis=1)
-    packed_grads = jnp.pad(
-        packed_grads, ((0, 0), (0, grad_lines * model - packed_grads.shape[1]))
-    ).reshape(shards, grad_lines, model)
-    last = jnp.concatenate(
-        [g.astype(BF).reshape(shards, own_rows, model) for g in grad_kinds + [grad_out]]
-        + [packed_grads.astype(BF)],
-        axis=1,
-    ).reshape(-1, model)
 
     def shard_sum(value):
         return lax.psum_scatter(value, "fsdp", scatter_dimension=0, tiled=True)
 
+    part_units = sum_units(cut(own), cut(other), n, shards).reshape(4, own_rows, model).astype(F32)
+    part_qkv = jnp.concatenate([part_units[t] for t in range(3)], axis=1)
     part_down = sum_over_ctx(shard_sum(grad_down), n).astype(F32)
     part_up = sum_over_ctx(shard_sum(grad_up), n).astype(F32)
-    part_last = sum_over_ctx(shard_sum(last), n).astype(F32)
-    part_qkv = jnp.concatenate(
-        [part_last[t * own_rows : (t + 1) * own_rows] for t in range(3)], axis=1
-    )
-    part_out = part_last[3 * own_rows : 4 * own_rows]
-    line_sums = part_last[4 * own_rows :].reshape(-1)
-    found, start = [], 0
-    for size in grad_sizes:
-        found.append(line_sums[start : start + size])
-        start += size
-    gain1, bias1, gain2, bias2, qkv_b, columns, up_b = found
+
+    line_sums = sum_lines(
+        jnp.concatenate([sums_one, sums_two, grad_up_b.reshape(-1, model)], axis=0), n, shards
+    )
+    f = lax.axis_index("fsdp")
+
+    def shard_of(first, count):
+        size = count * model // shards
+        return lax.dynamic_slice_in_dim(line_sums[first : first + count].reshape(-1), f * size, size, 0)
+
+    columns = shard_of(10, 1)
     return (
-        layer_out, tokens_grad, gain1, bias1, gain2, bias2, part_qkv, qkv_b, part_out, columns,
-        part_up, up_b, part_down, columns,
+        placed(layer_out), placed(tokens_grad), shard_of(4, 1), shard_of(5, 1), shard_of(8, 1),
+        shard_of(9, 1), part_qkv, shard_of(1, 3), part_units[3], columns, part_up,
+        shard_of(16, hidden // model), part_down, columns,
     )
 
 

time: 415 us -> 379 us (0.913); the launches traced: 409 us -> 379 us
  waiting for transfers between devices: 224 us -> 153 us
  starting transfers between devices: 28.7 us -> 83.5 us
  Pallas kernels: 70.2 us -> 81.5 us
  matrix products: 8.51 us -> 0 us
  other arithmetic: 23.4 us -> 14.9 us
  local copies, waits for them, and re-layouts: 38.9 us -> 31 us
    all_gather x3 -> x0, waiting for transfers between devices: 78.9 us -> none  [the longest x1 49 us: body(): w_down = lax.all_gather(down_weight, 'fsdp', axis=0, tiled=True)]
    all_gather x1, waiting for transfers between devices: 52.2 us -> 0.01 us  [body(): w_up = lax.all_gather(up_weight, 'fsdp', axis=0, tiled=True)]
    ppermute x0 -> x26, waiting for transfers between devices: none -> 51.8 us  [swap_shard(): return lax.ppermute(value, 'fsdp', [(i, i ^ shift) for i in range(m)])]
    ppermute x0 -> x26, starting transfers between devices: none -> 46.6 us  [swap_shard(): return lax.ppermute(value, 'fsdp', [(i, i ^ shift) for i in range(m)])]
    ppermute x24 -> x32, waiting for transfers between devices: 69.4 us -> 100 us  [swap(): return lax.ppermute(value, 'ctx', [(i, i ^ shift) for i in range(n)])]
    reduce_scatter x3 -> x2, waiting for transfers between devices: 21.5 us -> 0.01 us  [shard_sum(): return lax.psum_scatter(value, 'fsdp', scatter_dimension=0, tiled=True)]
    pallas_call x4, Pallas kernels: 19.6 us -> 33.3 us  [the longest x1 14 us: finish(): pl.pallas_call(functools.partial(finish_kernel, n, block_len, used, shard...]
    ppermute x24 -> x32, starting transfers between devices: 27.9 us -> 36.8 us  [swap(): return lax.ppermute(value, 'ctx', [(i, i ^ shift) for i in range(n)])]
  transfers between devices with their start and end apart: 31 -> 61, of which waited for: 19 -> 24; matrix products, arithmetic and copies ran while one was open for 12% -> 10% of each run, Pallas kernels for 17% -> 14%
where the time goes in v2:
time: 379 us
  waiting for transfers between devices  153 us (40%)
  starting transfers between devices  83.5 us (22%)
  Pallas kernels  81.5 us (22%)
  local copies, waits for them, and re-layouts  31 us (8%)
  other arithmetic  14.9 us (4%)
  between operations  14.4 us (4%)
    ppermute x32, waiting for transfers between devices, swap(): return lax.ppermute(value, 'ctx', [(i, i ^ shift) for i in range(n)])  100 us
    ppermute x26, waiting for transfers between devices, swap_shard(): return lax.ppermute(value, 'fsdp', [(i, i ^ shift) for i in range(m)])  51.8 us
    ppermute x26, starting transfers between devices, swap_shard(): return lax.ppermute(value, 'fsdp', [(i, i ^ shift) for i in range(m)])  46.6 us
    ppermute x32, starting transfers between devices, swap(): return lax.ppermute(value, 'ctx', [(i, i ^ shift) for i in range(n)])  36.8 us
    pallas_call x1, Pallas kernels, mlp(): pl.pallas_call(mlp_kernel, grid=(hidden // chunk,), in_specs=[whole, whol...  26.7 us
    pallas_call x1, Pallas kernels, attend(): pl.pallas_call(functools.partial(attend_kernel, n, block), grid_spec=pltp...  21.4 us
    pallas_call x1, Pallas kernels, finish(): pl.pallas_call(functools.partial(finish_kernel, n, block_len, used, shard...  14 us
    pallas_call x2, Pallas kernels, gather_units(): pl.pallas_call(functools.partial(assemble_kernel, where, len(pieces), sha...  10.9 us
  transfers between devices with their start and end apart: 61, of which 24 were waited for; matrix products, arithmetic and copies ran while one was open for 10% of the time, Pallas kernels for 14%

profile of v2, /device:TPU:0, one launch (start us, length us, event | category | flops | bytes accessed | tf_op | source)
XLA Modules:
  0.0 378.6 jit_solution(12732526477462865941)
XLA Ops:
  8.1 1.1 slice_bitcast_fusion.6
  10.3 3.1 collective-permute-start.4
  13.4 2.6 collective-permute-start.5
  16.7 1.6 constant_dynamic-slice_fusion.19.c_ref
  18.3 1.7 constant_dynamic-slice_fusion.17
  21.0 11.0 %collective-permute-done.5 = bf16[96,768]{1,0:T(8,128)(2,1)S(1)} collective-permute-done((bf16[96,768]{1,0:T(8,128)(2,1)S(1)}, bf16[96,768]{1,0:T(8,128)(2,1)S(1)}, u32[]{:S(2)}, u32[]{:S(2)}) %collective-permute-start.5) | collective-permute-done | bytes 147488 | tf_op jit(solution)/shard_map/ppermute | solution.py:476
  33.6 1.6 collective-permute-start.7
  35.2 1.5 collective-permute-start.8
  37.2 15.7 %collective-permute-start.2 = (bf16[4,1280]{1,0:T(4,128)(2,1)S(1)}, bf16[4,1280]{1,0:T(4,128)(2,1)S(1)}, u32[]{:S(2)}, u32[]{:S(2)}) collective-permute-start(bf16[4,1280]{1,0:T(4,128)(2,1)S(1)} %pad_maximum_fusion.10), channel_id=1, source_target_pairs={{0,4},{1,5},{2,6},{3,7},{4,0},{5,1},{6,2},{7,3},{8,12},{9,13},{10,... | collective-permute-start | bytes 30728 | tf_op jit(solution)/shard_map/ppermute | solution.py:476
  60.1 5.5 %assemble.2 = bf16[4,8,96,768]{3,2,1,0:T(8,128)(2,1)} custom-call(s32[2]{0:T(128)} %pad_add_fusion.1.at, bf16[4,96,768]{2,1,0:T(8,128)(2,1)} %copy-done, bf16[4,96,768]{2,1,0:T(8,128)(2,1)} %copy-done.8, bf16[3,96,768]{2,1,0:T(8,128)(2,1)} %copy-done.3, bf16[3,96,768]{2,1,0:T(8,128)(2,1)} %collective-permute-done.7.refs_3_, ...), custom_call_target="tpu_custom_call" | custom-call | bytes 9437184 | tf_op jit(solution)/shard_map/assemble/pallas_call | solution.py:513
  65.6 4.6 %collective-permute-start.21 = (bf16[96,768]{1,0:T(8,128)(2,1)S(1)}, bf16[96,768]{1,0:T(8,128)(2,1)S(1)}, u32[]{:S(2)}, u32[]{:S(2)}) collective-permute-start(bf16[96,768]{1,0:T(8,128)(2,1)S(1)} %dynamic-slice_bitcast_fusion.12), channel_id=1, source_target_pairs={{0,2},{1,3},{2,0},{3,1},{4,6},{5,7},{6,4},{7,5},{8,10},{9,11},{10,... | collective-permute-start | bytes 442376 | tf_op jit(solution)/shard_map/ppermute | solution.py:476
  70.2 2.3 collective-permute-start.22
  72.5 1.4 collective-permute-start.23
  74.5 2.6 collective-permute-done.21
  77.9 6.1 %collective-permute-done.23 = bf16[96,768]{1,0:T(8,128)(2,1)S(1)} collective-permute-done((bf16[96,768]{1,0:T(8,128)(2,1)S(1)}, bf16[96,768]{1,0:T(8,128)(2,1)S(1)}, u32[]{:S(2)}, u32[]{:S(2)}) %collective-permute-start.23) | collective-permute-done | bytes 147488 | tf_op jit(solution)/shard_map/ppermute | solution.py:476
  84.1 1.1 collective-permute-start.24
  85.2 8.5 %project.1 = (bf16[4,256,384]{2,1,0:T(8,128)(2,1)}, bf16[4,256,384]{2,1,0:T(8,128)(2,1)}, bf16[4,256,384]{2,1,0:T(8,128)(2,1)}, bf16[4,256,384]{2,1,0:T(8,128)(2,1)}) custom-call(s32[1]{0:T(128)} %bitcast.me, bf16[512,768]{1,0:T(8,128)(2,1)} %bitcast.125, bf16[512,768]{1,0:T(8,128)(2,1)} %bitcast.128, f32[1,768]{1,0:T(1,128)} %reshape.189.gain.refs_6_, ...), custom_call_target="tpu_custom_call" | custom-call | flops 2415919104 | bytes 9437184 | tf_op jit(solution)/shard_map/project/pallas_call | solution.py:124
  94.7 1.5 collective-permute-start.15
  98.5 1.1 collective-permute-start.25
  99.6 1.4 collective-permute-start.26
  102.3 46.5 %collective-permute-done.25.refs_4_ = bf16[3,96,768]{2,1,0:T(8,128)(2,1)S(1)} collective-permute-done((bf16[3,96,768]{2,1,0:T(8,128)(2,1)S(1)}, bf16[3,96,768]{2,1,0:T(8,128)(2,1)S(1)}, u32[]{:S(2)}, u32[]{:S(2)}) %collective-permute-start.25) | collective-permute-done | bytes 442400 | tf_op jit(solution)/shard_map/ppermute | solution.py:472
  150.3 21.4 %attend.1 = (bf16[4,256,384]{2,1,0:T(8,128)(2,1)}, bf16[4,256,384]{2,1,0:T(8,128)(2,1)}, bf16[4,256,384]{2,1,0:T(8,128)(2,1)}, bf16[4,256,384]{2,1,0:T(8,128)(2,1)}) custom-call(s32[1]{0:T(128)} %bitcast.me, bf16[4,256,384]{2,1,0:T(8,128)(2,1)} %get-tuple-element.39.refs_0_, bf16[4,256,384]{2,1,0:T(8,128)(2,1)} %copy-done.32, ...), custom_call_target="tpu_custom_call" | custom-call | flops 12079595520 | bytes 6291456 | tf_op jit(solution)/shard_map/attend/pallas_call | solution.py:284
  173.8 5.4 %assemble.3 = bf16[8,4,96,768]{3,2,1,0:T(8,128)(2,1)} custom-call(s32[2]{0:T(128)} %pad_add_fusion.1.at, bf16[4,96,768]{2,1,0:T(8,128)(2,1)} %bitcast.118, bf16[4,96,768]{2,1,0:T(8,128)(2,1)} %copy-done.9, bf16[3,96,768]{2,1,0:T(8,128)(2,1)} %copy-done.2, bf16[3,96,768]{2,1,0:T(8,128)(2,1)} %copy-done.10, bf16[3,96,768]{2,1,0:T(8,128)(2,1)} %copy-done.11, ...), custom_call_target="tpu_custom_call" | custom-call | bytes 9437184 | tf_op jit(solution)/shard_map/assemble/pallas_call | solution.py:513
  179.2 26.7 %mlp.1 = (f32[512,768]{1,0:T(8,128)}, f32[512,768]{1,0:T(8,128)}, bf16[768,3072]{1,0:T(8,128)(2,1)}, bf16[3072,768]{1,0:T(8,128)(2,1)}, f32[1,3072]{1,0:T(1,128)}, /*index=5*/f32[8,768]{1,0:T(8,128)}) custom-call(bf16[512,768]{1,0:T(8,128)(2,1)} %bitcast.126, bf16[512,768]{1,0:T(8,128)(2,1)} %bitcast.129, f32[1,768]{1,0:T(1,128)} %reshape.194.gain, ...), custom_call_target="tpu_custom_call" | custom-call | flops 14495514624 | bytes 23592960 | tf_op jit(solution)/shard_map/mlp/pallas_call | solution.py:355
  207.1 1.4 collective-permute-start.17
  209.3 1.4 collective-permute-start.19
  211.2 16.3 %collective-permute-done.17.refs_1_ = bf16[4,256,384]{2,1,0:T(8,128)(2,1)S(1)} collective-permute-done((bf16[4,256,384]{2,1,0:T(8,128)(2,1)S(1)}, bf16[4,256,384]{2,1,0:T(8,128)(2,1)S(1)}, u32[]{:S(2)}, u32[]{:S(2)}) %collective-permute-start.17) | collective-permute-done | bytes 786464 | tf_op jit(solution)/shard_map/ppermute | solution.py:472
  227.5 17.3 %collective-permute-done.18.refs_2_ = bf16[4,256,384]{2,1,0:T(8,128)(2,1)} collective-permute-done((bf16[4,256,384]{2,1,0:T(8,128)(2,1)S(1)}, bf16[4,256,384]{2,1,0:T(8,128)(2,1)}, u32[]{:S(2)}, u32[]{:S(2)}) %collective-permute-start.18) | collective-permute-done | bytes 786464 | tf_op jit(solution)/shard_map/ppermute | solution.py:472
  244.9 14.0 %finish.1 = (bf16[512,768]{1,0:T(8,128)(2,1)}, bf16[512,768]{1,0:T(8,128)(2,1)}, bf16[4,4,96,768]{3,2,1,0:T(8,128)(2,1)}, bf16[4,4,96,768]{3,2,1,0:T(8,128)(2,1)}, f32[8,768]{1,0:T(8,128)}) custom-call(s32[2]{0:T(128)} %pad_add_fusion.at, bf16[4,256,384]{2,1,0:T(8,128)(2,1)} %get-tuple-element.47.refs_0_, bf16[4,256,384]{2,1,0:T(8,128)(2,1)} %copy-done.33, ...), custom_call_target="tpu_custom_call" | custom-call | flops 4831838208 | bytes 15728640 | tf_op jit(solution)/shard_map/finish/pallas_call | solution.py:439
  261.5 2.2 collective-permute-done.36
  263.7 1.5 copy-done.1
  265.1 3.1 add_convert_fusion
  268.2 1.3 dynamic-slice_bitcast_fusion.2
  270.1 1.4 collective-permute-start.38
  271.4 1.5 collective-permute-start.39
  273.0 2.8 collective-permute-start.32
  275.8 5.0 %collective-permute-done.32 = f32[20,768]{1,0:T(8,128)S(1)} collective-permute-done((f32[20,768]{1,0:T(8,128)S(1)}, f32[20,768]{1,0:T(8,128)S(1)}, u32[]{:S(2)}, u32[]{:S(2)}) %collective-permute-start.32) | collective-permute-done | bytes 61472 | tf_op jit(solution)/shard_map/ppermute | solution.py:476
  280.8 3.3 collective-permute-start.33
  284.1 6.6 %collective-permute-done.33 = f32[20,768]{1,0:T(8,128)S(1)} collective-permute-done((f32[20,768]{1,0:T(8,128)S(1)}, f32[20,768]{1,0:T(8,128)S(1)}, u32[]{:S(2)}, u32[]{:S(2)}) %collective-permute-start.33) | collective-permute-done | bytes 61472 | tf_op jit(solution)/shard_map/ppermute | solution.py:476
  291.5 7.8 %collective-permute-done.34 = f32[20,768]{1,0:T(8,128)S(1)} collective-permute-done((f32[20,768]{1,0:T(8,128)S(1)}, f32[20,768]{1,0:T(8,128)S(1)}, u32[]{:S(2)}, u32[]{:S(2)}) %collective-permute-start.34) | collective-permute-done | bytes 61472 | tf_op jit(solution)/shard_map/ppermute | solution.py:472
  300.1 2.8 copy.38
  302.9 1.7 copy.39
  304.7 1.7 fusion.2
  306.5 3.2 collective-permute-start.40
  309.7 2.0 collective-permute-start.41
  311.7 1.4 collective-permute-start.42
  314.3 7.8 %collective-permute-done.40 = bf16[96,768]{1,0:T(8,128)(2,1)S(1)} collective-permute-done((bf16[96,768]{1,0:T(8,128)(2,1)S(1)}, bf16[96,768]{1,0:T(8,128)(2,1)S(1)}, u32[]{:S(2)}, u32[]{:S(2)}) %collective-permute-start.40) | collective-permute-done | bytes 147488 | tf_op jit(solution)/shard_map/ppermute | solution.py:476
  322.0 1.4 collective-permute-done.41
  323.4 6.9 %collective-permute-done.42 = bf16[96,768]{1,0:T(8,128)(2,1)S(1)} collective-permute-done((bf16[96,768]{1,0:T(8,128)(2,1)S(1)}, bf16[96,768]{1,0:T(8,128)(2,1)S(1)}, u32[]{:S(2)}, u32[]{:S(2)}) %collective-permute-start.42) | collective-permute-done | bytes 147488 | tf_op jit(solution)/shard_map/ppermute | solution.py:476
  330.4 1.5 collective-permute-start.43
  331.9 1.5 collective-permute-start.44
  336.5 3.8 collective-permute-done.44
  342.3 1.1 dynamic-slice_bitcast_fusion.5
  345.2 1.7 collective-permute-start.54
  346.9 1.1 dynamic-slice_bitcast_fusion.8
  350.1 1.4 collective-permute-start.48
  351.6 2.3 collective-permute-done.54
  355.7 1.8 collective-permute-start.56
  358.4 1.9 collective-permute-done.47
  362.2 1.6 collective-permute-start.50
  364.8 1.7 collective-permute-done.57
  366.8 1.1 bitcast_convert_fusion
  368.3 1.9 collective-permute-done.50
  370.4 1.2 bitcast_convert_fusion.1
  (219 shorter events, 47.2 us)
Async XLA Ops:
  7.3 171.9 %all-gather.2.cloned.1.call-start = ((), (), s32[]{:S(2)}) async-start(), calls=%async_computation.2 | async-start | bytes 5308416 | tf_op jit(solution)/shard_map/all_gather | solution.py:632
  8.0 334.3 %reduce-scatter.5.cloned.1.call-start = ((), (), s32[]{:S(2)}) async-start(), calls=%async_computation.4 | async-start | bytes 5308416 | tf_op jit(solution)/shard_map/reduce_scatter | solution.py:683
  10.3 10.7 %collective-permute-start.4 = (bf16[96,768]{1,0:T(8,128)(2,1)S(1)}, bf16[96,768]{1,0:T(8,128)(2,1)S(1)}, u32[]{:S(2)}, u32[]{:S(2)}) collective-permute-start(bf16[96,768]{1,0:T(8,128)(2,1)S(1)} %dynamic-slice_bitcast_fusion.13), channel_id=1, source_target_pairs={{0,2},{1,3},{2,0},{3,1},{4,6},{5,7},{6,4},{7,5},{8,10},{9,11},{10,... | collective-permute-start | bytes 442376 | tf_op jit(solution)/shard_map/ppermute | solution.py:476
  13.4 18.6 %collective-permute-start.5 = (bf16[96,768]{1,0:T(8,128)(2,1)S(1)}, bf16[96,768]{1,0:T(8,128)(2,1)S(1)}, u32[]{:S(2)}, u32[]{:S(2)}) collective-permute-start(bf16[96,768]{1,0:T(8,128)(2,1)S(1)} %dynamic-slice_bitcast_fusion.13), channel_id=1, source_target_pairs={{0,4},{1,5},{2,6},{3,7},{4,0},{5,1},{6,2},{7,3},{8,12},{9,13},{10,... | collective-permute-start | bytes 442376 | tf_op jit(solution)/shard_map/ppermute | solution.py:476
  15.9 16.0 %collective-permute-start.6 = (bf16[96,768]{1,0:T(8,128)(2,1)S(1)}, bf16[96,768]{1,0:T(8,128)(2,1)S(1)}, u32[]{:S(2)}, u32[]{:S(2)}) collective-permute-start(bf16[96,768]{1,0:T(8,128)(2,1)S(1)} %dynamic-slice_bitcast_fusion.13), channel_id=1, source_target_pairs={{0,6},{1,7},{2,4},{3,5},{4,2},{5,3},{6,0},{7,1},{8,14},{9,15},{10,... | collective-permute-start | bytes 442376 | tf_op jit(solution)/shard_map/ppermute | solution.py:476
  15.9 42.6 %collective-permute-start.3 = (bf16[4,96,768]{2,1,0:T(8,128)(2,1)S(1)}, bf16[4,96,768]{2,1,0:T(8,128)(2,1)S(1)}, u32[]{:S(2)}, u32[]{:S(2)}) collective-permute-start(bf16[4,96,768]{2,1,0:T(8,128)(2,1)S(1)} %pad_maximum_fusion.1.refs_0_), channel_id=1, source_target_pairs={{0,1},{1,0},{2,3},{3,2},{4,5},{5,4},{6,7},{7,6},{8,9},{9,8},{10,11... | collective-permute-start | bytes 1769480 | tf_op jit(solution)/shard_map/ppermute | solution.py:476
  16.1 3.9 %collective-permute-start = (bf16[1,1280]{1,0:T(2,128)(2,1)S(1)}, bf16[1,1280]{1,0:T(2,128)(2,1)S(1)}, u32[]{:S(2)}, u32[]{:S(2)}) collective-permute-start(bf16[1,1280]{1,0:T(2,128)(2,1)S(1)} %reshape_reshape.8), channel_id=1, source_target_pairs={{0,1},{1,0},{2,3},{3,2},{4,5},{5,4},{6,7},{7,6},{8,9},{9,8},{10,11... | collective-permute-start | bytes 7688 | tf_op jit(solution)/shard_map/ppermute | solution.py:476
  20.0 17.1 %collective-permute-start.1 = (bf16[2,1280]{1,0:T(2,128)(2,1)S(1)}, bf16[2,1280]{1,0:T(2,128)(2,1)S(1)}, u32[]{:S(2)}, u32[]{:S(2)}) collective-permute-start(bf16[2,1280]{1,0:T(2,128)(2,1)S(1)} %pad_maximum_fusion.11), channel_id=1, source_target_pairs={{0,2},{1,3},{2,0},{3,1},{4,6},{5,7},{6,4},{7,5},{8,10},{9,11},{10,... | collective-permute-start | bytes 15368 | tf_op jit(solution)/shard_map/ppermute | solution.py:476
  33.6 22.5 %collective-permute-start.7 = (bf16[3,96,768]{2,1,0:T(8,128)(2,1)S(1)}, bf16[3,96,768]{2,1,0:T(8,128)(2,1)}, u32[]{:S(2)}, u32[]{:S(2)}) collective-permute-start(bf16[3,96,768]{2,1,0:T(8,128)(2,1)S(1)} %pad_maximum_fusion.7.refs_2_), channel_id=1, source_target_pairs={{0,8},{8,0},{16,24},{24,16},{1,9},{9,1},{17,25},{25,17},{2,10},{10... | collective-permute-start | bytes 1327112 | tf_op jit(solution)/shard_map/ppermute | solution.py:472
  35.2 21.4 %collective-permute-start.8 = (bf16[3,96,768]{2,1,0:T(8,128)(2,1)S(1)}, bf16[3,96,768]{2,1,0:T(8,128)(2,1)}, u32[]{:S(2)}, u32[]{:S(2)}) collective-permute-start(bf16[3,96,768]{2,1,0:T(8,128)(2,1)S(1)} %pad_maximum_fusion.7.refs_2_), channel_id=1, source_target_pairs={{0,16},{8,24},{16,0},{24,8},{1,17},{9,25},{17,1},{25,9},{2,18},{10... | collective-permute-start | bytes 1327112 | tf_op jit(solution)/shard_map/ppermute | solution.py:472
  36.7 20.0 %collective-permute-start.9 = (bf16[3,96,768]{2,1,0:T(8,128)(2,1)S(1)}, bf16[3,96,768]{2,1,0:T(8,128)(2,1)}, u32[]{:S(2)}, u32[]{:S(2)}) collective-permute-start(bf16[3,96,768]{2,1,0:T(8,128)(2,1)S(1)} %pad_maximum_fusion.7.refs_2_), channel_id=1, source_target_pairs={{0,24},{8,16},{16,8},{24,0},{1,25},{9,17},{17,9},{25,1},{2,26},{10... | collective-permute-start | bytes 1327112 | tf_op jit(solution)/shard_map/ppermute | solution.py:472
  37.2 18.2 %collective-permute-start.2 = (bf16[4,1280]{1,0:T(4,128)(2,1)S(1)}, bf16[4,1280]{1,0:T(4,128)(2,1)S(1)}, u32[]{:S(2)}, u32[]{:S(2)}) collective-permute-start(bf16[4,1280]{1,0:T(4,128)(2,1)S(1)} %pad_maximum_fusion.10), channel_id=1, source_target_pairs={{0,4},{1,5},{2,6},{3,7},{4,0},{5,1},{6,2},{7,3},{8,12},{9,13},{10,... | collective-permute-start | bytes 30728 | tf_op jit(solution)/shard_map/ppermute | solution.py:476
  56.0 2.6 collective-permute-start.10
  56.1 2.7 collective-permute-start.11
  56.6 2.9 collective-permute-start.12
  56.7 3.4 collective-permute-start.13
  65.6 11.5 %collective-permute-start.21 = (bf16[96,768]{1,0:T(8,128)(2,1)S(1)}, bf16[96,768]{1,0:T(8,128)(2,1)S(1)}, u32[]{:S(2)}, u32[]{:S(2)}) collective-permute-start(bf16[96,768]{1,0:T(8,128)(2,1)S(1)} %dynamic-slice_bitcast_fusion.12), channel_id=1, source_target_pairs={{0,2},{1,3},{2,0},{3,1},{4,6},{5,7},{6,4},{7,5},{8,10},{9,11},{10,... | collective-permute-start | bytes 442376 | tf_op jit(solution)/shard_map/ppermute | solution.py:476
  70.2 7.8 %collective-permute-start.22 = (bf16[96,768]{1,0:T(8,128)(2,1)S(1)}, bf16[96,768]{1,0:T(8,128)(2,1)S(1)}, u32[]{:S(2)}, u32[]{:S(2)}) collective-permute-start(bf16[96,768]{1,0:T(8,128)(2,1)S(1)} %dynamic-slice_bitcast_fusion.12), channel_id=1, source_target_pairs={{0,4},{1,5},{2,6},{3,7},{4,0},{5,1},{6,2},{7,3},{8,12},{9,13},{10,... | collective-permute-start | bytes 442376 | tf_op jit(solution)/shard_map/ppermute | solution.py:476
  72.5 11.5 %collective-permute-start.23 = (bf16[96,768]{1,0:T(8,128)(2,1)S(1)}, bf16[96,768]{1,0:T(8,128)(2,1)S(1)}, u32[]{:S(2)}, u32[]{:S(2)}) collective-permute-start(bf16[96,768]{1,0:T(8,128)(2,1)S(1)} %dynamic-slice_bitcast_fusion.12), channel_id=1, source_target_pairs={{0,6},{1,7},{2,4},{3,5},{4,2},{5,3},{6,0},{7,1},{8,14},{9,15},{10,... | collective-permute-start | bytes 442376 | tf_op jit(solution)/shard_map/ppermute | solution.py:476
  84.1 64.8 %copy-start.2 = (bf16[3,96,768]{2,1,0:T(8,128)(2,1)}, bf16[3,96,768]{2,1,0:T(8,128)(2,1)S(1)}, u32[]{:S(2)}) copy-start(bf16[3,96,768]{2,1,0:T(8,128)(2,1)S(1)} %pad_maximum_fusion.8.refs_2_) | copy-start | bytes 1327108
  84.1 15.5 %collective-permute-start.24 = (bf16[3,96,768]{2,1,0:T(8,128)(2,1)S(1)}, bf16[3,96,768]{2,1,0:T(8,128)(2,1)S(1)}, u32[]{:S(2)}, u32[]{:S(2)}) collective-permute-start(bf16[3,96,768]{2,1,0:T(8,128)(2,1)S(1)} %pad_maximum_fusion.8.refs_2_), channel_id=1, source_target_pairs={{0,8},{8,0},{16,24},{24,16},{1,9},{9,1},{17,25},{25,17},{2,10},{10... | collective-permute-start | bytes 1327112 | tf_op jit(solution)/shard_map/ppermute | solution.py:472
  93.6 55.8 %collective-permute-start.14 = (bf16[4,256,384]{2,1,0:T(8,128)(2,1)}, bf16[4,256,384]{2,1,0:T(8,128)(2,1)S(1)}, u32[]{:S(2)}, u32[]{:S(2)}) collective-permute-start(bf16[4,256,384]{2,1,0:T(8,128)(2,1)} %get-tuple-element.40), channel_id=1, source_target_pairs={{0,8},{8,0},{16,24},{24,16},{1,9},{9,1},{17,25},{25,17},{2,10},{10... | collective-permute-start | bytes 2359304 | tf_op jit(solution)/shard_map/ppermute | solution.py:472
  94.7 54.8 %collective-permute-start.15 = (bf16[4,256,384]{2,1,0:T(8,128)(2,1)}, bf16[4,256,384]{2,1,0:T(8,128)(2,1)}, u32[]{:S(2)}, u32[]{:S(2)}) collective-permute-start(bf16[4,256,384]{2,1,0:T(8,128)(2,1)} %get-tuple-element.41), channel_id=1, source_target_pairs={{0,16},{8,24},{16,0},{24,8},{1,17},{9,25},{17,1},{25,9},{2,18},{10... | collective-permute-start | bytes 2359304 | tf_op jit(solution)/shard_map/ppermute | solution.py:472
  96.2 53.7 %collective-permute-start.16 = (bf16[4,256,384]{2,1,0:T(8,128)(2,1)}, bf16[4,256,384]{2,1,0:T(8,128)(2,1)}, u32[]{:S(2)}, u32[]{:S(2)}) collective-permute-start(bf16[4,256,384]{2,1,0:T(8,128)(2,1)} %get-tuple-element.42), channel_id=1, source_target_pairs={{0,24},{8,16},{16,8},{24,0},{1,25},{9,17},{17,9},{25,1},{2,26},{10... | collective-permute-start | bytes 2359304 | tf_op jit(solution)/shard_map/ppermute | solution.py:472
  98.5 50.4 %collective-permute-start.25 = (bf16[3,96,768]{2,1,0:T(8,128)(2,1)S(1)}, bf16[3,96,768]{2,1,0:T(8,128)(2,1)S(1)}, u32[]{:S(2)}, u32[]{:S(2)}) collective-permute-start(bf16[3,96,768]{2,1,0:T(8,128)(2,1)S(1)} %pad_maximum_fusion.8.refs_2_), channel_id=1, source_target_pairs={{0,16},{8,24},{16,0},{24,8},{1,17},{9,25},{17,1},{25,9},{2,18},{10... | collective-permute-start | bytes 1327112 | tf_op jit(solution)/shard_map/ppermute | solution.py:472
  99.6 72.1 %copy-start.10 = (bf16[3,96,768]{2,1,0:T(8,128)(2,1)}, bf16[3,96,768]{2,1,0:T(8,128)(2,1)S(1)}, u32[]{:S(2)}) copy-start(bf16[3,96,768]{2,1,0:T(8,128)(2,1)S(1)} %collective-permute-done.24.refs_3_) | copy-start | bytes 1327108
  99.6 49.2 %collective-permute-start.26 = (bf16[3,96,768]{2,1,0:T(8,128)(2,1)S(1)}, bf16[3,96,768]{2,1,0:T(8,128)(2,1)S(1)}, u32[]{:S(2)}, u32[]{:S(2)}) collective-permute-start(bf16[3,96,768]{2,1,0:T(8,128)(2,1)S(1)} %pad_maximum_fusion.8.refs_2_), channel_id=1, source_target_pairs={{0,24},{8,16},{16,8},{24,0},{1,25},{9,17},{17,9},{25,1},{2,26},{10... | collective-permute-start | bytes 1327112 | tf_op jit(solution)/shard_map/ppermute | solution.py:472
  148.8 23.0 %collective-permute-start.20 = (bf16[4,96,768]{2,1,0:T(8,128)(2,1)S(1)}, bf16[4,96,768]{2,1,0:T(8,128)(2,1)S(1)}, u32[]{:S(2)}, u32[]{:S(2)}) collective-permute-start(bf16[4,96,768]{2,1,0:T(8,128)(2,1)S(1)} %bitcast.120), channel_id=1, source_target_pairs={{0,1},{1,0},{2,3},{3,2},{4,5},{5,4},{6,7},{7,6},{8,9},{9,8},{10,11... | collective-permute-start | bytes 1769480 | tf_op jit(solution)/shard_map/ppermute | solution.py:476
  148.9 22.9 %collective-permute-start.27 = (bf16[3,96,768]{2,1,0:T(8,128)(2,1)S(1)}, bf16[3,96,768]{2,1,0:T(8,128)(2,1)S(1)}, u32[]{:S(2)}, u32[]{:S(2)}) collective-permute-start(bf16[3,96,768]{2,1,0:T(8,128)(2,1)S(1)} %pad_maximum_fusion.8.refs_2_), channel_id=1, source_target_pairs={{0,1},{1,0},{2,3},{3,2},{4,5},{5,4},{6,7},{7,6},{8,9},{9,8},{10,11... | collective-permute-start | bytes 1327112 | tf_op jit(solution)/shard_map/ppermute | solution.py:476
  149.4 22.4 %collective-permute-start.28 = (bf16[3,96,768]{2,1,0:T(8,128)(2,1)S(1)}, bf16[3,96,768]{2,1,0:T(8,128)(2,1)S(1)}, u32[]{:S(2)}, u32[]{:S(2)}) collective-permute-start(bf16[3,96,768]{2,1,0:T(8,128)(2,1)S(1)} %collective-permute-done.24.refs_3_), channel_id=1, source_target_pairs={{0,1},{1,0},{2,3},{3,2},{4,5},{5,4},{6,7},{7,6},{8,9},{9,8},{10,11... | collective-permute-start | bytes 1327112 | tf_op jit(solution)/shard_map/ppermute | solution.py:476
  149.5 22.3 %collective-permute-start.29 = (bf16[3,96,768]{2,1,0:T(8,128)(2,1)S(1)}, bf16[3,96,768]{2,1,0:T(8,128)(2,1)S(1)}, u32[]{:S(2)}, u32[]{:S(2)}) collective-permute-start(bf16[3,96,768]{2,1,0:T(8,128)(2,1)S(1)} %collective-permute-done.25.refs_4_), channel_id=1, source_target_pairs={{0,1},{1,0},{2,3},{3,2},{4,5},{5,4},{6,7},{7,6},{8,9},{9,8},{10,11... | collective-permute-start | bytes 1327112 | tf_op jit(solution)/shard_map/ppermute | solution.py:476
  149.9 21.9 %collective-permute-start.30 = (bf16[3,96,768]{2,1,0:T(8,128)(2,1)S(1)}, bf16[3,96,768]{2,1,0:T(8,128)(2,1)S(1)}, u32[]{:S(2)}, u32[]{:S(2)}) collective-permute-start(bf16[3,96,768]{2,1,0:T(8,128)(2,1)S(1)} %collective-permute-done.26.refs_5_), channel_id=1, source_target_pairs={{0,1},{1,0},{2,3},{3,2},{4,5},{5,4},{6,7},{7,6},{8,9},{9,8},{10,11... | collective-permute-start | bytes 1327112 | tf_op jit(solution)/shard_map/ppermute | solution.py:476
  205.9 141.0 %reduce-scatter.3.cloned.1.call-start = ((), (), s32[]{:S(2)}) async-start(), calls=%async_computation.3 | async-start | bytes 5308416 | tf_op jit(solution)/shard_map/reduce_scatter | solution.py:683
  207.1 20.4 %collective-permute-start.17 = (bf16[4,256,384]{2,1,0:T(8,128)(2,1)S(1)}, bf16[4,256,384]{2,1,0:T(8,128)(2,1)S(1)}, u32[]{:S(2)}, u32[]{:S(2)}) collective-permute-start(bf16[4,256,384]{2,1,0:T(8,128)(2,1)S(1)} %copy-done.31), channel_id=1, source_target_pairs={{0,8},{8,0},{16,24},{24,16},{1,9},{9,1},{17,25},{25,17},{2,10},{10... | collective-permute-start | bytes 2359304 | tf_op jit(solution)/shard_map/ppermute | solution.py:472
  208.6 36.3 %collective-permute-start.18 = (bf16[4,256,384]{2,1,0:T(8,128)(2,1)S(1)}, bf16[4,256,384]{2,1,0:T(8,128)(2,1)}, u32[]{:S(2)}, u32[]{:S(2)}) collective-permute-start(bf16[4,256,384]{2,1,0:T(8,128)(2,1)S(1)} %copy-done.30), channel_id=1, source_target_pairs={{0,16},{8,24},{16,0},{24,8},{1,17},{9,25},{17,1},{25,9},{2,18},{10... | collective-permute-start | bytes 2359304 | tf_op jit(solution)/shard_map/ppermute | solution.py:472
  209.3 35.6 %collective-permute-start.19 = (bf16[4,256,384]{2,1,0:T(8,128)(2,1)S(1)}, bf16[4,256,384]{2,1,0:T(8,128)(2,1)}, u32[]{:S(2)}, u32[]{:S(2)}) collective-permute-start(bf16[4,256,384]{2,1,0:T(8,128)(2,1)S(1)} %copy-done.29), channel_id=1, source_target_pairs={{0,24},{8,16},{16,8},{24,0},{1,25},{9,17},{17,9},{25,1},{2,26},{10... | collective-permute-start | bytes 2359304 | tf_op jit(solution)/shard_map/ppermute | solution.py:472
  258.8 4.8 %collective-permute-start.36 = (bf16[4,4,96,768]{3,2,1,0:T(8,128)(2,1)}, bf16[4,4,96,768]{3,2,1,0:T(8,128)(2,1)S(1)}, u32[]{:S(2)}, u32[]{:S(2)}) collective-permute-start(bf16[4,4,96,768]{3,2,1,0:T(8,128)(2,1)} %get-tuple-element.61), channel_id=1, source_target_pairs={{0,1},{1,0},{2,3},{3,2},{4,5},{5,4},{6,7},{7,6},{8,9},{9,8},{10,11... | collective-permute-start | bytes 7077896 | tf_op jit(solution)/shard_map/ppermute | solution.py:476
  260.9 12.1 %collective-permute-start.31 = (f32[20,768]{1,0:T(8,128)S(1)}, f32[20,768]{1,0:T(8,128)S(1)}, u32[]{:S(2)}, u32[]{:S(2)}) collective-permute-start(f32[20,768]{1,0:T(8,128)S(1)} %constant_dynamic-update-slice_fusion), channel_id=1, source_target_pairs={{0,1},{1,0},{2,3},{3,2},{4,5},{5,4},{6,7},{7,6},{8,9},{9,8},{10,11... | collective-permute-start | bytes 184328 | tf_op jit(solution)/shard_map/ppermute | solution.py:476
  269.5 35.3 %collective-permute-start.37 = (bf16[4,96,768]{2,1,0:T(8,128)(2,1)}, bf16[4,96,768]{2,1,0:T(8,128)(2,1)}, u32[]{:S(2)}, u32[]{:S(2)}) collective-permute-start(bf16[4,96,768]{2,1,0:T(8,128)(2,1)} %get-tuple-element.64), channel_id=1, source_target_pairs={{0,8},{8,0},{16,24},{24,16},{1,9},{9,1},{17,25},{25,17},{2,10},{10... | collective-permute-start | bytes 1769480 | tf_op jit(solution)/shard_map/ppermute | solution.py:472
  270.1 34.7 %collective-permute-start.38 = (bf16[4,96,768]{2,1,0:T(8,128)(2,1)}, bf16[4,96,768]{2,1,0:T(8,128)(2,1)}, u32[]{:S(2)}, u32[]{:S(2)}) collective-permute-start(bf16[4,96,768]{2,1,0:T(8,128)(2,1)} %get-tuple-element.66), channel_id=1, source_target_pairs={{0,16},{8,24},{16,0},{24,8},{1,17},{9,25},{17,1},{25,9},{2,18},{10... | collective-permute-start | bytes 1769480 | tf_op jit(solution)/shard_map/ppermute | solution.py:472
  271.4 33.3 %collective-permute-start.39 = (bf16[4,96,768]{2,1,0:T(8,128)(2,1)}, bf16[4,96,768]{2,1,0:T(8,128)(2,1)}, u32[]{:S(2)}, u32[]{:S(2)}) collective-permute-start(bf16[4,96,768]{2,1,0:T(8,128)(2,1)} %get-tuple-element.65), channel_id=1, source_target_pairs={{0,24},{8,16},{16,8},{24,0},{1,25},{9,17},{17,9},{25,1},{2,26},{10... | collective-permute-start | bytes 1769480 | tf_op jit(solution)/shard_map/ppermute | solution.py:472
  273.0 7.8 %collective-permute-start.32 = (f32[20,768]{1,0:T(8,128)S(1)}, f32[20,768]{1,0:T(8,128)S(1)}, u32[]{:S(2)}, u32[]{:S(2)}) collective-permute-start(f32[20,768]{1,0:T(8,128)S(1)} %add.159), channel_id=1, source_target_pairs={{0,2},{1,3},{2,0},{3,1},{4,6},{5,7},{6,4},{7,5},{8,10},{9,11},{10,... | collective-permute-start | bytes 184328 | tf_op jit(solution)/shard_map/ppermute | solution.py:476
  280.8 9.9 %collective-permute-start.33 = (f32[20,768]{1,0:T(8,128)S(1)}, f32[20,768]{1,0:T(8,128)S(1)}, u32[]{:S(2)}, u32[]{:S(2)}) collective-permute-start(f32[20,768]{1,0:T(8,128)S(1)} %add.160), channel_id=1, source_target_pairs={{0,4},{1,5},{2,6},{3,7},{4,0},{5,1},{6,2},{7,3},{8,12},{9,13},{10,... | collective-permute-start | bytes 184328 | tf_op jit(solution)/shard_map/ppermute | solution.py:476
  290.7 8.7 %collective-permute-start.34 = (f32[20,768]{1,0:T(8,128)S(1)}, f32[20,768]{1,0:T(8,128)S(1)}, u32[]{:S(2)}, u32[]{:S(2)}) collective-permute-start(f32[20,768]{1,0:T(8,128)S(1)} %add.161), channel_id=1, source_target_pairs={{0,8},{8,0},{16,24},{24,16},{1,9},{9,1},{17,25},{25,17},{2,10},{10... | collective-permute-start | bytes 184328 | tf_op jit(solution)/shard_map/ppermute | solution.py:472
  299.3 5.3 %collective-permute-start.35 = (f32[20,768]{1,0:T(8,128)S(1)}, f32[20,768]{1,0:T(8,128)S(1)}, u32[]{:S(2)}, u32[]{:S(2)}) collective-permute-start(f32[20,768]{1,0:T(8,128)S(1)} %add.162), channel_id=1, source_target_pairs={{0,16},{8,24},{16,0},{24,8},{1,17},{9,25},{17,1},{25,9},{2,18},{10... | collective-permute-start | bytes 184328 | tf_op jit(solution)/shard_map/ppermute | solution.py:472
  304.7 66.9 %copy-start.34 = (f32[96]{0:T(128)}, f32[96]{0:T(128)S(1)}, u32[]{:S(2)}) copy-start(f32[96]{0:T(128)S(1)} %fusion.17) | copy-start | bytes 1156
  306.5 15.5 %collective-permute-start.40 = (bf16[96,768]{1,0:T(8,128)(2,1)S(1)}, bf16[96,768]{1,0:T(8,128)(2,1)S(1)}, u32[]{:S(2)}, u32[]{:S(2)}) collective-permute-start(bf16[96,768]{1,0:T(8,128)(2,1)S(1)} %get-tuple-element.89), channel_id=1, source_target_pairs={{0,2},{1,3},{2,0},{3,1},{4,6},{5,7},{6,4},{7,5},{8,10},{9,11},{10,... | collective-permute-start | bytes 442376 | tf_op jit(solution)/shard_map/ppermute | solution.py:476
  309.7 13.7 %collective-permute-start.41 = (bf16[96,768]{1,0:T(8,128)(2,1)S(1)}, bf16[96,768]{1,0:T(8,128)(2,1)S(1)}, u32[]{:S(2)}, u32[]{:S(2)}) collective-permute-start(bf16[96,768]{1,0:T(8,128)(2,1)S(1)} %get-tuple-element.91), channel_id=1, source_target_pairs={{0,4},{1,5},{2,6},{3,7},{4,0},{5,1},{6,2},{7,3},{8,12},{9,13},{10,... | collective-permute-start | bytes 442376 | tf_op jit(solution)/shard_map/ppermute | solution.py:476
  311.7 18.6 %collective-permute-start.42 = (bf16[96,768]{1,0:T(8,128)(2,1)S(1)}, bf16[96,768]{1,0:T(8,128)(2,1)S(1)}, u32[]{:S(2)}, u32[]{:S(2)}) collective-permute-start(bf16[96,768]{1,0:T(8,128)(2,1)S(1)} %get-tuple-element.90), channel_id=1, source_target_pairs={{0,6},{1,7},{2,4},{3,5},{4,2},{5,3},{6,0},{7,1},{8,14},{9,15},{10,... | collective-permute-start | bytes 442376 | tf_op jit(solution)/shard_map/ppermute | solution.py:476
  330.4 6.1 %collective-permute-start.43 = (bf16[96,768]{1,0:T(8,128)(2,1)S(1)}, bf16[96,768]{1,0:T(8,128)(2,1)S(1)}, u32[]{:S(2)}, u32[]{:S(2)}) collective-permute-start(bf16[96,768]{1,0:T(8,128)(2,1)S(1)} %fusion.11), channel_id=1, source_target_pairs={{0,8},{8,0},{16,24},{24,16},{1,9},{9,1},{17,25},{25,17},{2,10},{10... | collective-permute-start | bytes 442376 | tf_op jit(solution)/shard_map/ppermute | solution.py:472
  331.9 8.3 %collective-permute-start.44 = (bf16[96,768]{1,0:T(8,128)(2,1)S(1)}, bf16[96,768]{1,0:T(8,128)(2,1)S(1)}, u32[]{:S(2)}, u32[]{:S(2)}) collective-permute-start(bf16[96,768]{1,0:T(8,128)(2,1)S(1)} %fusion.11), channel_id=1, source_target_pairs={{0,16},{8,24},{16,0},{24,8},{1,17},{9,25},{17,1},{25,9},{2,18},{10... | collective-permute-start | bytes 442376 | tf_op jit(solution)/shard_map/ppermute | solution.py:472
  333.4 6.8 %collective-permute-start.45 = (bf16[96,768]{1,0:T(8,128)(2,1)S(1)}, bf16[96,768]{1,0:T(8,128)(2,1)S(1)}, u32[]{:S(2)}, u32[]{:S(2)}) collective-permute-start(bf16[96,768]{1,0:T(8,128)(2,1)S(1)} %fusion.11), channel_id=1, source_target_pairs={{0,24},{8,16},{16,8},{24,0},{1,25},{9,17},{17,9},{25,1},{2,26},{10... | collective-permute-start | bytes 442376 | tf_op jit(solution)/shard_map/ppermute | solution.py:472
  343.4 6.8 %collective-permute-start.52 = (bf16[96,768]{1,0:T(8,128)(2,1)S(1)}, bf16[96,768]{1,0:T(8,128)(2,1)S(1)}, u32[]{:S(2)}, u32[]{:S(2)}) collective-permute-start(bf16[96,768]{1,0:T(8,128)(2,1)S(1)} %get-tuple-element.75), channel_id=1, source_target_pairs={{0,8},{8,0},{16,24},{24,16},{1,9},{9,1},{17,25},{25,17},{2,10},{10... | collective-permute-start | bytes 442376 | tf_op jit(solution)/shard_map/ppermute | solution.py:472
  344.4 7.2 %collective-permute-start.53 = (bf16[96,768]{1,0:T(8,128)(2,1)S(1)}, bf16[96,768]{1,0:T(8,128)(2,1)S(1)}, u32[]{:S(2)}, u32[]{:S(2)}) collective-permute-start(bf16[96,768]{1,0:T(8,128)(2,1)S(1)} %get-tuple-element.77), channel_id=1, source_target_pairs={{0,16},{8,24},{16,0},{24,8},{1,17},{9,25},{17,1},{25,9},{2,18},{10... | collective-permute-start | bytes 442376 | tf_op jit(solution)/shard_map/ppermute | solution.py:472
  345.2 8.6 %collective-permute-start.54 = (bf16[96,768]{1,0:T(8,128)(2,1)S(1)}, bf16[96,768]{1,0:T(8,128)(2,1)S(1)}, u32[]{:S(2)}, u32[]{:S(2)}) collective-permute-start(bf16[96,768]{1,0:T(8,128)(2,1)S(1)} %get-tuple-element.76), channel_id=1, source_target_pairs={{0,24},{8,16},{16,8},{24,0},{1,25},{9,17},{17,9},{25,1},{2,26},{10... | collective-permute-start | bytes 442376 | tf_op jit(solution)/shard_map/ppermute | solution.py:472
  348.0 9.5 %collective-permute-start.46 = (bf16[24,3072]{1,0:T(8,128)(2,1)S(1)}, bf16[24,3072]{1,0:T(8,128)(2,1)S(1)}, u32[]{:S(2)}, u32[]{:S(2)}) collective-permute-start(bf16[24,3072]{1,0:T(8,128)(2,1)S(1)} %get-tuple-element.82), channel_id=1, source_target_pairs={{0,8},{8,0},{16,24},{24,16},{1,9},{9,1},{17,25},{25,17},{2,10},{10... | collective-permute-start | bytes 442376 | tf_op jit(solution)/shard_map/ppermute | solution.py:472
  349.0 11.3 %collective-permute-start.47 = (bf16[24,3072]{1,0:T(8,128)(2,1)S(1)}, bf16[24,3072]{1,0:T(8,128)(2,1)S(1)}, u32[]{:S(2)}, u32[]{:S(2)}) collective-permute-start(bf16[24,3072]{1,0:T(8,128)(2,1)S(1)} %get-tuple-element.84), channel_id=1, source_target_pairs={{0,16},{8,24},{16,0},{24,8},{1,17},{9,25},{17,1},{25,9},{2,18},{10... | collective-permute-start | bytes 442376 | tf_op jit(solution)/shard_map/ppermute | solution.py:472
  350.1 10.1 %collective-permute-start.48 = (bf16[24,3072]{1,0:T(8,128)(2,1)S(1)}, bf16[24,3072]{1,0:T(8,128)(2,1)S(1)}, u32[]{:S(2)}, u32[]{:S(2)}) collective-permute-start(bf16[24,3072]{1,0:T(8,128)(2,1)S(1)} %get-tuple-element.83), channel_id=1, source_target_pairs={{0,24},{8,16},{16,8},{24,0},{1,25},{9,17},{17,9},{25,1},{2,26},{10... | collective-permute-start | bytes 442376 | tf_op jit(solution)/shard_map/ppermute | solution.py:472
  354.8 9.0 %collective-permute-start.55 = (bf16[96,768]{1,0:T(8,128)(2,1)S(1)}, bf16[96,768]{1,0:T(8,128)(2,1)S(1)}, u32[]{:S(2)}, u32[]{:S(2)}) collective-permute-start(bf16[96,768]{1,0:T(8,128)(2,1)S(1)} %fusion.5), channel_id=1, source_target_pairs={{0,8},{8,0},{16,24},{24,16},{1,9},{9,1},{17,25},{25,17},{2,10},{10... | collective-permute-start | bytes 442376 | tf_op jit(solution)/shard_map/ppermute | solution.py:472
  355.7 9.1 %collective-permute-start.56 = (bf16[96,768]{1,0:T(8,128)(2,1)S(1)}, bf16[96,768]{1,0:T(8,128)(2,1)S(1)}, u32[]{:S(2)}, u32[]{:S(2)}) collective-permute-start(bf16[96,768]{1,0:T(8,128)(2,1)S(1)} %fusion.5), channel_id=1, source_target_pairs={{0,16},{8,24},{16,0},{24,8},{1,17},{9,25},{17,1},{25,9},{2,18},{10... | collective-permute-start | bytes 442376 | tf_op jit(solution)/shard_map/ppermute | solution.py:472
  357.5 9.0 %collective-permute-start.57 = (bf16[96,768]{1,0:T(8,128)(2,1)S(1)}, bf16[96,768]{1,0:T(8,128)(2,1)S(1)}, u32[]{:S(2)}, u32[]{:S(2)}) collective-permute-start(bf16[96,768]{1,0:T(8,128)(2,1)S(1)} %fusion.5), channel_id=1, source_target_pairs={{0,24},{8,16},{16,8},{24,0},{1,25},{9,17},{17,9},{25,1},{2,26},{10... | collective-permute-start | bytes 442376 | tf_op jit(solution)/shard_map/ppermute | solution.py:472
  361.3 7.1 %collective-permute-start.49 = (bf16[24,3072]{1,0:T(8,128)(2,1)S(1)}, bf16[24,3072]{1,0:T(8,128)(2,1)S(1)}, u32[]{:S(2)}, u32[]{:S(2)}) collective-permute-start(bf16[24,3072]{1,0:T(8,128)(2,1)S(1)} %fusion.8), channel_id=1, source_target_pairs={{0,8},{8,0},{16,24},{24,16},{1,9},{9,1},{17,25},{25,17},{2,10},{10... | collective-permute-start | bytes 442376 | tf_op jit(solution)/shard_map/ppermute | solution.py:472
  362.2 8.0 %collective-permute-start.50 = (bf16[24,3072]{1,0:T(8,128)(2,1)S(1)}, bf16[24,3072]{1,0:T(8,128)(2,1)S(1)}, u32[]{:S(2)}, u32[]{:S(2)}) collective-permute-start(bf16[24,3072]{1,0:T(8,128)(2,1)S(1)} %fusion.8), channel_id=1, source_target_pairs={{0,16},{8,24},{16,0},{24,8},{1,17},{9,25},{17,1},{25,9},{2,18},{10... | collective-permute-start | bytes 442376 | tf_op jit(solution)/shard_map/ppermute | solution.py:472
  363.8 6.4 %collective-permute-start.51 = (bf16[24,3072]{1,0:T(8,128)(2,1)S(1)}, bf16[24,3072]{1,0:T(8,128)(2,1)S(1)}, u32[]{:S(2)}, u32[]{:S(2)}) collective-permute-start(bf16[24,3072]{1,0:T(8,128)(2,1)S(1)} %fusion.8), channel_id=1, source_target_pairs={{0,24},{8,16},{16,8},{24,0},{1,25},{9,17},{17,9},{25,1},{2,26},{10... | collective-permute-start | bytes 442376 | tf_op jit(solution)/shard_map/ppermute | solution.py:472
  (32 other events, 386.5 us)
Sparse Core Ops, SparseCore 0:
  9.7 59.4 all-gather.1
  206.1 56.7 reduce-scatter.4
  265.2 63.4 reduce-scatter.2

commit v3 on v2

--- a/solution.py
+++ b/solution.py
@@ -120,7 +120,7 @@
     rows, model = tokens.shape
     whole = pl.BlockSpec((rows, model), lambda kind, me_ref: (0, 0))
     line = pl.BlockSpec((1, model), lambda kind, me_ref: (0, 0))
-    own = pl.BlockSpec((block_len, LANES), lambda kind, me_ref: (0, 0))
+    own = pl.BlockSpec((block_len, LANES), lambda kind, me_ref: (me_ref[0], 0))
     return pl.pallas_call(
         functools.partial(project_kernel, n, block_len, used),
         grid_spec=pltpu.PrefetchScalarGridSpec(
@@ -148,7 +148,7 @@
             transcendentals=0,
         ),
         name="project",
-    )(me, tokens, cot, gain, bias, w, b.reshape(3, 1, model), *tables)
+    )(me, tokens, cot, gain, bias, w, b.reshape(3, 1, model), *(jnp.asarray(t) for t in tables))
 
 
 def attend_kernel(n, block, me, *refs):
@@ -299,7 +299,7 @@
         out_shape=[jax.ShapeDtypeStruct((4, block, width), BF)] * n,
         compiler_params=pltpu.CompilerParams(vmem_limit_bytes=VMEM),
         cost_estimate=pl.CostEstimate(
-            flops=12 * work * 4 * HD, bytes_accessed=2 * 8 * length * width, transcendentals=work
+            flops=12 * work * 4 * HD * 10, bytes_accessed=2 * 8 * length * width, transcendentals=work
         ),
         name="attend",
     )(me, *pieces, *(jnp.asarray(t).reshape(n, block, LANES) for t in tables))
@@ -486,14 +486,25 @@
             out[unit, shard] = ins[piece][index]
 
 
-def gather_units(units, n, m, shard_first=False):
-    q, f = lax.axis_index("ctx"), lax.axis_index("fsdp")
+def along_z(units, m):
+    mine = pick(units, lax.axis_index("ctx"))
+    return jnp.stack([swap_shard(mine, step, m) for step in range(2, m, 2)])
+
+
+def gather_lines(lines, m):
+    chips = jnp.stack([lines] + [swap_shard(lines, step, m) for step in range(2, m, 2)])
+    both = jnp.stack([chips, swap_shard(chips, 1, m)], axis=1).reshape((m,) + lines.shape)
+    return in_order(both, lax.axis_index("fsdp"))
+
+
+def between_columns(along, n):
+    return [along] + [swap(along, shift, n) for shift in range(1, n)]
+
+
+def between_cores(units, columns, n, m, shard_first=False):
+    other = swap_shard(units, 1, m)
+    crossed = [swap_shard(held, 1, m) for held in columns]
     steps = list(range(2, m, 2))
-    mine = lax.dynamic_index_in_dim(units, q, 0, keepdims=False)
-    other = swap_shard(units, 1, m)
-    along = jnp.stack([swap_shard(mine, step, m) for step in steps])
-    columns = [along] + [swap(along, shift, n) for shift in range(1, n)]
-    crossed = [swap_shard(held, 1, m) for held in columns]
     pieces = [units, other] + columns + crossed
     where = []
     for unit in range(n):
@@ -510,6 +521,7 @@
                     )
                 )
     full = ((m, n) if shard_first else (n, m)) + units.shape[1:]
+    at = jnp.stack([lax.axis_index("ctx"), lax.axis_index("fsdp")]).astype(jnp.int32)
     return pl.pallas_call(
         functools.partial(assemble_kernel, where, len(pieces), shard_first),
         grid_spec=pltpu.PrefetchScalarGridSpec(
@@ -520,51 +532,47 @@
         ),
         out_shape=jax.ShapeDtypeStruct(full, units.dtype),
         compiler_params=pltpu.CompilerParams(vmem_limit_bytes=VMEM),
-        cost_estimate=pl.CostEstimate(
-            flops=0, bytes_accessed=4 * n * m * mine.size, transcendentals=0
-        ),
+        cost_estimate=pl.CostEstimate(flops=0, bytes_accessed=4 * m * units.size, transcendentals=0),
         name="assemble",
-    )(jnp.stack([q, f]).astype(jnp.int32), *pieces)
+    )(at, *pieces)
 
 
 def add_up(*pieces):
     return sum(p.astype(F32) for p in pieces).astype(BF)
 
 
-def sum_units(own, other, n, m):
+def pick(value, at, axis=0):
+    return lax.dynamic_index_in_dim(value, at, axis, keepdims=False)
+
+
+def sum_units(own, other, lines, shard, n, m):
     q, z = lax.axis_index("ctx"), lax.axis_index("fsdp") // 2
-
-    def pick(value, at, axis):
-        return lax.dynamic_index_in_dim(value, at, axis, keepdims=False)
-
+    steps = range(1, n)
+    shard_parts = shard.reshape((n, shard.shape[0] // n) + shard.shape[1:])
+
+    own, other, shard_parts = lax.optimization_barrier((own, other, shard_parts))
     chip = add_up(own, swap_shard(other, 1, m))
-    unit = add_up(pick(chip, q, 0), *[swap(pick(chip, q ^ s, 0), s, n) for s in range(1, n)])
-    own = add_up(
-        pick(unit, z, 0), *[swap_shard(pick(unit, z ^ s, 0), 2 * s, m) for s in range(1, m // 2)]
-    )
-    gathered = jnp.stack([own] + [swap(own, s, n) for s in range(1, n)])
-    return jnp.stack([pick(gathered, q ^ at, 0) for at in range(n)])
-
-
-def sum_lines(lines, n, m):
-    step = 1
-    while step < m:
-        lines = lines + swap_shard(lines, step, m)
-        step *= 2
-    step = 1
-    while step < n:
-        lines = lines + swap(lines, step, n)
-        step *= 2
-    return lines
-
-
-def gather_lines(line, m):
-    f = lax.axis_index("fsdp")
-    step = 1
-    while step < m:
-        line = jnp.concatenate([line, swap_shard(line, step, m)], axis=0)
-        step *= 2
-    return jnp.take(line, f ^ jnp.arange(m), axis=0)
+    lines = lines + swap_shard(lines, 1, m)
+    shard_sum = add_up(pick(shard_parts, q), *[swap(pick(shard_parts, q ^ s), s, n) for s in steps])
+    unit = add_up(pick(chip, q), *[swap(pick(chip, q ^ s), s, n) for s in steps])
+    lines = sum_in_order([lines] + [swap(lines, s, n) for s in steps], q)
+    unit, shard_sum = lax.optimization_barrier((unit, shard_sum))
+    shard_all = [shard_sum] + [swap(shard_sum, s, n) for s in steps]
+    z_steps = range(1, m // 2)
+    own = add_up(pick(unit, z), *[swap_shard(pick(unit, z ^ s), 2 * s, m) for s in z_steps])
+    lines = sum_in_order([lines] + [swap_shard(lines, 2 * s, m) for s in z_steps], z)
+    own, shard_all = lax.optimization_barrier((own, shard_all))
+    every = in_order([own] + [swap(own, s, n) for s in steps], q)
+    return every, in_order(shard_all, q).reshape(shard.shape), lines
+
+
+def in_order(pieces, at):
+    stacked = jnp.stack(pieces)
+    return jnp.stack([pick(stacked, at ^ place) for place in range(len(pieces))])
+
+
+def sum_in_order(pieces, at):
+    return jnp.sum(in_order(pieces, at), axis=0)
 
 
 def sum_over_ctx(shard, n):
@@ -620,50 +628,55 @@
     )
     sizes = [v.shape[0] for v in vectors]
     packed = jnp.concatenate(vectors)
-    lines = -(-packed.shape[0] // LANES)
+    lines = -(-packed.shape[0] // (8 * LANES)) * 8
     packed = jnp.pad(packed, (0, lines * LANES - packed.shape[0])).reshape(lines, LANES)
-    flat = gather_lines(packed.reshape(1, lines * LANES), shards)
+
+    units = jnp.concatenate(
+        [qkv_weight[None, :, t * model : (t + 1) * model] for t in range(3)] + [out_weight[None]]
+    ).reshape(n, own_rows // parts, model)
+    along_units = along_z(units, shards)
+    flat = gather_lines(packed, shards).reshape(shards, lines * LANES)
+    down_units = down_weight.reshape(n, down_weight.shape[0] // n, model)
+    down_units, up_weight, along_units = lax.optimization_barrier(
+        (down_units, up_weight, along_units)
+    )
+    w_up = lax.all_gather(up_weight, "fsdp", axis=0, tiled=True)
+    unit_columns = between_columns(along_units, n)
+    along_down = along_z(down_units, shards)
+    w_units = (
+        between_cores(units, unit_columns, n, shards)
+        .reshape(4, parts, shards, own_rows // parts, model)
+        .transpose(0, 2, 1, 3, 4)
+        .reshape(4, model, model)
+    )
+    along_down, _ = lax.optimization_barrier((along_down, w_units))
+    down_columns = between_columns(along_down, n)
     whole, start = [], 0
     for size in sizes:
         whole.append(flat[:, start : start + size].astype(F32).reshape(1, shards * size))
         start += size
     gain_one, bias_one, gain_two, bias_two, b_qkv, b_out, b_up, b_down = whole
 
-    w_up = lax.all_gather(up_weight, "fsdp", axis=0, tiled=True)
-    units = jnp.concatenate(
-        [qkv_weight[None, :, t * model : (t + 1) * model] for t in range(3)] + [out_weight[None]]
-    )
-    w_units = gather_units(units.reshape(n, own_rows // parts, model), n, shards)
-    w_units = (
-        w_units.reshape(4, parts, shards, own_rows // parts, model)
-        .transpose(0, 2, 1, 3, 4)
-        .reshape(4, model, model)
-    )
-    w_out = w_units[3]
-    down_units, _ = lax.optimization_barrier(
-        (down_weight.reshape(n, down_weight.shape[0] // n, model), w_units)
-    )
-    w_down = gather_units(down_units, n, shards, True).reshape(hidden, model)
-
     inputs = tokens.transpose(1, 0, 2).reshape(rows, model)
     cot = cotangent.transpose(1, 0, 2).reshape(rows, model)
 
     tables = rotary_tables(n * block_len)
-    own_tables = tuple(
-        lax.dynamic_slice_in_dim(jnp.asarray(t), me * block_len, block_len, 0) for t in tables
-    )
+    def shard_sum(value):
+        return lax.psum_scatter(value, "fsdp", scatter_dimension=0, tiled=True)
 
     sent = project(
-        n, me_arr, inputs, cot, gain_one, bias_one, w_units, b_qkv, own_tables, block_len, width, used
+        n, me_arr, inputs, cot, gain_one, bias_one, w_units, b_qkv, tables, block_len, width, used
     )
     pieces = [sent[0]] + [swap(sent[shift], shift, n) for shift in range(1, n)]
-    answers = attend(n, me_arr, pieces, tables)
-    mlp_inputs, *answers = lax.optimization_barrier((inputs, *answers))
-    answers = [answers[0]] + [swap(answers[shift], shift, n) for shift in range(1, n)]
-
+    mlp_inputs, down_columns, _ = lax.optimization_barrier((inputs, down_columns, sent))
+    w_down = between_cores(down_units, down_columns, n, shards, True).reshape(hidden, model)
     base, grad_base, grad_up, grad_down, grad_up_b, sums_two = mlp(
         mlp_inputs, cot, gain_two, bias_two, b_out + b_down, w_up, b_up, w_down
     )
+    grad_down, pieces = lax.optimization_barrier((grad_down, pieces))
+    answers = attend(n, me_arr, pieces, tables)
+    answers = [answers[0]] + [swap(answers[shift], shift, n) for shift in range(1, n)]
+    shard_down, grad_up, answers = lax.optimization_barrier((shard_sum(grad_down), grad_up, answers))
     core = lax.axis_index("fsdp") % 2
     layer_out, tokens_grad, own, other, sums_one = finish(
         n, me, core, answers, inputs, cot, gain_one, bias_one, base, grad_base, w_units, shards, used
@@ -679,17 +692,14 @@
             .reshape(n, shards // 2, own_rows // parts, model)
         )
 
-    def shard_sum(value):
-        return lax.psum_scatter(value, "fsdp", scatter_dimension=0, tiled=True)
-
-    part_units = sum_units(cut(own), cut(other), n, shards).reshape(4, own_rows, model).astype(F32)
+    lines = jnp.concatenate([sums_one, sums_two, grad_up_b.reshape(-1, model)], axis=0)
+    part_units, part_down, line_sums = sum_units(
+        cut(own), cut(other), lines, shard_down, n, shards
+    )
+    part_units = part_units.reshape(4, own_rows, model).astype(F32)
+    part_down = part_down.astype(F32)
     part_qkv = jnp.concatenate([part_units[t] for t in range(3)], axis=1)
-    part_down = sum_over_ctx(shard_sum(grad_down), n).astype(F32)
     part_up = sum_over_ctx(shard_sum(grad_up), n).astype(F32)
-
-    line_sums = sum_lines(
-        jnp.concatenate([sums_one, sums_two, grad_up_b.reshape(-1, model)], axis=0), n, shards
-    )
     f = lax.axis_index("fsdp")
 
     def shard_of(first, count):

time: 379 us -> 327 us (0.86)
  waiting for transfers between devices: 153 us -> 127 us
  starting transfers between devices: 83.5 us -> 71.2 us
  local copies, waits for them, and re-layouts: 31 us -> 19.9 us
    ppermute x32 -> x33, waiting for transfers between devices: 100 us -> 74.7 us  [swap(): return lax.ppermute(value, 'ctx', [(i, i ^ shift) for i in range(n)])]
    ppermute x26 -> x28, starting transfers between devices: 46.6 us -> 32 us  [swap_shard(): return lax.ppermute(value, 'fsdp', [(i, i ^ shift) for i in range(m)])]
    reshape x2 -> x0, local copies, waits for them, and re-layouts: 4.51 us -> none  [placed(): return value.reshape(seq_count, block_len, model).transpose(1, 0, 2)]
    transpose x0 -> x1, local copies, waits for them, and re-layouts: none -> 4.12 us  [placed(): return value.reshape(seq_count, block_len, model).transpose(1, 0, 2)]
    ppermute x32 -> x33, starting transfers between devices: 36.8 us -> 38.9 us  [swap(): return lax.ppermute(value, 'ctx', [(i, i ^ shift) for i in range(n)])]
    ppermute x26 -> x28, waiting for transfers between devices: 51.8 us -> 50.9 us  [swap_shard(): return lax.ppermute(value, 'fsdp', [(i, i ^ shift) for i in range(m)])]
  transfers between devices with their start and end apart: 61 -> 64, of which waited for: 24 -> 29; matrix products, arithmetic and copies ran while one was open for 10% -> 8% of each run, Pallas kernels for 14% -> 25%
where the time goes in v3:
time: 327 us
  waiting for transfers between devices  127 us (39%)
  Pallas kernels  81.3 us (25%)
  starting transfers between devices  71.2 us (22%)
  local copies, waits for them, and re-layouts  19.9 us (6%)
  between operations  14.5 us (4%)
  other arithmetic  12.4 us (4%)
    ppermute x33, waiting for transfers between devices, swap(): return lax.ppermute(value, 'ctx', [(i, i ^ shift) for i in range(n)])  74.7 us
    ppermute x28, waiting for transfers between devices, swap_shard(): return lax.ppermute(value, 'fsdp', [(i, i ^ shift) for i in range(m)])  50.9 us
    ppermute x33, starting transfers between devices, swap(): return lax.ppermute(value, 'ctx', [(i, i ^ shift) for i in range(n)])  38.9 us
    ppermute x28, starting transfers between devices, swap_shard(): return lax.ppermute(value, 'fsdp', [(i, i ^ shift) for i in range(m)])  32 us
    pallas_call x1, Pallas kernels, mlp(): pl.pallas_call(mlp_kernel, grid=(hidden // chunk,), in_specs=[whole, whol...  26.5 us
    pallas_call x1, Pallas kernels, attend(): pl.pallas_call(functools.partial(attend_kernel, n, block), grid_spec=pltp...  21.4 us
    pallas_call x1, Pallas kernels, finish(): pl.pallas_call(functools.partial(finish_kernel, n, block_len, used, shard...  14 us
    pallas_call x2, Pallas kernels, between_cores(): pl.pallas_call(functools.partial(assemble_kernel, where, len(pieces), sha...  10.9 us
  transfers between devices with their start and end apart: 64, of which 29 were waited for; matrix products, arithmetic and copies ran while one was open for 8% of the time, Pallas kernels for 25%

profile of v3, /device:TPU:0, one launch (start us, length us, event | category | flops | bytes accessed | tf_op | source)
XLA Modules:
  0.0 326.7 jit_solution(4903256559457978044)
XLA Ops:
  7.3 1.2 slice_bitcast_fusion.6
  9.6 3.1 collective-permute-start
  12.7 2.6 collective-permute-start.1
  15.3 3.3 collective-permute-done
  18.6 8.1 %collective-permute-done.1 = bf16[96,768]{1,0:T(8,128)(2,1)S(1)} collective-permute-done((bf16[96,768]{1,0:T(8,128)(2,1)S(1)}, bf16[96,768]{1,0:T(8,128)(2,1)S(1)}, u32[]{:S(2)}, u32[]{:S(2)}) %collective-permute-start.1) | collective-permute-done | bytes 147488 | tf_op jit(solution)/shard_map/ppermute | solution.py:476
  27.0 2.4 collective-permute-start.17
  30.5 1.4 collective-permute-start.19
  31.9 2.0 collective-permute-done.18
  33.9 2.0 collective-permute-done.19
  38.5 1.6 collective-permute-start.7
  40.0 1.5 collective-permute-start.8
  42.3 1.8 collective-permute-start.4
  44.1 13.2 %collective-permute-done.3 = bf16[96,768]{1,0:T(8,128)(2,1)S(1)} collective-permute-done((bf16[96,768]{1,0:T(8,128)(2,1)S(1)}, bf16[96,768]{1,0:T(8,128)(2,1)S(1)}, u32[]{:S(2)}, u32[]{:S(2)}) %collective-permute-start.3) | collective-permute-done | bytes 147488 | tf_op jit(solution)/shard_map/ppermute | solution.py:476
  57.3 1.7 collective-permute-done.4
  59.0 2.5 collective-permute-start.5
  61.5 8.4 %collective-permute-done.5 = bf16[96,768]{1,0:T(8,128)(2,1)S(1)} collective-permute-done((bf16[96,768]{1,0:T(8,128)(2,1)S(1)}, bf16[96,768]{1,0:T(8,128)(2,1)S(1)}, u32[]{:S(2)}, u32[]{:S(2)}) %collective-permute-start.5) | collective-permute-done | bytes 147488 | tf_op jit(solution)/shard_map/ppermute | solution.py:476
  74.3 5.5 %assemble.2 = bf16[4,8,96,768]{3,2,1,0:T(8,128)(2,1)} custom-call(s32[2]{0:T(128)} %pad_add_fusion.1.at, bf16[4,96,768]{2,1,0:T(8,128)(2,1)} %copy-done, bf16[4,96,768]{2,1,0:T(8,128)(2,1)} %copy-done.8, bf16[3,96,768]{2,1,0:T(8,128)(2,1)} %copy-done.2, bf16[3,96,768]{2,1,0:T(8,128)(2,1)} %copy-done.10, bf16[3,96,768]{2,1,0:T(8,128)(2,1)} %copy-done.11, ...), custom_call_target="tpu_custom_call" | custom-call | bytes 9437184 | tf_op jit(solution)/shard_map/assemble/pallas_call | solution.py:525
  79.8 1.5 collective-permute-start.14
  81.3 1.5 collective-permute-start.15
  85.5 8.5 %project.1 = (bf16[4,256,384]{2,1,0:T(8,128)(2,1)}, bf16[4,256,384]{2,1,0:T(8,128)(2,1)}, bf16[4,256,384]{2,1,0:T(8,128)(2,1)}, bf16[4,256,384]{2,1,0:T(8,128)(2,1)}) custom-call(s32[1]{0:T(128)} %bitcast.me, bf16[512,768]{1,0:T(8,128)(2,1)} %bitcast.146, bf16[512,768]{1,0:T(8,128)(2,1)} %bitcast.143, f32[1,768]{1,0:T(1,128)} %reshape.209.gain.refs_6_, ...), custom_call_target="tpu_custom_call" | custom-call | flops 2415919104 | bytes 9437184 | tf_op jit(solution)/shard_map/project/pallas_call | solution.py:124
  94.0 8.6 %collective-permute-done.15.refs_4_ = bf16[3,96,768]{2,1,0:T(8,128)(2,1)S(1)} collective-permute-done((bf16[3,96,768]{2,1,0:T(8,128)(2,1)S(1)}, bf16[3,96,768]{2,1,0:T(8,128)(2,1)S(1)}, u32[]{:S(2)}, u32[]{:S(2)}) %collective-permute-start.15) | collective-permute-done | bytes 442400 | tf_op jit(solution)/shard_map/ppermute | solution.py:472
  107.8 1.2 collective-permute-start.26
  109.9 1.4 collective-permute-start.28
  111.3 5.4 %assemble.3 = bf16[8,4,96,768]{3,2,1,0:T(8,128)(2,1)} custom-call(s32[2]{0:T(128)} %pad_add_fusion.1.at, bf16[4,96,768]{2,1,0:T(8,128)(2,1)} %bitcast.138, bf16[4,96,768]{2,1,0:T(8,128)(2,1)} %copy-done.7, bf16[3,96,768]{2,1,0:T(8,128)(2,1)} %copy-done.3, bf16[3,96,768]{2,1,0:T(8,128)(2,1)} %copy-done.12, bf16[3,96,768]{2,1,0:T(8,128)(2,1)} %copy-done.13, ...), custom_call_target="tpu_custom_call" | custom-call | bytes 9437184 | tf_op jit(solution)/shard_map/assemble/pallas_call | solution.py:525
  116.8 26.5 %mlp.1 = (f32[512,768]{1,0:T(8,128)}, f32[512,768]{1,0:T(8,128)}, bf16[768,3072]{1,0:T(8,128)(2,1)}, bf16[3072,768]{1,0:T(8,128)(2,1)}, f32[1,3072]{1,0:T(1,128)}, /*index=5*/f32[8,768]{1,0:T(8,128)}) custom-call(bf16[512,768]{1,0:T(8,128)(2,1)} %bitcast.147, bf16[512,768]{1,0:T(8,128)(2,1)} %bitcast.144, f32[1,768]{1,0:T(1,128)} %reshape.214.gain, ...), custom_call_target="tpu_custom_call" | custom-call | flops 14495514624 | bytes 23592960 | tf_op jit(solution)/shard_map/mlp/pallas_call | solution.py:355
  143.8 1.6 collective-permute-done.28.refs_3_
  145.7 21.4 %attend.1 = (bf16[4,256,384]{2,1,0:T(8,128)(2,1)}, bf16[4,256,384]{2,1,0:T(8,128)(2,1)}, bf16[4,256,384]{2,1,0:T(8,128)(2,1)}, bf16[4,256,384]{2,1,0:T(8,128)(2,1)}) custom-call(s32[1]{0:T(128)} %bitcast.me, bf16[4,256,384]{2,1,0:T(8,128)(2,1)} %get-tuple-element.79.refs_0_, bf16[4,256,384]{2,1,0:T(8,128)(2,1)} %collective-permute-done.26.refs_1_, ...), custom_call_target="tpu_custom_call" | custom-call | flops 120795955200 | bytes 6291456 | tf_op jit(solution)/shard_map/attend/pallas_call | solution.py:284
  167.9 1.6 collective-permute-start.30
  169.5 1.2 collective-permute-start.31
  170.7 17.2 %collective-permute-done.29.refs_1_ = bf16[4,256,384]{2,1,0:T(8,128)(2,1)S(1)} collective-permute-done((bf16[4,256,384]{2,1,0:T(8,128)(2,1)}, bf16[4,256,384]{2,1,0:T(8,128)(2,1)S(1)}, u32[]{:S(2)}, u32[]{:S(2)}) %collective-permute-start.29) | collective-permute-done | bytes 786464 | tf_op jit(solution)/shard_map/ppermute | solution.py:472
  187.9 15.4 %collective-permute-done.30.refs_2_ = bf16[4,256,384]{2,1,0:T(8,128)(2,1)S(1)} collective-permute-done((bf16[4,256,384]{2,1,0:T(8,128)(2,1)}, bf16[4,256,384]{2,1,0:T(8,128)(2,1)S(1)}, u32[]{:S(2)}, u32[]{:S(2)}) %collective-permute-start.30) | collective-permute-done | bytes 786464 | tf_op jit(solution)/shard_map/ppermute | solution.py:472
  203.3 1.7 reduce-scatter.3.cloned.1.call-done
  205.6 14.0 %finish.1 = (bf16[512,768]{1,0:T(8,128)(2,1)}, bf16[512,768]{1,0:T(8,128)(2,1)}, bf16[4,4,96,768]{3,2,1,0:T(8,128)(2,1)}, bf16[4,4,96,768]{3,2,1,0:T(8,128)(2,1)}, f32[8,768]{1,0:T(8,128)}) custom-call(s32[2]{0:T(128)} %pad_add_fusion.at, bf16[4,256,384]{2,1,0:T(8,128)(2,1)} %get-tuple-element.87.refs_0_, bf16[4,256,384]{2,1,0:T(8,128)(2,1)} %copy-done.30, ...), custom_call_target="tpu_custom_call" | custom-call | flops 4831838208 | bytes 15728640 | tf_op jit(solution)/shard_map/finish/pallas_call | solution.py:439
  222.2 1.5 collective-permute-start.43
  224.4 1.5 collective-permute-start.33
  225.9 1.5 collective-permute-start.34
  227.9 4.1 %copy_bitcast_fusion = (bf16[256,2,768]{2,1,0:T(2,128)(2,1)}, bf16[256,2,768]{2,1,0:T(2,128)(2,1)}) fusion(bf16[2,256,768]{2,1,0:T(8,128)(2,1)} %bitcast.150, bf16[2,256,768]{2,1,0:T(8,128)(2,1)} %bitcast.149), kind=kLoop, calls=%fused_computation.6 | loop fusion | bytes 3145728 | tf_op jit(solution)/shard_map/transpose | solution.py:686
  232.1 1.4 collective-permute-start.44
  233.5 1.5 collective-permute-start.45
  235.0 5.4 %collective-permute-start.36 = (f32[20,768]{1,0:T(8,128)S(1)}, f32[20,768]{1,0:T(8,128)S(1)}, u32[]{:S(2)}, u32[]{:S(2)}) collective-permute-start(f32[20,768]{1,0:T(8,128)S(1)} %fusion.19), channel_id=1, source_target_pairs={{0,2},{1,3},{2,0},{3,1},{4,6},{5,7},{6,4},{7,5},{8,10},{9,11},{10,... | collective-permute-start | bytes 184328 | tf_op jit(solution)/shard_map/ppermute | solution.py:476
  240.4 1.6 collective-permute-start.37
  242.9 1.5 collective-permute-start.38
  246.5 1.4 collective-permute-start.42
  248.0 3.1 collective-permute-done.37
  251.1 2.7 collective-permute-done.38
  253.9 6.8 %collective-permute-done.40 = bf16[4,96,768]{2,1,0:T(8,128)(2,1)S(1)} collective-permute-done((bf16[4,96,768]{2,1,0:T(8,128)(2,1)S(1)}, bf16[4,96,768]{2,1,0:T(8,128)(2,1)S(1)}, u32[]{:S(2)}, u32[]{:S(2)}) %collective-permute-start.40) | collective-permute-done | bytes 589856 | tf_op jit(solution)/shard_map/ppermute | solution.py:472
  260.7 10.1 %collective-permute-done.41 = bf16[4,96,768]{2,1,0:T(8,128)(2,1)S(1)} collective-permute-done((bf16[4,96,768]{2,1,0:T(8,128)(2,1)S(1)}, bf16[4,96,768]{2,1,0:T(8,128)(2,1)S(1)}, u32[]{:S(2)}, u32[]{:S(2)}) %collective-permute-start.41) | collective-permute-done | bytes 589856 | tf_op jit(solution)/shard_map/ppermute | solution.py:472
  271.1 2.9 collective-permute-start.46
  274.0 1.6 collective-permute-start.47
  275.6 1.4 collective-permute-start.48
  278.4 1.5 collective-permute-start.50
  279.9 1.8 collective-permute-start.51
  281.7 4.6 %collective-permute-done.47 = bf16[96,768]{1,0:T(8,128)(2,1)S(1)} collective-permute-done((bf16[96,768]{1,0:T(8,128)(2,1)S(1)}, bf16[96,768]{1,0:T(8,128)(2,1)S(1)}, u32[]{:S(2)}, u32[]{:S(2)}) %collective-permute-start.47) | collective-permute-done | bytes 147488 | tf_op jit(solution)/shard_map/ppermute | solution.py:476
  287.0 2.6 collective-permute-start.53
  292.1 1.8 collective-permute-done.53
  293.9 3.2 collective-permute-done.54
  300.1 2.7 collective-permute-start.57
  303.9 2.1 collective-permute-done.55
  306.0 2.8 collective-permute-done.56
  309.8 1.7 collective-permute-start.58
  312.0 1.3 collective-permute-start.60
  313.4 1.1 bitcast_convert_fusion
  315.0 3.2 collective-permute-done.59
  318.5 1.2 bitcast_convert_fusion.1
  (221 shorter events, 39.7 us)
Async XLA Ops:
  7.3 109.5 %all-gather.2.cloned.1.call-start = ((), (), s32[]{:S(2)}) async-start(), calls=%async_computation.2 | async-start | bytes 5308416 | tf_op jit(solution)/shard_map/all_gather | solution.py:643
  9.6 8.9 %collective-permute-start = (bf16[96,768]{1,0:T(8,128)(2,1)S(1)}, bf16[96,768]{1,0:T(8,128)(2,1)S(1)}, u32[]{:S(2)}, u32[]{:S(2)}) collective-permute-start(bf16[96,768]{1,0:T(8,128)(2,1)S(1)} %dynamic-slice_bitcast_fusion.13), channel_id=1, source_target_pairs={{0,2},{1,3},{2,0},{3,1},{4,6},{5,7},{6,4},{7,5},{8,10},{9,11},{10,... | collective-permute-start | bytes 442376 | tf_op jit(solution)/shard_map/ppermute | solution.py:476
  12.7 14.0 %collective-permute-start.1 = (bf16[96,768]{1,0:T(8,128)(2,1)S(1)}, bf16[96,768]{1,0:T(8,128)(2,1)S(1)}, u32[]{:S(2)}, u32[]{:S(2)}) collective-permute-start(bf16[96,768]{1,0:T(8,128)(2,1)S(1)} %dynamic-slice_bitcast_fusion.13), channel_id=1, source_target_pairs={{0,4},{1,5},{2,6},{3,7},{4,0},{5,1},{6,2},{7,3},{8,12},{9,13},{10,... | collective-permute-start | bytes 442376 | tf_op jit(solution)/shard_map/ppermute | solution.py:476
  15.3 11.4 %collective-permute-start.2 = (bf16[96,768]{1,0:T(8,128)(2,1)S(1)}, bf16[96,768]{1,0:T(8,128)(2,1)S(1)}, u32[]{:S(2)}, u32[]{:S(2)}) collective-permute-start(bf16[96,768]{1,0:T(8,128)(2,1)S(1)} %dynamic-slice_bitcast_fusion.13), channel_id=1, source_target_pairs={{0,6},{1,7},{2,4},{3,5},{4,2},{5,3},{6,0},{7,1},{8,14},{9,15},{10,... | collective-permute-start | bytes 442376 | tf_op jit(solution)/shard_map/ppermute | solution.py:476
  26.8 178.1 %reduce-scatter.3.cloned.1.call-start = ((), (), s32[]{:S(2)}) async-start(), calls=%async_computation.3 | async-start | bytes 5308416 | tf_op jit(solution)/shard_map/reduce_scatter | solution.py:665
  27.0 4.8 %collective-permute-start.17 = (bf16[16,128]{1,0:T(8,128)(2,1)S(1)}, bf16[16,128]{1,0:T(8,128)(2,1)S(1)}, u32[]{:S(2)}, u32[]{:S(2)}) collective-permute-start(bf16[16,128]{1,0:T(8,128)(2,1)S(1)} %get-tuple-element.155), channel_id=1, source_target_pairs={{0,2},{1,3},{2,0},{3,1},{4,6},{5,7},{6,4},{7,5},{8,10},{9,11},{10,... | collective-permute-start | bytes 12296 | tf_op jit(solution)/shard_map/ppermute | solution.py:476
  29.4 4.5 %collective-permute-start.18 = (bf16[16,128]{1,0:T(8,128)(2,1)S(1)}, bf16[16,128]{1,0:T(8,128)(2,1)S(1)}, u32[]{:S(2)}, u32[]{:S(2)}) collective-permute-start(bf16[16,128]{1,0:T(8,128)(2,1)S(1)} %get-tuple-element.155), channel_id=1, source_target_pairs={{0,4},{1,5},{2,6},{3,7},{4,0},{5,1},{6,2},{7,3},{8,12},{9,13},{10,... | collective-permute-start | bytes 12296 | tf_op jit(solution)/shard_map/ppermute | solution.py:476
  30.5 5.4 %collective-permute-start.19 = (bf16[16,128]{1,0:T(8,128)(2,1)S(1)}, bf16[16,128]{1,0:T(8,128)(2,1)S(1)}, u32[]{:S(2)}, u32[]{:S(2)}) collective-permute-start(bf16[16,128]{1,0:T(8,128)(2,1)S(1)} %get-tuple-element.155), channel_id=1, source_target_pairs={{0,6},{1,7},{2,4},{3,5},{4,2},{5,3},{6,0},{7,1},{8,14},{9,15},{10,... | collective-permute-start | bytes 12296 | tf_op jit(solution)/shard_map/ppermute | solution.py:476
  35.9 2.5 collective-permute-start.20
  38.5 31.5 %collective-permute-start.7 = (bf16[3,96,768]{2,1,0:T(8,128)(2,1)S(1)}, bf16[3,96,768]{2,1,0:T(8,128)(2,1)S(1)}, u32[]{:S(2)}, u32[]{:S(2)}) collective-permute-start(bf16[3,96,768]{2,1,0:T(8,128)(2,1)S(1)} %pad_maximum_fusion.7.refs_2_), channel_id=1, source_target_pairs={{0,8},{8,0},{16,24},{24,16},{1,9},{9,1},{17,25},{25,17},{2,10},{10... | collective-permute-start | bytes 1327112 | tf_op jit(solution)/shard_map/ppermute | solution.py:472
  40.0 30.4 %collective-permute-start.8 = (bf16[3,96,768]{2,1,0:T(8,128)(2,1)S(1)}, bf16[3,96,768]{2,1,0:T(8,128)(2,1)S(1)}, u32[]{:S(2)}, u32[]{:S(2)}) collective-permute-start(bf16[3,96,768]{2,1,0:T(8,128)(2,1)S(1)} %pad_maximum_fusion.7.refs_2_), channel_id=1, source_target_pairs={{0,16},{8,24},{16,0},{24,8},{1,17},{9,25},{17,1},{25,9},{2,18},{10... | collective-permute-start | bytes 1327112 | tf_op jit(solution)/shard_map/ppermute | solution.py:472
  41.6 29.0 %collective-permute-start.9 = (bf16[3,96,768]{2,1,0:T(8,128)(2,1)S(1)}, bf16[3,96,768]{2,1,0:T(8,128)(2,1)}, u32[]{:S(2)}, u32[]{:S(2)}) collective-permute-start(bf16[3,96,768]{2,1,0:T(8,128)(2,1)S(1)} %pad_maximum_fusion.7.refs_2_), channel_id=1, source_target_pairs={{0,24},{8,16},{16,8},{24,0},{1,25},{9,17},{17,9},{25,1},{2,26},{10... | collective-permute-start | bytes 1327112 | tf_op jit(solution)/shard_map/ppermute | solution.py:472
  42.0 15.2 %collective-permute-start.3 = (bf16[96,768]{1,0:T(8,128)(2,1)S(1)}, bf16[96,768]{1,0:T(8,128)(2,1)S(1)}, u32[]{:S(2)}, u32[]{:S(2)}) collective-permute-start(bf16[96,768]{1,0:T(8,128)(2,1)S(1)} %dynamic-slice_bitcast_fusion.12), channel_id=1, source_target_pairs={{0,2},{1,3},{2,0},{3,1},{4,6},{5,7},{6,4},{7,5},{8,10},{9,11},{10,... | collective-permute-start | bytes 442376 | tf_op jit(solution)/shard_map/ppermute | solution.py:476
  42.3 16.8 %collective-permute-start.4 = (bf16[96,768]{1,0:T(8,128)(2,1)S(1)}, bf16[96,768]{1,0:T(8,128)(2,1)S(1)}, u32[]{:S(2)}, u32[]{:S(2)}) collective-permute-start(bf16[96,768]{1,0:T(8,128)(2,1)S(1)} %dynamic-slice_bitcast_fusion.12), channel_id=1, source_target_pairs={{0,4},{1,5},{2,6},{3,7},{4,0},{5,1},{6,2},{7,3},{8,12},{9,13},{10,... | collective-permute-start | bytes 442376 | tf_op jit(solution)/shard_map/ppermute | solution.py:476
  57.3 16.2 %collective-permute-start.6 = (bf16[4,96,768]{2,1,0:T(8,128)(2,1)S(1)}, bf16[4,96,768]{2,1,0:T(8,128)(2,1)S(1)}, u32[]{:S(2)}, u32[]{:S(2)}) collective-permute-start(bf16[4,96,768]{2,1,0:T(8,128)(2,1)S(1)} %pad_maximum_fusion.1.refs_0_), channel_id=1, source_target_pairs={{0,1},{1,0},{2,3},{3,2},{4,5},{5,4},{6,7},{7,6},{8,9},{9,8},{10,11... | collective-permute-start | bytes 1769480 | tf_op jit(solution)/shard_map/ppermute | solution.py:476
  59.0 10.9 %collective-permute-start.5 = (bf16[96,768]{1,0:T(8,128)(2,1)S(1)}, bf16[96,768]{1,0:T(8,128)(2,1)S(1)}, u32[]{:S(2)}, u32[]{:S(2)}) collective-permute-start(bf16[96,768]{1,0:T(8,128)(2,1)S(1)} %dynamic-slice_bitcast_fusion.12), channel_id=1, source_target_pairs={{0,6},{1,7},{2,4},{3,5},{4,2},{5,3},{6,0},{7,1},{8,14},{9,15},{10,... | collective-permute-start | bytes 442376 | tf_op jit(solution)/shard_map/ppermute | solution.py:476
  70.0 3.5 %collective-permute-start.10 = (bf16[3,96,768]{2,1,0:T(8,128)(2,1)S(1)}, bf16[3,96,768]{2,1,0:T(8,128)(2,1)}, u32[]{:S(2)}, u32[]{:S(2)}) collective-permute-start(bf16[3,96,768]{2,1,0:T(8,128)(2,1)S(1)} %pad_maximum_fusion.7.refs_2_), channel_id=1, source_target_pairs={{0,1},{1,0},{2,3},{3,2},{4,5},{5,4},{6,7},{7,6},{8,9},{9,8},{10,11... | collective-permute-start | bytes 1327112 | tf_op jit(solution)/shard_map/ppermute | solution.py:476
  70.0 3.5 %collective-permute-start.11 = (bf16[3,96,768]{2,1,0:T(8,128)(2,1)S(1)}, bf16[3,96,768]{2,1,0:T(8,128)(2,1)}, u32[]{:S(2)}, u32[]{:S(2)}) collective-permute-start(bf16[3,96,768]{2,1,0:T(8,128)(2,1)S(1)} %collective-permute-done.7.refs_3_), channel_id=1, source_target_pairs={{0,1},{1,0},{2,3},{3,2},{4,5},{5,4},{6,7},{7,6},{8,9},{9,8},{10,11... | collective-permute-start | bytes 1327112 | tf_op jit(solution)/shard_map/ppermute | solution.py:476
  70.5 3.3 %collective-permute-start.12 = (bf16[3,96,768]{2,1,0:T(8,128)(2,1)S(1)}, bf16[3,96,768]{2,1,0:T(8,128)(2,1)}, u32[]{:S(2)}, u32[]{:S(2)}) collective-permute-start(bf16[3,96,768]{2,1,0:T(8,128)(2,1)S(1)} %collective-permute-done.8.refs_4_), channel_id=1, source_target_pairs={{0,1},{1,0},{2,3},{3,2},{4,5},{5,4},{6,7},{7,6},{8,9},{9,8},{10,11... | collective-permute-start | bytes 1327112 | tf_op jit(solution)/shard_map/ppermute | solution.py:476
  70.6 3.2 collective-permute-start.13
  79.8 14.2 %collective-permute-start.14 = (bf16[3,96,768]{2,1,0:T(8,128)(2,1)S(1)}, bf16[3,96,768]{2,1,0:T(8,128)(2,1)S(1)}, u32[]{:S(2)}, u32[]{:S(2)}) collective-permute-start(bf16[3,96,768]{2,1,0:T(8,128)(2,1)S(1)} %pad_maximum_fusion.8.refs_2_), channel_id=1, source_target_pairs={{0,8},{8,0},{16,24},{24,16},{1,9},{9,1},{17,25},{25,17},{2,10},{10... | collective-permute-start | bytes 1327112 | tf_op jit(solution)/shard_map/ppermute | solution.py:472
  81.3 21.3 %collective-permute-start.15 = (bf16[3,96,768]{2,1,0:T(8,128)(2,1)S(1)}, bf16[3,96,768]{2,1,0:T(8,128)(2,1)S(1)}, u32[]{:S(2)}, u32[]{:S(2)}) collective-permute-start(bf16[3,96,768]{2,1,0:T(8,128)(2,1)S(1)} %pad_maximum_fusion.8.refs_2_), channel_id=1, source_target_pairs={{0,16},{8,24},{16,0},{24,8},{1,17},{9,25},{17,1},{25,9},{2,18},{10... | collective-permute-start | bytes 1327112 | tf_op jit(solution)/shard_map/ppermute | solution.py:472
  82.8 19.8 %collective-permute-start.16 = (bf16[3,96,768]{2,1,0:T(8,128)(2,1)S(1)}, bf16[3,96,768]{2,1,0:T(8,128)(2,1)S(1)}, u32[]{:S(2)}, u32[]{:S(2)}) collective-permute-start(bf16[3,96,768]{2,1,0:T(8,128)(2,1)S(1)} %pad_maximum_fusion.8.refs_2_), channel_id=1, source_target_pairs={{0,24},{8,16},{16,8},{24,0},{1,25},{9,17},{17,9},{25,1},{2,26},{10... | collective-permute-start | bytes 1327112 | tf_op jit(solution)/shard_map/ppermute | solution.py:472
  85.5 22.3 %collective-permute-start.21 = (bf16[4,96,768]{2,1,0:T(8,128)(2,1)S(1)}, bf16[4,96,768]{2,1,0:T(8,128)(2,1)S(1)}, u32[]{:S(2)}, u32[]{:S(2)}) collective-permute-start(bf16[4,96,768]{2,1,0:T(8,128)(2,1)S(1)} %bitcast.140), channel_id=1, source_target_pairs={{0,1},{1,0},{2,3},{3,2},{4,5},{5,4},{6,7},{7,6},{8,9},{9,8},{10,11... | collective-permute-start | bytes 1769480 | tf_op jit(solution)/shard_map/ppermute | solution.py:476
  102.7 6.3 %collective-permute-start.22 = (bf16[3,96,768]{2,1,0:T(8,128)(2,1)S(1)}, bf16[3,96,768]{2,1,0:T(8,128)(2,1)S(1)}, u32[]{:S(2)}, u32[]{:S(2)}) collective-permute-start(bf16[3,96,768]{2,1,0:T(8,128)(2,1)S(1)} %pad_maximum_fusion.8.refs_2_), channel_id=1, source_target_pairs={{0,1},{1,0},{2,3},{3,2},{4,5},{5,4},{6,7},{7,6},{8,9},{9,8},{10,11... | collective-permute-start | bytes 1327112 | tf_op jit(solution)/shard_map/ppermute | solution.py:476
  102.7 7.1 %collective-permute-start.23 = (bf16[3,96,768]{2,1,0:T(8,128)(2,1)S(1)}, bf16[3,96,768]{2,1,0:T(8,128)(2,1)}, u32[]{:S(2)}, u32[]{:S(2)}) collective-permute-start(bf16[3,96,768]{2,1,0:T(8,128)(2,1)S(1)} %collective-permute-done.14.refs_3_), channel_id=1, source_target_pairs={{0,1},{1,0},{2,3},{3,2},{4,5},{5,4},{6,7},{7,6},{8,9},{9,8},{10,11... | collective-permute-start | bytes 1327112 | tf_op jit(solution)/shard_map/ppermute | solution.py:476
  103.2 8.0 %collective-permute-start.24 = (bf16[3,96,768]{2,1,0:T(8,128)(2,1)S(1)}, bf16[3,96,768]{2,1,0:T(8,128)(2,1)}, u32[]{:S(2)}, u32[]{:S(2)}) collective-permute-start(bf16[3,96,768]{2,1,0:T(8,128)(2,1)S(1)} %collective-permute-done.15.refs_4_), channel_id=1, source_target_pairs={{0,1},{1,0},{2,3},{3,2},{4,5},{5,4},{6,7},{7,6},{8,9},{9,8},{10,11... | collective-permute-start | bytes 1327112 | tf_op jit(solution)/shard_map/ppermute | solution.py:476
  103.3 8.0 %collective-permute-start.25 = (bf16[3,96,768]{2,1,0:T(8,128)(2,1)S(1)}, bf16[3,96,768]{2,1,0:T(8,128)(2,1)}, u32[]{:S(2)}, u32[]{:S(2)}) collective-permute-start(bf16[3,96,768]{2,1,0:T(8,128)(2,1)S(1)} %collective-permute-done.16.refs_5_), channel_id=1, source_target_pairs={{0,1},{1,0},{2,3},{3,2},{4,5},{5,4},{6,7},{7,6},{8,9},{9,8},{10,11... | collective-permute-start | bytes 1327112 | tf_op jit(solution)/shard_map/ppermute | solution.py:476
  107.8 35.5 %collective-permute-start.26 = (bf16[4,256,384]{2,1,0:T(8,128)(2,1)}, bf16[4,256,384]{2,1,0:T(8,128)(2,1)}, u32[]{:S(2)}, u32[]{:S(2)}) collective-permute-start(bf16[4,256,384]{2,1,0:T(8,128)(2,1)} %get-tuple-element.67), channel_id=1, source_target_pairs={{0,8},{8,0},{16,24},{24,16},{1,9},{9,1},{17,25},{25,17},{2,10},{10... | collective-permute-start | bytes 2359304 | tf_op jit(solution)/shard_map/ppermute | solution.py:472
  109.0 34.9 %collective-permute-start.27 = (bf16[4,256,384]{2,1,0:T(8,128)(2,1)}, bf16[4,256,384]{2,1,0:T(8,128)(2,1)}, u32[]{:S(2)}, u32[]{:S(2)}) collective-permute-start(bf16[4,256,384]{2,1,0:T(8,128)(2,1)} %get-tuple-element.68), channel_id=1, source_target_pairs={{0,16},{8,24},{16,0},{24,8},{1,17},{9,25},{17,1},{25,9},{2,18},{10... | collective-permute-start | bytes 2359304 | tf_op jit(solution)/shard_map/ppermute | solution.py:472
  109.9 35.6 %collective-permute-start.28 = (bf16[4,256,384]{2,1,0:T(8,128)(2,1)}, bf16[4,256,384]{2,1,0:T(8,128)(2,1)}, u32[]{:S(2)}, u32[]{:S(2)}) collective-permute-start(bf16[4,256,384]{2,1,0:T(8,128)(2,1)} %get-tuple-element.69), channel_id=1, source_target_pairs={{0,24},{8,16},{16,8},{24,0},{1,25},{9,17},{17,9},{25,1},{2,26},{10... | collective-permute-start | bytes 2359304 | tf_op jit(solution)/shard_map/ppermute | solution.py:472
  145.5 152.8 %reduce-scatter.5.cloned.1.call-start = ((), (), s32[]{:S(2)}) async-start(), calls=%async_computation.4 | async-start | bytes 5308416 | tf_op jit(solution)/shard_map/reduce_scatter | solution.py:665
  167.2 20.7 %collective-permute-start.29 = (bf16[4,256,384]{2,1,0:T(8,128)(2,1)}, bf16[4,256,384]{2,1,0:T(8,128)(2,1)S(1)}, u32[]{:S(2)}, u32[]{:S(2)}) collective-permute-start(bf16[4,256,384]{2,1,0:T(8,128)(2,1)} %get-tuple-element.84), channel_id=1, source_target_pairs={{0,8},{8,0},{16,24},{24,16},{1,9},{9,1},{17,25},{25,17},{2,10},{10... | collective-permute-start | bytes 2359304 | tf_op jit(solution)/shard_map/ppermute | solution.py:472
  167.9 35.3 %collective-permute-start.30 = (bf16[4,256,384]{2,1,0:T(8,128)(2,1)}, bf16[4,256,384]{2,1,0:T(8,128)(2,1)S(1)}, u32[]{:S(2)}, u32[]{:S(2)}) collective-permute-start(bf16[4,256,384]{2,1,0:T(8,128)(2,1)} %get-tuple-element.85), channel_id=1, source_target_pairs={{0,16},{8,24},{16,0},{24,8},{1,17},{9,25},{17,1},{25,9},{2,18},{10... | collective-permute-start | bytes 2359304 | tf_op jit(solution)/shard_map/ppermute | solution.py:472
  169.5 33.8 %collective-permute-start.31 = (bf16[4,256,384]{2,1,0:T(8,128)(2,1)}, bf16[4,256,384]{2,1,0:T(8,128)(2,1)S(1)}, u32[]{:S(2)}, u32[]{:S(2)}) collective-permute-start(bf16[4,256,384]{2,1,0:T(8,128)(2,1)} %get-tuple-element.86), channel_id=1, source_target_pairs={{0,24},{8,16},{16,8},{24,0},{1,25},{9,17},{17,9},{25,1},{2,26},{10... | collective-permute-start | bytes 2359304 | tf_op jit(solution)/shard_map/ppermute | solution.py:472
  219.6 20.9 %collective-permute-start.39 = (bf16[4,4,96,768]{3,2,1,0:T(8,128)(2,1)}, bf16[4,4,96,768]{3,2,1,0:T(8,128)(2,1)S(1)}, u32[]{:S(2)}, u32[]{:S(2)}) collective-permute-start(bf16[4,4,96,768]{3,2,1,0:T(8,128)(2,1)} %get-tuple-element.102), channel_id=1, source_target_pairs={{0,1},{1,0},{2,3},{3,2},{4,5},{5,4},{6,7},{7,6},{8,9},{9,8},{10,11... | collective-permute-start | bytes 7077896 | tf_op jit(solution)/shard_map/ppermute | solution.py:476
  221.7 2.7 collective-permute-start.32
  222.2 20.7 %collective-permute-start.43 = (bf16[96,768]{1,0:T(8,128)(2,1)S(1)}, bf16[96,768]{1,0:T(8,128)(2,1)S(1)}, u32[]{:S(2)}, u32[]{:S(2)}) collective-permute-start(bf16[96,768]{1,0:T(8,128)(2,1)S(1)} %get-tuple-element.137), channel_id=1, source_target_pairs={{0,8},{8,0},{16,24},{24,16},{1,9},{9,1},{17,25},{25,17},{2,10},{10... | collective-permute-start | bytes 442376 | tf_op jit(solution)/shard_map/ppermute | solution.py:472
  224.4 7.7 %collective-permute-start.33 = (f32[20,768]{1,0:T(8,128)S(1)}, f32[20,768]{1,0:T(8,128)S(1)}, u32[]{:S(2)}, u32[]{:S(2)}) collective-permute-start(f32[20,768]{1,0:T(8,128)S(1)} %add.166), channel_id=1, source_target_pairs={{0,8},{8,0},{16,24},{24,16},{1,9},{9,1},{17,25},{25,17},{2,10},{10... | collective-permute-start | bytes 184328 | tf_op jit(solution)/shard_map/ppermute | solution.py:472
  225.9 7.6 %collective-permute-start.34 = (f32[20,768]{1,0:T(8,128)S(1)}, f32[20,768]{1,0:T(8,128)S(1)}, u32[]{:S(2)}, u32[]{:S(2)}) collective-permute-start(f32[20,768]{1,0:T(8,128)S(1)} %add.166), channel_id=1, source_target_pairs={{0,16},{8,24},{16,0},{24,8},{1,17},{9,25},{17,1},{25,9},{2,18},{10... | collective-permute-start | bytes 184328 | tf_op jit(solution)/shard_map/ppermute | solution.py:472
  227.4 7.6 %collective-permute-start.35 = (f32[20,768]{1,0:T(8,128)S(1)}, f32[20,768]{1,0:T(8,128)S(1)}, u32[]{:S(2)}, u32[]{:S(2)}) collective-permute-start(f32[20,768]{1,0:T(8,128)S(1)} %add.166), channel_id=1, source_target_pairs={{0,24},{8,16},{16,8},{24,0},{1,25},{9,17},{17,9},{25,1},{2,26},{10... | collective-permute-start | bytes 184328 | tf_op jit(solution)/shard_map/ppermute | solution.py:472
  232.1 12.4 %collective-permute-start.44 = (bf16[96,768]{1,0:T(8,128)(2,1)S(1)}, bf16[96,768]{1,0:T(8,128)(2,1)S(1)}, u32[]{:S(2)}, u32[]{:S(2)}) collective-permute-start(bf16[96,768]{1,0:T(8,128)(2,1)S(1)} %get-tuple-element.139), channel_id=1, source_target_pairs={{0,16},{8,24},{16,0},{24,8},{1,17},{9,25},{17,1},{25,9},{2,18},{10... | collective-permute-start | bytes 442376 | tf_op jit(solution)/shard_map/ppermute | solution.py:472
  233.5 11.5 %collective-permute-start.45 = (bf16[96,768]{1,0:T(8,128)(2,1)S(1)}, bf16[96,768]{1,0:T(8,128)(2,1)S(1)}, u32[]{:S(2)}, u32[]{:S(2)}) collective-permute-start(bf16[96,768]{1,0:T(8,128)(2,1)S(1)} %get-tuple-element.138), channel_id=1, source_target_pairs={{0,24},{8,16},{16,8},{24,0},{1,25},{9,17},{17,9},{25,1},{2,26},{10... | collective-permute-start | bytes 442376 | tf_op jit(solution)/shard_map/ppermute | solution.py:472
  235.0 11.5 %collective-permute-start.36 = (f32[20,768]{1,0:T(8,128)S(1)}, f32[20,768]{1,0:T(8,128)S(1)}, u32[]{:S(2)}, u32[]{:S(2)}) collective-permute-start(f32[20,768]{1,0:T(8,128)S(1)} %fusion.19), channel_id=1, source_target_pairs={{0,2},{1,3},{2,0},{3,1},{4,6},{5,7},{6,4},{7,5},{8,10},{9,11},{10,... | collective-permute-start | bytes 184328 | tf_op jit(solution)/shard_map/ppermute | solution.py:476
  240.4 10.7 %collective-permute-start.37 = (f32[20,768]{1,0:T(8,128)S(1)}, f32[20,768]{1,0:T(8,128)S(1)}, u32[]{:S(2)}, u32[]{:S(2)}) collective-permute-start(f32[20,768]{1,0:T(8,128)S(1)} %fusion.19), channel_id=1, source_target_pairs={{0,4},{1,5},{2,6},{3,7},{4,0},{5,1},{6,2},{7,3},{8,12},{9,13},{10,... | collective-permute-start | bytes 184328 | tf_op jit(solution)/shard_map/ppermute | solution.py:476
  242.9 10.9 %collective-permute-start.38 = (f32[20,768]{1,0:T(8,128)S(1)}, f32[20,768]{1,0:T(8,128)S(1)}, u32[]{:S(2)}, u32[]{:S(2)}) collective-permute-start(f32[20,768]{1,0:T(8,128)S(1)} %fusion.19), channel_id=1, source_target_pairs={{0,6},{1,7},{2,4},{3,5},{4,2},{5,3},{6,0},{7,1},{8,14},{9,15},{10,... | collective-permute-start | bytes 184328 | tf_op jit(solution)/shard_map/ppermute | solution.py:476
  244.4 16.3 %collective-permute-start.40 = (bf16[4,96,768]{2,1,0:T(8,128)(2,1)S(1)}, bf16[4,96,768]{2,1,0:T(8,128)(2,1)S(1)}, u32[]{:S(2)}, u32[]{:S(2)}) collective-permute-start(bf16[4,96,768]{2,1,0:T(8,128)(2,1)S(1)} %get-tuple-element.112), channel_id=1, source_target_pairs={{0,8},{8,0},{16,24},{24,16},{1,9},{9,1},{17,25},{25,17},{2,10},{10... | collective-permute-start | bytes 1769480 | tf_op jit(solution)/shard_map/ppermute | solution.py:472
  245.0 25.7 %collective-permute-start.41 = (bf16[4,96,768]{2,1,0:T(8,128)(2,1)S(1)}, bf16[4,96,768]{2,1,0:T(8,128)(2,1)S(1)}, u32[]{:S(2)}, u32[]{:S(2)}) collective-permute-start(bf16[4,96,768]{2,1,0:T(8,128)(2,1)S(1)} %get-tuple-element.114), channel_id=1, source_target_pairs={{0,16},{8,24},{16,0},{24,8},{1,17},{9,25},{17,1},{25,9},{2,18},{10... | collective-permute-start | bytes 1769480 | tf_op jit(solution)/shard_map/ppermute | solution.py:472
  246.5 24.2 %collective-permute-start.42 = (bf16[4,96,768]{2,1,0:T(8,128)(2,1)S(1)}, bf16[4,96,768]{2,1,0:T(8,128)(2,1)S(1)}, u32[]{:S(2)}, u32[]{:S(2)}) collective-permute-start(bf16[4,96,768]{2,1,0:T(8,128)(2,1)S(1)} %get-tuple-element.113), channel_id=1, source_target_pairs={{0,24},{8,16},{16,8},{24,0},{1,25},{9,17},{17,9},{25,1},{2,26},{10... | collective-permute-start | bytes 1769480 | tf_op jit(solution)/shard_map/ppermute | solution.py:472
  271.1 8.8 %collective-permute-start.46 = (bf16[96,768]{1,0:T(8,128)(2,1)S(1)}, bf16[96,768]{1,0:T(8,128)(2,1)S(1)}, u32[]{:S(2)}, u32[]{:S(2)}) collective-permute-start(bf16[96,768]{1,0:T(8,128)(2,1)S(1)} %get-tuple-element.134), channel_id=1, source_target_pairs={{0,2},{1,3},{2,0},{3,1},{4,6},{5,7},{6,4},{7,5},{8,10},{9,11},{10,... | collective-permute-start | bytes 442376 | tf_op jit(solution)/shard_map/ppermute | solution.py:476
  274.0 12.3 %collective-permute-start.47 = (bf16[96,768]{1,0:T(8,128)(2,1)S(1)}, bf16[96,768]{1,0:T(8,128)(2,1)S(1)}, u32[]{:S(2)}, u32[]{:S(2)}) collective-permute-start(bf16[96,768]{1,0:T(8,128)(2,1)S(1)} %get-tuple-element.136), channel_id=1, source_target_pairs={{0,4},{1,5},{2,6},{3,7},{4,0},{5,1},{6,2},{7,3},{8,12},{9,13},{10,... | collective-permute-start | bytes 442376 | tf_op jit(solution)/shard_map/ppermute | solution.py:476
  275.6 10.7 %collective-permute-start.48 = (bf16[96,768]{1,0:T(8,128)(2,1)S(1)}, bf16[96,768]{1,0:T(8,128)(2,1)S(1)}, u32[]{:S(2)}, u32[]{:S(2)}) collective-permute-start(bf16[96,768]{1,0:T(8,128)(2,1)S(1)} %get-tuple-element.135), channel_id=1, source_target_pairs={{0,6},{1,7},{2,4},{3,5},{4,2},{5,3},{6,0},{7,1},{8,14},{9,15},{10,... | collective-permute-start | bytes 442376 | tf_op jit(solution)/shard_map/ppermute | solution.py:476
  278.2 8.2 %collective-permute-start.49 = (bf16[96,768]{1,0:T(8,128)(2,1)S(1)}, bf16[96,768]{1,0:T(8,128)(2,1)S(1)}, u32[]{:S(2)}, u32[]{:S(2)}) collective-permute-start(bf16[96,768]{1,0:T(8,128)(2,1)S(1)} %fusion.11), channel_id=1, source_target_pairs={{0,8},{8,0},{16,24},{24,16},{1,9},{9,1},{17,25},{25,17},{2,10},{10... | collective-permute-start | bytes 442376 | tf_op jit(solution)/shard_map/ppermute | solution.py:472
  278.4 7.9 %collective-permute-start.50 = (bf16[96,768]{1,0:T(8,128)(2,1)S(1)}, bf16[96,768]{1,0:T(8,128)(2,1)S(1)}, u32[]{:S(2)}, u32[]{:S(2)}) collective-permute-start(bf16[96,768]{1,0:T(8,128)(2,1)S(1)} %fusion.11), channel_id=1, source_target_pairs={{0,16},{8,24},{16,0},{24,8},{1,17},{9,25},{17,1},{25,9},{2,18},{10... | collective-permute-start | bytes 442376 | tf_op jit(solution)/shard_map/ppermute | solution.py:472
  279.9 7.0 %collective-permute-start.51 = (bf16[96,768]{1,0:T(8,128)(2,1)S(1)}, bf16[96,768]{1,0:T(8,128)(2,1)S(1)}, u32[]{:S(2)}, u32[]{:S(2)}) collective-permute-start(bf16[96,768]{1,0:T(8,128)(2,1)S(1)} %fusion.11), channel_id=1, source_target_pairs={{0,24},{8,16},{16,8},{24,0},{1,25},{9,17},{17,9},{25,1},{2,26},{10... | collective-permute-start | bytes 442376 | tf_op jit(solution)/shard_map/ppermute | solution.py:472
  286.9 5.1 %collective-permute-start.52 = (bf16[96,768]{1,0:T(8,128)(2,1)S(1)}, bf16[96,768]{1,0:T(8,128)(2,1)S(1)}, u32[]{:S(2)}, u32[]{:S(2)}) collective-permute-start(bf16[96,768]{1,0:T(8,128)(2,1)S(1)} %fusion.8), channel_id=1, source_target_pairs={{0,8},{8,0},{16,24},{24,16},{1,9},{9,1},{17,25},{25,17},{2,10},{10... | collective-permute-start | bytes 442376 | tf_op jit(solution)/shard_map/ppermute | solution.py:472
  287.0 6.9 %collective-permute-start.53 = (bf16[96,768]{1,0:T(8,128)(2,1)S(1)}, bf16[96,768]{1,0:T(8,128)(2,1)S(1)}, u32[]{:S(2)}, u32[]{:S(2)}) collective-permute-start(bf16[96,768]{1,0:T(8,128)(2,1)S(1)} %fusion.8), channel_id=1, source_target_pairs={{0,16},{8,24},{16,0},{24,8},{1,17},{9,25},{17,1},{25,9},{2,18},{10... | collective-permute-start | bytes 442376 | tf_op jit(solution)/shard_map/ppermute | solution.py:472
  289.6 7.6 %collective-permute-start.54 = (bf16[96,768]{1,0:T(8,128)(2,1)S(1)}, bf16[96,768]{1,0:T(8,128)(2,1)S(1)}, u32[]{:S(2)}, u32[]{:S(2)}) collective-permute-start(bf16[96,768]{1,0:T(8,128)(2,1)S(1)} %fusion.8), channel_id=1, source_target_pairs={{0,24},{8,16},{16,8},{24,0},{1,25},{9,17},{17,9},{25,1},{2,26},{10... | collective-permute-start | bytes 442376 | tf_op jit(solution)/shard_map/ppermute | solution.py:472
  299.3 6.7 %collective-permute-start.55 = (bf16[24,3072]{1,0:T(8,128)(2,1)S(1)}, bf16[24,3072]{1,0:T(8,128)(2,1)S(1)}, u32[]{:S(2)}, u32[]{:S(2)}) collective-permute-start(bf16[24,3072]{1,0:T(8,128)(2,1)S(1)} %get-tuple-element.127), channel_id=1, source_target_pairs={{0,8},{8,0},{16,24},{24,16},{1,9},{9,1},{17,25},{25,17},{2,10},{10... | collective-permute-start | bytes 442376 | tf_op jit(solution)/shard_map/ppermute | solution.py:472
  299.4 9.4 %collective-permute-start.56 = (bf16[24,3072]{1,0:T(8,128)(2,1)S(1)}, bf16[24,3072]{1,0:T(8,128)(2,1)S(1)}, u32[]{:S(2)}, u32[]{:S(2)}) collective-permute-start(bf16[24,3072]{1,0:T(8,128)(2,1)S(1)} %get-tuple-element.129), channel_id=1, source_target_pairs={{0,16},{8,24},{16,0},{24,8},{1,17},{9,25},{17,1},{25,9},{2,18},{10... | collective-permute-start | bytes 442376 | tf_op jit(solution)/shard_map/ppermute | solution.py:472
  300.1 8.7 %collective-permute-start.57 = (bf16[24,3072]{1,0:T(8,128)(2,1)S(1)}, bf16[24,3072]{1,0:T(8,128)(2,1)S(1)}, u32[]{:S(2)}, u32[]{:S(2)}) collective-permute-start(bf16[24,3072]{1,0:T(8,128)(2,1)S(1)} %get-tuple-element.128), channel_id=1, source_target_pairs={{0,24},{8,16},{16,8},{24,0},{1,25},{9,17},{17,9},{25,1},{2,26},{10... | collective-permute-start | bytes 442376 | tf_op jit(solution)/shard_map/ppermute | solution.py:472
  309.8 5.2 %collective-permute-start.58 = (bf16[24,3072]{1,0:T(8,128)(2,1)S(1)}, bf16[24,3072]{1,0:T(8,128)(2,1)S(1)}, u32[]{:S(2)}, u32[]{:S(2)}) collective-permute-start(bf16[24,3072]{1,0:T(8,128)(2,1)S(1)} %fusion.5), channel_id=1, source_target_pairs={{0,8},{8,0},{16,24},{24,16},{1,9},{9,1},{17,25},{25,17},{2,10},{10... | collective-permute-start | bytes 442376 | tf_op jit(solution)/shard_map/ppermute | solution.py:472
  311.6 6.7 %collective-permute-start.59 = (bf16[24,3072]{1,0:T(8,128)(2,1)S(1)}, bf16[24,3072]{1,0:T(8,128)(2,1)S(1)}, u32[]{:S(2)}, u32[]{:S(2)}) collective-permute-start(bf16[24,3072]{1,0:T(8,128)(2,1)S(1)} %fusion.5), channel_id=1, source_target_pairs={{0,16},{8,24},{16,0},{24,8},{1,17},{9,25},{17,1},{25,9},{2,18},{10... | collective-permute-start | bytes 442376 | tf_op jit(solution)/shard_map/ppermute | solution.py:472
  312.0 6.2 %collective-permute-start.60 = (bf16[24,3072]{1,0:T(8,128)(2,1)S(1)}, bf16[24,3072]{1,0:T(8,128)(2,1)S(1)}, u32[]{:S(2)}, u32[]{:S(2)}) collective-permute-start(bf16[24,3072]{1,0:T(8,128)(2,1)S(1)} %fusion.5), channel_id=1, source_target_pairs={{0,24},{8,16},{16,8},{24,0},{1,25},{9,17},{17,9},{25,1},{2,26},{10... | collective-permute-start | bytes 442376 | tf_op jit(solution)/shard_map/ppermute | solution.py:472
  (34 other events, 551.0 us)
Sparse Core Ops, SparseCore 0:
  26.9 64.9 all-gather.1
  145.6 59.2 reduce-scatter.2
  207.2 59.8 reduce-scatter.4

commit v4 on v3

v4 whole, which is shorter than its diff:
```python
import functools

import jax
import jax.numpy as jnp
import numpy as np
from jax import lax
from jax.experimental import pallas as pl
from jax.experimental.pallas import tpu as pltpu
from jax.sharding import PartitionSpec as P

H = 12
HD = 64
ROT = 16
LANES = 128
EPS = 1e-05
MASKED = -1e30
VMEM = 56 * 1024 * 1024
BF = jnp.bfloat16
F32 = jnp.float32


def dot(left, right, dims=((1,), (0,))):
    return lax.dot_general(left, right, (dims, ((), ())), preferred_element_type=F32)


def back_dot(left, right):
    return dot(left, right, ((1,), (1,)))


def outer_sum(left, right):
    return dot(left, right, ((0,), (0,)))


def normalized(values):
    center = values - jnp.mean(values, axis=-1, keepdims=True)
    spread = jnp.mean(center * center, axis=-1, keepdims=True)
    inverse = lax.rsqrt(spread + EPS)
    return center * inverse, inverse


def norm_back(hat, inverse, gain, grad):
    scaled = grad * gain
    first = jnp.mean(scaled, axis=-1, keepdims=True)
    second = jnp.mean(scaled * hat, axis=-1, keepdims=True)
    return (
        inverse * (scaled - first - hat * second),
        jnp.sum(grad * hat, axis=0, keepdims=True),
        jnp.sum(grad, axis=0, keepdims=True),
    )


def rotary_tables(length):
    half = ROT // 2
    inverse = np.float32(10000.0) ** (-np.arange(0, ROT, 2, dtype=np.float32) / np.float32(ROT))
    phase = np.arange(length, dtype=np.float32)[:, None] * inverse[None, :].astype(np.float32)
    cosine, sine = np.cos(phase), np.sin(phase)
    c = np.ones((length, HD), np.float32)
    s1 = np.zeros((length, HD), np.float32)
    s2 = np.zeros((length, HD), np.float32)
    c[:, :half] = cosine
    c[:, half:ROT] = cosine
    s1[:, :half] = -sine
    s2[:, half:ROT] = sine
    return tuple(np.concatenate([t, t], axis=1) for t in (c, s1, s2))


def turn(values, c, s1, s2):
    half = ROT // 2
    return (
        values * c
        + pltpu.roll(values, LANES - half, 1) * s1
        + pltpu.roll(values, half, 1) * s2
    )


def project_kernel(
    n, block_len, used, me, tokens, cot, vectors, c_ref, s1_ref, s2_ref, *rest
):
    own, other = rest[:2]
    columns, crossed = rest[2 : 2 + n], rest[2 + n : 2 + 2 * n]
    outs = rest[2 + 2 * n : 2 + 3 * n]
    w, normed, b, laid = rest[2 + 3 * n :]
    kind = pl.program_id(0)
    model = tokens.shape[1]
    parts = n // 4
    f = me[1]

    for part in range(parts):
        unit = kind * parts + part
        laid[f, part] = own[unit]
        laid[f ^ 1, part] = other[unit]
        for shift in range(n):

            @pl.when((unit ^ me[0]) == shift)
            def _(shift=shift, part=part):
                for index in range(columns[shift].shape[0]):
                    step = 2 * (index + 1)
                    laid[f ^ step, part] = columns[shift][index]
                    laid[f ^ step ^ 1, part] = crossed[shift][index]

    w[0] = laid[...].reshape(model, model)

    @pl.when(kind == 0)
    def _():
        hat, _inverse = normalized(tokens[...].astype(F32))
        normed[...] = (hat * vectors[0:1, :model] + vectors[1:2, :model]).astype(BF)

    for t in range(3):

        @pl.when(kind == t)
        def _(t=t):
            b[...] = vectors[4:5, t * model : (t + 1) * model]

    width = outs[0].shape[-1]
    per = w.shape[-1] // width

    def operands(shift, left):
        group = jnp.minimum(me[0] ^ shift, used - 1)
        rows = pl.multiple_of((group // per) * block_len, block_len)
        cols = pl.multiple_of((group % per) * width, LANES)
        return left[pl.ds(rows, block_len)], pl.ds(cols, width)

    @pl.when(kind < 2)
    def _():
        c, s1, s2 = c_ref[...], s1_ref[...], s2_ref[...]
        for shift in range(n):
            left, cols = operands(shift, normed)
            full = dot(left, w[0, :, cols]) + b[:, cols]
            for j in range(width // LANES):
                at = slice(j * LANES, (j + 1) * LANES)
                outs[shift][0, :, at] = turn(full[:, at], c, s1, s2).astype(BF)

    @pl.when(kind == 2)
    def _():
        for shift in range(n):
            left, cols = operands(shift, normed)
            outs[shift][0] = (dot(left, w[0, :, cols]) + b[:, cols]).astype(BF)

    @pl.when(kind == 3)
    def _():
        for shift in range(n):
            left, cols = operands(shift, cot)
            outs[shift][0] = back_dot(left, w[0, cols]).astype(BF)


def project(n, m, at, tokens, cot, vectors, pieces, tables, block_len, width, used):
    rows, model = tokens.shape
    parts = n // 4
    whole = pl.BlockSpec((rows, model), lambda kind, me_ref: (0, 0))
    own = pl.BlockSpec((block_len, LANES), lambda kind, me_ref: (me_ref[0], 0))
    return pl.pallas_call(
        functools.partial(project_kernel, n, block_len, used),
        grid_spec=pltpu.PrefetchScalarGridSpec(
            num_scalar_prefetch=1,
            grid=(4,),
            in_specs=[
                whole,
                whole,
                pl.BlockSpec(vectors.shape, lambda kind, me_ref: (0, 0)),
                own,
                own,
                own,
            ]
            + [pl.BlockSpec(p.shape, lambda kind, me_ref: (0, 0, 0)) for p in pieces],
            out_specs=[pl.BlockSpec((1, block_len, width), lambda kind, me_ref: (kind, 0, 0))] * n
            + [pl.BlockSpec((1, model, model), lambda kind, me_ref: (kind, 0, 0))],
            scratch_shapes=[
                pltpu.VMEM((rows, model), BF),
                pltpu.VMEM((1, model), F32),
                pltpu.VMEM((m, parts, model // m // parts, model), BF),
            ],
        ),
        out_shape=[jax.ShapeDtypeStruct((4, block_len, width), BF)] * n
        + [jax.ShapeDtypeStruct((4, model, model), BF)],
        compiler_params=pltpu.CompilerParams(vmem_limit_bytes=VMEM),
        cost_estimate=pl.CostEstimate(
            flops=8 * rows * model * model,
            bytes_accessed=2 * (4 * model * model + 6 * rows * model),
            transcendentals=0,
        ),
        name="project",
    )(at, tokens, cot, vectors, *(jnp.asarray(t) for t in tables), *pieces)


def attend_kernel(n, block, me, *refs):
    ins = refs[:n]
    c_ref, s1_ref, s2_ref = refs[n : n + 3]
    outs = refs[n + 3 : 2 * n + 3]
    (q_s, k_s, v_s, g_s, qt_s, kt_s, vt_s, gt_s, sc, pb, dk, dv, o_s, dq_s) = refs[2 * n + 3 :]
    two = 2 * block
    scale = HD**-0.5

    for shift in range(n):
        at = ins[shift]
        place = me[0] ^ shift
        for kind, plain, flipped in ((0, q_s, qt_s), (1, k_s, kt_s), (2, v_s, vt_s), (3, g_s, gt_s)):
            piece = at[kind].astype(F32)
            if kind == 0:
                piece = piece * scale
            plain[place] = piece.astype(BF)
            flipped[place] = piece.T.astype(BF)

    lane = lax.broadcasted_iota(jnp.int32, (block, LANES), 1) < HD
    row = lax.broadcasted_iota(jnp.int32, (LANES, block), 0) < HD
    key_at = lax.broadcasted_iota(jnp.int32, (block, two), 0)
    query_at = lax.broadcasted_iota(jnp.int32, (block, two), 1)
    query_at = jnp.where(query_at >= block, query_at - block, query_at)
    allowed = key_at <= query_at

    def beside(flipped):
        zero = jnp.zeros_like(flipped)
        return jnp.concatenate([jnp.where(row, flipped, zero), jnp.where(row, zero, flipped)], axis=1)

    def below(plain):
        zero = jnp.zeros_like(plain)
        return jnp.concatenate([jnp.where(lane, plain, zero), jnp.where(lane, zero, plain)], axis=0)

    def loop(upto, body, init):
        if isinstance(upto, int):
            for j in range(upto):
                init = body(j, init)
            return init
        return lax.fori_loop(0, upto, body, init)

    def query_block(i, _):
        queries_t = beside(qt_s[i].astype(F32)).astype(BF)
        grads_t = beside(gt_s[i].astype(F32)).astype(BF)
        queries = below(q_s[i].astype(F32)).astype(BF)
        grads = below(g_s[i].astype(F32)).astype(BF)

        def score(j, top):
            found = dot(k_s[j], queries_t)
            sc[j] = found
            return jnp.maximum(top, jnp.max(found, axis=0, keepdims=True))

        diagonal = jnp.where(allowed, dot(k_s[i], queries_t), MASKED)
        sc[i] = diagonal
        top = loop(i, score, jnp.max(diagonal, axis=0, keepdims=True))

        def weigh(j, total):
            exps = jnp.exp(sc[j] - top)
            sc[j] = exps
            return total + jnp.sum(exps, axis=0, keepdims=True)

        total = loop(i + 1, weigh, jnp.zeros((1, two), F32))
        inverse = 1.0 / total

        def mix(j, heads):
            probs = sc[j] * inverse
            sc[j] = probs
            low = probs.astype(BF)
            pb[j] = low
            return tuple(
                heads[h] + dot(vt_s[j, h * HD : (h + 1) * HD], low[:, h * block : (h + 1) * block])
                for h in range(2)
            )

        none = jnp.zeros((HD, block), F32)
        heads = loop(i + 1, mix, (none, none))
        delta = jnp.concatenate(
            [
                jnp.sum(heads[h] * gt_s[i, h * HD : (h + 1) * HD].astype(F32), axis=0, keepdims=True)
                for h in range(2)
            ],
            axis=1,
        )
        o_s[i] = jnp.concatenate(heads, axis=0).T.astype(BF)

        def back(j, found, first):
            grad_scores = (sc[j] * (dot(v_s[j], grads_t) - delta)).astype(BF)
            key_part = dot(grad_scores, queries)
            value_part = dot(pb[j], grads)
            if first:
                dk[j] = key_part
                dv[j] = value_part
            else:
                dk[j] = dk[j] + key_part
                dv[j] = dv[j] + value_part
            return tuple(
                found[h]
                + dot(kt_s[j, h * HD : (h + 1) * HD], grad_scores[:, h * block : (h + 1) * block])
                for h in range(2)
            )

        found = back(i, (none, none), True)
        found = loop(i, lambda j, kept: back(j, kept, False), found)
        grad_query = jnp.concatenate(found, axis=0).T * scale
        dq_s[i] = turn(grad_query, c_ref[i], -s1_ref[i], -s2_ref[i]).astype(BF)
        return 0

    if n <= 4:
        for i in range(n):
            query_block(i, 0)
    else:
        lax.fori_loop(0, n, query_block, 0)

    for shift in range(n):
        place = me[0] ^ shift
        c, s1, s2 = c_ref[place], -s1_ref[place], -s2_ref[place]
        outs[shift][0] = o_s[place]
        outs[shift][1] = dq_s[place]
        outs[shift][2] = turn(dk[place], c, s1, s2).astype(BF)
        outs[shift][3] = dv[place].astype(BF)


def attend(n, me, pieces, tables):
    _, block, width = pieces[0].shape
    length = n * block
    spec = pl.BlockSpec((4, block, LANES), lambda j, me_ref: (0, 0, j))
    table_spec = pl.BlockSpec((n, block, LANES), lambda j, me_ref: (0, 0, 0))
    plain = pltpu.VMEM((n, block, LANES), BF)
    flipped = pltpu.VMEM((n, LANES, block), BF)
    total = pltpu.VMEM((n, block, LANES), F32)
    work = width // HD * length * (length + block) // 2
    return pl.pallas_call(
        functools.partial(attend_kernel, n, block),
        grid_spec=pltpu.PrefetchScalarGridSpec(
            num_scalar_prefetch=1,
            grid=(width // LANES,),
            in_specs=[spec] * n + [table_spec] * 3,
            out_specs=[spec] * n,
            scratch_shapes=[
                plain, plain, plain, plain,
                flipped, flipped, flipped, flipped,
                pltpu.VMEM((n, block, 2 * block), F32),
                pltpu.VMEM((n, block, 2 * block), BF),
                total, total, plain, plain,
            ],
        ),
        out_shape=[jax.ShapeDtypeStruct((4, block, width), BF)] * n,
        compiler_params=pltpu.CompilerParams(vmem_limit_bytes=VMEM),
        cost_estimate=pl.CostEstimate(
            flops=12 * work * 4 * HD * 10, bytes_accessed=2 * 8 * length * width, transcendentals=work
        ),
        name="attend",
    )(me, *pieces, *(jnp.asarray(t).reshape(n, block, LANES) for t in tables))


def mlp_kernel(last, *refs):
    tokens, cot, vectors, w_up, b_up, w_down = refs[:6]
    model = tokens.shape[1]
    if last:
        start_out, start_grad, out, grad_in, grad_up, grad_down, grad_b, sums, normed = refs[6:]
    else:
        out, grad_in, grad_up, grad_down, grad_b, normed = refs[6:]
    step = pl.program_id(0)
    row = 7 if last else 6
    gain, bias = vectors[2:3, :model], vectors[3:4, :model]

    @pl.when(step == 0)
    def _():
        values = tokens[...].astype(F32)
        hat, _inverse = normalized(values)
        normed[...] = (hat * gain + bias).astype(BF)
        if last:
            out[...] = start_out[...]
            grad_in[...] = start_grad[...]
        else:
            out[...] = values + (vectors[5:6, :model] + vectors[8:9, :model])
            grad_in[...] = jnp.zeros_like(grad_in)

    up = w_up[...].reshape(model, -1)
    down = w_down[...].reshape(-1, model)
    hidden = dot(normed[...], up) + b_up[row : row + 1]
    share = 0.5 + 0.5 * lax.erf(hidden * (0.5**0.5))
    slope = share + hidden * (jnp.exp(-0.5 * hidden * hidden) * ((2.0 * np.pi) ** -0.5))
    active = (hidden * share).astype(BF)
    grad_hidden = (back_dot(cot[...], down) * slope).astype(BF)
    grad_b[...] = jnp.sum(grad_hidden.astype(F32), axis=0, keepdims=True)
    out[...] = out[...] + dot(active, down)
    grad_in[...] = grad_in[...] + back_dot(grad_hidden, up)
    grad_down[...] = outer_sum(active, cot[...]).astype(BF).reshape(grad_down.shape)
    grad_up[...] = outer_sum(normed[...], grad_hidden).astype(BF).reshape(grad_up.shape)

    if last:

        @pl.when(step == pl.num_programs(0) - 1)
        def _():
            hat, inverse = normalized(tokens[...].astype(F32))
            upstream = cot[...].astype(F32)
            back, grad_gain, grad_bias = norm_back(hat, inverse, gain, grad_in[...])
            grad_in[...] = upstream + back
            sums[0:1] = grad_gain
            sums[1:2] = grad_bias
            sums[2:3] = jnp.sum(upstream, axis=0, keepdims=True)
            sums[3:8] = jnp.zeros((5, sums.shape[1]), F32)


def mlp(tokens, cot, vectors, weights, start=None):
    rows, model = tokens.shape
    shards, units, shard_rows, _ = weights.shape
    half = units // 2 * model
    chunk = model // 2
    group = chunk * shards // half
    last = start is not None
    whole = pl.BlockSpec((rows, model), lambda j: (0, 0))
    line = pl.BlockSpec((1, chunk), lambda j: (0, j))
    tall = (shards, 1, shard_rows, chunk)
    flat = (group, units // 2, shard_rows, model)
    total = jax.ShapeDtypeStruct((rows, model), F32)
    grads = jax.ShapeDtypeStruct((shards, units // 2, shard_rows, model), BF)
    return pl.pallas_call(
        functools.partial(mlp_kernel, last),
        grid=(half // chunk,),
        in_specs=[
            whole,
            whole,
            pl.BlockSpec(vectors.shape, lambda j: (0, 0)),
            pl.BlockSpec(tall, lambda j: (0, j // 2, 0, j % 2)),
            pl.BlockSpec((16, chunk), lambda j: (0, j)),
            pl.BlockSpec(flat, lambda j: (j, 1, 0, 0)),
        ]
        + [whole] * (2 * last),
        out_specs=[
            whole,
            whole,
            pl.BlockSpec(tall, lambda j: (0, j // 2, 0, j % 2)),
            pl.BlockSpec(flat, lambda j: (j, 0, 0, 0)),
            line,
        ]
        + ([pl.BlockSpec((8, model), lambda j: (0, 0))] if last else []),
        out_shape=[total, total, grads, grads, jax.ShapeDtypeStruct((1, half), F32)]
        + ([jax.ShapeDtypeStruct((8, model), F32)] if last else []),
        scratch_shapes=[pltpu.VMEM((rows, model), BF)],
        compiler_params=pltpu.CompilerParams(vmem_limit_bytes=VMEM),
        cost_estimate=pl.CostEstimate(
            flops=12 * rows * model * half,
            bytes_accessed=8 * model * half + 12 * rows * model,
            transcendentals=2 * rows * half,
        ),
        name="mlp",
    )(tokens, cot, vectors, weights, vectors, weights, *(start or ()))


def finish_kernel(n, block_len, used, shards, at, *refs):
    answers = refs[:n]
    tokens, cot, vectors, base, grad_base, w, sums_two, grad_b = refs[n : n + 8]
    out, grad_out, own, other, line_own, line_other = refs[n + 8 : n + 14]
    held, normed, grads, grad_in, sums, lines = refs[n + 14 :]
    kind = pl.program_id(0)
    model = tokens.shape[1]
    width = answers[0].shape[-1]
    per = model // width

    for shift in range(n):
        group = jnp.minimum(at[0] ^ shift, used - 1)
        rows = pl.multiple_of((group // per) * block_len, block_len)
        cols = pl.multiple_of((group % per) * width, LANES)
        if used == n:
            held[pl.ds(rows, block_len), pl.ds(cols, width)] = answers[shift][0]
        else:

            @pl.when((at[0] ^ shift) < used)
            def _(rows=rows, cols=cols, shift=shift):
                held[pl.ds(rows, block_len), pl.ds(cols, width)] = answers[shift][0]

    @pl.when(kind == 0)
    def _():
        hat, _inverse = normalized(tokens[...].astype(F32))
        normed[...] = (hat * vectors[0:1, :model] + vectors[1:2, :model]).T.astype(BF)
        grad_in[...] = jnp.zeros_like(grad_in)
        out[...] = (base[...] + dot(held[...], w[0])).astype(BF)
        grads[...] = outer_sum(held[...], cot[...]).astype(BF).reshape(grads.shape)

    @pl.when(kind > 0)
    def _():
        grads[...] = dot(normed[...], held[...]).astype(BF).reshape(grads.shape)
        grad_in[...] = grad_in[...] + back_dot(held[...], w[0])
        sums[pl.ds(kind, 1)] = jnp.sum(held[...].astype(F32), axis=0, keepdims=True)

    for z in range(shards // 2):
        own[0, z] = grads[z, at[1]]
        other[0, z] = grads[z, at[1] ^ 1]

    @pl.when(kind == 3)
    def _():
        hat, inverse = normalized(tokens[...].astype(F32))
        back, grad_gain, grad_bias = norm_back(hat, inverse, vectors[0:1, :model], grad_in[...])
        grad_out[...] = (grad_base[...] + back).astype(BF)
        qkv = jnp.concatenate([sums[t : t + 1] for t in (1, 2, 3)], axis=1)
        whole = [
            grad_gain, grad_bias, sums_two[0:1], sums_two[1:2], sums_two[2:3], qkv, grad_b[0:1],
            grad_b[1:2],
        ]
        lines[...] = jnp.zeros_like(lines)
        for index, line in enumerate(whole):
            size = line.shape[1] // shards
            for f in range(shards):
                lines[f // 2, f % 2, index : index + 1, :size] = line[:, f * size : (f + 1) * size]
        for z in range(shards // 2):
            line_own[z] = lines[z, at[1]]
            line_other[z] = lines[z, at[1] ^ 1]


def finish(n, me, core, answers, tokens, cot, vectors, base, grad_base, w, sums_two, grad_b, shards, used):
    rows, model = tokens.shape
    block_len, width = answers[0].shape[1:]
    whole = pl.BlockSpec((rows, model), lambda kind, at: (0, 0))
    own_rows = model // shards

    def unit(kind, at):
        return lax.rem(kind + 3, 4)

    half = pl.BlockSpec(
        (1, shards // 2, own_rows, model), lambda kind, at: (unit(kind, at), 0, 0, 0)
    )
    half_shape = jax.ShapeDtypeStruct((4, shards // 2, own_rows, model), BF)
    half_lines = pl.BlockSpec((shards // 2, 8, model), lambda kind, at: (0, 0, 0))
    half_lines_shape = jax.ShapeDtypeStruct((shards // 2, 8, model), F32)
    return pl.pallas_call(
        functools.partial(finish_kernel, n, block_len, used, shards),
        grid_spec=pltpu.PrefetchScalarGridSpec(
            num_scalar_prefetch=1,
            grid=(4,),
            in_specs=[pl.BlockSpec((1, block_len, width), lambda kind, at: (kind, 0, 0))] * n
            + [
                whole,
                whole,
                pl.BlockSpec(vectors.shape, lambda kind, at: (0, 0)),
                whole,
                whole,
                pl.BlockSpec((1, model, model), lambda kind, at: (unit(kind, at), 0, 0)),
                pl.BlockSpec((8, model), lambda kind, at: (0, 0)),
                pl.BlockSpec(grad_b.shape, lambda kind, at: (0, 0)),
            ],
            out_specs=[whole, whole, half, half, half_lines, half_lines],
            scratch_shapes=[
                pltpu.VMEM((rows, model), BF),
                pltpu.VMEM((model, rows), BF),
                pltpu.VMEM((shards // 2, 2, own_rows, model), BF),
                pltpu.VMEM((rows, model), F32),
                pltpu.VMEM((8, model), F32),
                pltpu.VMEM((shards // 2, 2, 8, model), F32),
            ],
        ),
        out_shape=[
            jax.ShapeDtypeStruct((rows, model), BF),
            jax.ShapeDtypeStruct((rows, model), BF),
            half_shape,
            half_shape,
            half_lines_shape,
            half_lines_shape,
        ],
        compiler_params=pltpu.CompilerParams(vmem_limit_bytes=VMEM),
        cost_estimate=pl.CostEstimate(
            flops=16 * rows * model * model, bytes_accessed=40 * rows * model, transcendentals=0
        ),
        name="finish",
    )(
        jnp.stack([me, core]).astype(jnp.int32),
        *answers, tokens, cot, vectors, base, grad_base, w, sums_two, grad_b,
    )


def swap(value, shift, n):
    return lax.ppermute(value, "ctx", [(i, i ^ shift) for i in range(n)])


def swap_shard(value, shift, m):
    return lax.ppermute(value, "fsdp", [(i, i ^ shift) for i in range(m)])


def pack_kernel(*refs):
    out = refs[-1]
    rows = []
    for ref in refs[:-1]:
        line = ref[...].astype(F32)
        rows.append(jnp.concatenate([line, jnp.zeros((1, out.shape[1] - line.shape[1]), F32)], axis=1))
    rows.append(jnp.zeros((out.shape[0] - len(rows), out.shape[1]), F32))
    out[...] = jnp.concatenate(rows, axis=0).astype(BF)


def pack(vectors, width):
    return pl.pallas_call(
        pack_kernel,
        out_shape=jax.ShapeDtypeStruct((16, width), BF),
        name="pack",
    )(*[v.reshape(1, -1) for v in vectors])


def unpack_kernel(sizes, half, at, own, other, out):
    chips = own.shape[0]
    out[...] = jnp.zeros_like(out)
    rows = []
    for f in range(2 * chips):
        rel = f ^ at[0]
        both = jnp.where(rel % 2 == 0, own[rel // 2].astype(F32), other[rel // 2].astype(F32))
        rows.append(both)
    for index, size in enumerate(sizes):
        if index == half + 1:
            continue
        if index == half:
            cut = size // 2
            for h in range(2):
                line = [r[index : index + 1, h * cut : (h + 1) * cut] for r in rows]
                out[index + h : index + h + 1, : len(rows) * cut] = jnp.concatenate(line, axis=1)
        else:
            line = [r[index : index + 1, :size] for r in rows]
            out[index : index + 1, : len(rows) * size] = jnp.concatenate(line, axis=1)


def unpack(f, own, other, sizes, half):
    width = 2 * own.shape[0] * max(sizes[:half] + [sizes[half] // 2])
    full = pl.BlockSpec(own.shape, lambda i, at: (0, 0, 0))
    return pl.pallas_call(
        functools.partial(unpack_kernel, sizes, half),
        grid_spec=pltpu.PrefetchScalarGridSpec(
            num_scalar_prefetch=1,
            grid=(1,),
            in_specs=[full, full],
            out_specs=pl.BlockSpec((16, width), lambda i, at: (0, 0)),
        ),
        out_shape=jax.ShapeDtypeStruct((16, width), F32),
        name="unpack",
    )(f.astype(jnp.int32).reshape(1), own, other)


def along_z(units, m, extra=None):
    mine = pick(units, lax.axis_index("ctx"))
    rows = mine.shape[0]
    if extra is None:
        return [swap_shard(mine, step, m) for step in range(2, m, 2)]
    mine = jnp.concatenate([mine, extra], axis=0)
    came = [swap_shard(mine, step, m) for step in range(2, m, 2)]
    return jnp.stack([c[:rows] for c in came]), jnp.stack([extra] + [c[rows:] for c in came])


def between_columns(along, n):
    return [along] + [swap(along, shift, n) for shift in range(1, n)]


def assemble_kernel(where, at, *refs):
    out = refs[-1]
    for piece, index, place in where:
        unit, shard = place(at)
        out[shard, unit] = refs[piece][index]


def assemble(at, pieces, n, m):
    where = []
    for unit in range(n):
        where.append((0, unit, lambda at, unit=unit: (unit, at[1])))
        where.append((1, unit, lambda at, unit=unit: (unit, at[1] ^ 1)))
    for core in range(2):
        for shift in range(n):
            for index in range(m // 2 - 1):
                where.append(
                    (
                        2 + core * n + shift,
                        index,
                        lambda at, shift=shift, flip=2 * (index + 1) ^ core: (at[0] ^ shift, at[1] ^ flip),
                    )
                )
    full = (m, n) + pieces[0].shape[1:]
    return pl.pallas_call(
        functools.partial(assemble_kernel, where),
        grid_spec=pltpu.PrefetchScalarGridSpec(
            num_scalar_prefetch=1,
            grid=(1,),
            in_specs=[pl.BlockSpec(p.shape, lambda i, at: (0, 0, 0)) for p in pieces],
            out_specs=pl.BlockSpec(full, lambda i, at: (0, 0, 0, 0)),
        ),
        out_shape=jax.ShapeDtypeStruct(full, pieces[0].dtype),
        compiler_params=pltpu.CompilerParams(vmem_limit_bytes=VMEM),
        name="assemble",
    )(at, *pieces)


def add_up(*pieces):
    return sum(p.astype(F32) for p in pieces).astype(BF)


def pick(value, at, axis=0):
    return lax.dynamic_index_in_dim(value, at, axis, keepdims=False)


def swapped(value, n):
    return [value] + [swap(value, s, n) for s in range(1, n)]


def sum_over_ctx(shard, n):
    steps = [2**i for i in range(n.bit_length() - 1)]
    half = shard.shape[0] // 2
    halves = [shard[:half], shard[half:]]
    for i in range(len(steps)):
        for j in range(2):
            value = halves[j] if i == 0 else add_up(*halves[j])
            halves[j] = (value, swap(value, steps[(i + j) % len(steps)], n))
    return [term for half in halves for term in half]


def lay_kernel(shards, *refs):
    up, down = refs[8:]
    model = up.shape[1] // 4
    size = up.shape[1] // shards // 2
    ups = []
    for h in range(2):
        terms = refs[4 * h : 4 * h + 4]
        total = terms[0][...].astype(F32) + terms[1][...].astype(F32)
        ups.append(jnp.concatenate([total[0], total[1]], axis=1))
        rows = down.shape[0] // 4
        for unit in range(2):
            at = (2 * h + unit) * rows
            down[at : at + rows] = terms[2][unit].astype(F32) + terms[3][unit].astype(F32)
    for f in range(shards):
        line = [ups[h][:, f * size : (f + 1) * size] for h in range(2)]
        up[:, 2 * f * size : 2 * (f + 1) * size] = jnp.concatenate(line, axis=1)


def lay(first, second, shards, up_shape, down_shape):
    return pl.pallas_call(
        functools.partial(lay_kernel, shards),
        out_shape=[jax.ShapeDtypeStruct(up_shape, F32), jax.ShapeDtypeStruct(down_shape, F32)],
        compiler_params=pltpu.CompilerParams(vmem_limit_bytes=VMEM),
        name="lay",
    )(*first, *second)


def in_order(pieces, at):
    stacked = jnp.stack(pieces)
    return jnp.stack([pick(stacked, at ^ place) for place in range(len(pieces))])


def body(
    tokens,
    norm1_gain,
    norm1_bias,
    norm2_gain,
    norm2_bias,
    qkv_weight,
    qkv_bias,
    out_weight,
    out_bias,
    up_weight,
    up_bias,
    down_weight,
    down_bias,
    cotangent,
):
    block_len, seq_count, model = tokens.shape
    n = lax.axis_size("ctx")
    shards = lax.axis_size("fsdp")
    rows = block_len * seq_count
    hidden = up_weight.shape[1]
    me = lax.axis_index("ctx")
    me_arr = me.astype(jnp.int32).reshape(1)
    width = -(-seq_count * model // (n * LANES)) * LANES
    used = seq_count * model // width
    per = model // width

    parts = n // 4
    own_rows = out_weight.shape[0]

    vectors = (
        norm1_gain, norm1_bias, norm2_gain, norm2_bias, qkv_bias, out_bias, up_bias, out_bias,
        down_bias,
    )
    sizes = [v.shape[0] for v in vectors]
    packed = pack(vectors, model)

    per_shard = hidden // shards // 2

    def half_weights(h):
        up = up_weight.reshape(own_rows, shards, 2, per_shard)[:, :, h].reshape(own_rows, -1, model)
        down = down_weight[h * per_shard : (h + 1) * per_shard].reshape(-1, own_rows, model)
        return jnp.concatenate([up.transpose(1, 0, 2), down], axis=0)

    units = jnp.concatenate(
        [qkv_weight[None, :, t * model : (t + 1) * model] for t in range(3)] + [out_weight[None]]
    ).reshape(n, own_rows // parts, model)
    along_units, chips = along_z(units, shards, packed)
    first_half, second_half, _ = lax.optimization_barrier(
        (half_weights(0), half_weights(1), along_units)
    )
    w_first = lax.all_gather(first_half, "fsdp", axis=0, tiled=False)
    unit_columns = between_columns(along_units, n)
    vectors = unpack(
        lax.axis_index("fsdp"), chips, swap_shard(chips, 1, shards), sizes, 6
    )
    vectors, unit_columns = lax.optimization_barrier((vectors, unit_columns))
    crossed = [swap_shard(held, 1, shards) for held in unit_columns]
    unit_pieces = [units, swap_shard(units, 1, shards)] + unit_columns + crossed

    inputs = tokens.transpose(1, 0, 2).reshape(rows, model)
    cot = cotangent.transpose(1, 0, 2).reshape(rows, model)

    tables = rotary_tables(n * block_len)
    def shard_sum(value):
        return lax.psum_scatter(value, "fsdp", scatter_dimension=0, tiled=False)

    at = jnp.stack([me, lax.axis_index("fsdp")]).astype(jnp.int32)
    *sent, w_units = project(
        n, shards, at, inputs, cot, vectors, unit_pieces, tables, block_len, width, used
    )
    pieces = [sent[0]] + [swap(sent[shift], shift, n) for shift in range(1, n)]
    mlp_inputs, second_half, _ = lax.optimization_barrier((inputs, second_half, (sent, w_first)))
    second_units = second_half.reshape(n, -1, model)
    along_second = along_z(second_units, shards)
    base, grad_base, grad_up, grad_down, grad_b_first = mlp(
        mlp_inputs, cot, vectors, w_first
    )
    first_grads, pieces = lax.optimization_barrier(
        (jnp.concatenate([grad_up, grad_down], axis=1), pieces)
    )
    first_shard = shard_sum(first_grads)
    along_second, _ = lax.optimization_barrier((along_second, pieces))
    second_columns = between_columns(jnp.stack(along_second), n)
    made = attend(n, me_arr, pieces, tables)
    mlp_inputs, second_columns, second_units, _ = lax.optimization_barrier(
        (inputs, second_columns, second_units, made)
    )
    second_pieces = [second_units, swap_shard(second_units, 1, shards)] + second_columns
    second_pieces += [swap_shard(held, 1, shards) for held in second_columns]
    w_second = assemble(at, second_pieces, n, shards).reshape(shards, 4, own_rows, model)
    answers = [made[0]] + [swap(made[shift], shift, n) for shift in range(1, n)]
    base, grad_base, grad_up, grad_down, grad_b_second, sums_two = mlp(
        mlp_inputs, cot, vectors, w_second, start=(base, grad_base)
    )
    second_grads, answers = lax.optimization_barrier(
        (jnp.concatenate([grad_up, grad_down], axis=1), answers)
    )
    second_shard = shard_sum(second_grads)
    core = lax.axis_index("fsdp") % 2
    layer_out, tokens_grad, own, other, line_own, line_other = finish(
        n, me, core, answers, inputs, cot, vectors, base, grad_base, w_units, sums_two,
        jnp.concatenate([grad_b_first, grad_b_second]), shards, used,
    )

    def placed(value):
        return value.reshape(seq_count, block_len, model).transpose(1, 0, 2)

    z = lax.axis_index("fsdp") // 2
    chip = add_up(own, swap_shard(other, 1, shards))
    line_chip = add_up(line_own, swap_shard(line_other, 1, shards))
    chip = jnp.concatenate([chip, jnp.pad(line_chip[None], ((0, 3), (0, 0), (0, 0), (0, 0)))], axis=2)
    chip = (
        chip.reshape(4, shards // 2, parts, -1, model)
        .transpose(0, 2, 1, 3, 4)
        .reshape(n, shards // 2, -1, model)
    )
    unit = add_up(pick(chip, me), *[swap(pick(chip, me ^ s), s, n) for s in range(1, n)])
    unit, first_shard, second_shard = lax.optimization_barrier((unit, first_shard, second_shard))
    first_sum, second_sum = sum_over_ctx(first_shard, n), sum_over_ctx(second_shard, n)
    mine = add_up(
        pick(unit, z),
        *[swap_shard(pick(unit, z ^ s), 2 * s, shards) for s in range(1, shards // 2)],
    )
    unit_all = swapped(mine, n)
    part_units = in_order(unit_all, me).reshape(4, -1, model).astype(F32)
    line_sums = part_units[0, own_rows:]
    part_units = part_units[:, :own_rows]
    part_qkv = jnp.concatenate([part_units[t] for t in range(3)], axis=1)
    part_up, part_down = lay(first_sum, second_sum, shards, up_weight.shape, down_weight.shape)
    sizes = [own_rows] * 5 + [3 * own_rows, per_shard, per_shard]
    gain1, bias1, gain2, bias2, columns, qkv_b, *up_b = [
        line_sums[index, :size] for index, size in enumerate(sizes)
    ]
    return (
        placed(layer_out), placed(tokens_grad), gain1, bias1, gain2, bias2, part_qkv, qkv_b,
        part_units[3], columns, part_up, jnp.concatenate(up_b), part_down, columns,
    )


def solution(mesh):
    blocks = P("ctx", "fsdp", None)
    line, matrix = P("fsdp"), P("fsdp", None)
    return jax.shard_map(
        body,
        mesh=mesh,
        in_specs=(
            blocks, line, line, line, line, matrix, line, matrix, line, matrix, line, matrix, line,
            blocks,
        ),
        out_specs=(
            blocks, blocks, line, line, line, line, matrix, line, matrix, line, matrix, line,
            matrix, line,
        ),
        check_vma=False,
    )
```

time: 327 us -> 299 us (0.914); the launches traced: 327 us -> 293 us
  waiting for transfers between devices: 127 us -> 87.6 us
  starting transfers between devices: 71.2 us -> 46.5 us
  other arithmetic: 12.4 us -> 23.1 us
  local copies, waits for them, and re-layouts: 19.9 us -> 30.1 us
  Pallas kernels: 81.3 us -> 90.8 us
    ppermute x28 -> x22, waiting for transfers between devices: 50.9 us -> 22.8 us  [swap_shard(): return lax.ppermute(value, 'fsdp', [(i, i ^ shift) for i in range(m)])]
    ppermute x33 -> x26, waiting for transfers between devices: 74.7 us -> 55.7 us  [swap(): return lax.ppermute(value, 'ctx', [(i, i ^ shift) for i in range(n)])]
    ppermute x28 -> x22, starting transfers between devices: 32 us -> 16.6 us  [swap_shard(): return lax.ppermute(value, 'fsdp', [(i, i ^ shift) for i in range(m)])]
    concatenate x0 -> x8, other arithmetic: none -> 13.5 us  [the longest x2 10 us: body(): jnp.concatenate([grad_up, grad_down], axis=1)]
    ppermute x33 -> x26, starting transfers between devices: 38.9 us -> 29.4 us  [swap(): return lax.ppermute(value, 'ctx', [(i, i ^ shift) for i in range(n)])]
    all_gather x1, waiting for transfers between devices: 0.01 us -> 8.98 us  [body(): w_first = lax.all_gather(first_half, 'fsdp', axis=0, tiled=False)]
    pallas_call x3 -> x6, Pallas kernels: 37.4 us -> 43.8 us  [the longest x2 31.6 us: mlp(): pl.pallas_call(functools.partial(mlp_kernel, last), grid=(half // chunk,)...]
    slice x3 -> x6, local copies, waits for them, and re-layouts: 0.02 us -> 5.03 us  [the longest x1 3.26 us: half_weights(): up_weight.reshape(own_rows, shards, 2, per_shard)[:, :, h]]
  transfers between devices with their start and end apart: 64 -> 51, of which waited for: 29 -> 22; matrix products, arithmetic and copies ran while one was open for 8% -> 13% of each run, Pallas kernels for 25% -> 29%
where the time goes in v4:
time: 299 us; the launch traced here: 293 us
  Pallas kernels  90.8 us (30%)
  waiting for transfers between devices  87.6 us (29%)
  starting transfers between devices  46.5 us (16%)
  local copies, waits for them, and re-layouts  30.1 us (10%)
  other arithmetic  23.1 us (8%)
  between operations  14.9 us (5%)
    ppermute x26, waiting for transfers between devices, swap(): return lax.ppermute(value, 'ctx', [(i, i ^ shift) for i in range(n)])  55.7 us
    pallas_call x2, Pallas kernels, mlp(): pl.pallas_call(functools.partial(mlp_kernel, last), grid=(half // chunk,)...  31.6 us
    ppermute x26, starting transfers between devices, swap(): return lax.ppermute(value, 'ctx', [(i, i ^ shift) for i in range(n)])  29.4 us
    ppermute x22, waiting for transfers between devices, swap_shard(): return lax.ppermute(value, 'fsdp', [(i, i ^ shift) for i in range(m)])  22.8 us
    pallas_call x1, Pallas kernels, attend(): pl.pallas_call(functools.partial(attend_kernel, n, block), grid_spec=pltp...  21.6 us
    ppermute x22, starting transfers between devices, swap_shard(): return lax.ppermute(value, 'fsdp', [(i, i ^ shift) for i in range(m)])  16.6 us
    pallas_call x1, Pallas kernels, finish(): pl.pallas_call(functools.partial(finish_kernel, n, block_len, used, shard...  14.3 us
    pallas_call x1, Pallas kernels, project(): pl.pallas_call(functools.partial(project_kernel, n, block_len, used), gri...  11.2 us
  transfers between devices with their start and end apart: 51, of which 22 were waited for; matrix products, arithmetic and copies ran while one was open for 13% of the time, Pallas kernels for 29%

profile of v4, /device:TPU:0, one launch (start us, length us, event | category | flops | bytes accessed | tf_op | source)
XLA Modules:
  0.0 293.0 jit_solution(1029081385500750312)
XLA Ops:
  7.3 1.3 reshape.98.refs_4_
  8.6 1.2 reshape.100.refs_6_
  9.8 1.1 slice_bitcast_fusion.5
  10.9 1.0 pad_maximum_fusion.6.rest_0_
  11.9 1.6 pack.1
  13.5 1.4 pad_maximum_fusion.9
  15.0 5.0 %collective-permute-start.2 = (bf16[112,768]{1,0:T(8,128)(2,1)}, bf16[112,768]{1,0:T(8,128)(2,1)S(1)}, u32[]{:S(2)}, u32[]{:S(2)}) collective-permute-start(bf16[112,768]{1,0:T(8,128)(2,1)} %pad_maximum_fusion.9), channel_id=1, source_target_pairs={{0,6},{1,7},{2,4},{3,5},{4,2},{5,3},{6,0},{7,1},{8,14},{9,15},{10,... | collective-permute-start | bytes 516104 | tf_op jit(solution)/shard_map/ppermute | solution.py:560
  21.6 3.3 %slice_reduce_fusion = (bf16[96,8,192]{2,1,0:T(8,128)(2,1)S(1)}, bf16[96,8,192]{2,1,0:T(8,128)(2,1)S(1)}) fusion(bf16[96,8,2,192]{3,2,1,0:T(2,128)(2,1)S(1)} %reshape.91), kind=kLoop, calls=%fused_computation.11 | loop fusion | bytes 1179648 | tf_op jit(solution)/shard_map/slice | solution.py:764
  26.9 8.0 %collective-permute-done.1 = bf16[112,768]{1,0:T(8,128)(2,1)} collective-permute-done((bf16[112,768]{1,0:T(8,128)(2,1)}, bf16[112,768]{1,0:T(8,128)(2,1)}, u32[]{:S(2)}, u32[]{:S(2)}) %collective-permute-start.1) | collective-permute-done | bytes 172064 | tf_op jit(solution)/shard_map/ppermute | solution.py:560
  38.1 2.5 collective-permute-start.6
  43.2 1.3 collective-permute-done.3.other
  45.1 1.8 unpack.1.vectors.refs_2_.refs_4_.refs_6_
  46.9 5.2 %collective-permute-done.6.rest_5_ = bf16[3,96,768]{2,1,0:T(8,128)(2,1)} collective-permute-done((bf16[3,96,768]{2,1,0:T(8,128)(2,1)S(1)}, bf16[3,96,768]{2,1,0:T(8,128)(2,1)}, u32[]{:S(2)}, u32[]{:S(2)}) %collective-permute-start.6) | collective-permute-done | bytes 442400 | tf_op jit(solution)/shard_map/ppermute | solution.py:556
  52.1 9.0 %collective-permute-done.5.rest_4_ = bf16[3,96,768]{2,1,0:T(8,128)(2,1)} collective-permute-done((bf16[3,96,768]{2,1,0:T(8,128)(2,1)S(1)}, bf16[3,96,768]{2,1,0:T(8,128)(2,1)}, u32[]{:S(2)}, u32[]{:S(2)}) %collective-permute-start.5) | collective-permute-done | bytes 442400 | tf_op jit(solution)/shard_map/ppermute | solution.py:556
  62.3 1.0 copy.52
  63.2 1.0 copy.57
  66.1 11.2 %project.1 = (bf16[4,256,384]{2,1,0:T(8,128)(2,1)}, bf16[4,256,384]{2,1,0:T(8,128)(2,1)}, bf16[4,256,384]{2,1,0:T(8,128)(2,1)}, bf16[4,256,384]{2,1,0:T(8,128)(2,1)}, bf16[4,768,768]{2,1,0:T(8,128)(2,1)}) custom-call(s32[2]{0:T(128)} %pad_add_fusion.1.me.at, bf16[512,768]{1,0:T(8,128)(2,1)} %bitcast.111, bf16[512,768]{1,0:T(8,128)(2,1)} %bitcast.115, ...), custom_call_target="tpu_custom_call" | custom-call | flops 2415919104 | bytes 9437184 | tf_op jit(solution)/shard_map/project/pallas_call | solution.py:151
  77.3 1.5 collective-permute-start.15
  79.5 1.2 collective-permute-start.17
  80.8 9.0 %all-gather.3.cloned.1.call-done = bf16[32,96,768]{2,1,0:T(8,128)(2,1)} async-done(((bf16[4,96,768]{2,1,0:T(8,128)(2,1)}), bf16[32,96,768]{2,1,0:T(8,128)(2,1)}) %all-gather.3.cloned.1.call-update) | async-done | bytes 4718608 | tf_op jit(solution)/shard_map/all_gather | solution.py:775
  91.2 13.9 %mlp.2 = (f32[512,768]{1,0:T(8,128)}, f32[512,768]{1,0:T(8,128)}, bf16[8,2,96,768]{3,2,1,0:T(8,128)(2,1)}, bf16[8,2,96,768]{3,2,1,0:T(8,128)(2,1)}, f32[1,1536]{1,0:T(1,128)}) custom-call(bf16[512,768]{1,0:T(8,128)(2,1)} %bitcast.112, bf16[512,768]{1,0:T(8,128)(2,1)} %bitcast.116, f32[16,2304]{1,0:T(8,128)} %unpack.1.vectors.refs_2_.refs_4_.refs_6_, ...), custom_call_target="tpu_custom_call" | custom-call | flops 7247757312 | bytes 14155776 | tf_op jit(solution)/shard_map/mlp/pallas_call | solution.py:402
  105.2 3.0 %collective-permute-start.12 = (bf16[96,768]{1,0:T(8,128)(2,1)S(1)}, bf16[96,768]{1,0:T(8,128)(2,1)S(1)}, u32[]{:S(2)}, u32[]{:S(2)}) collective-permute-start(bf16[96,768]{1,0:T(8,128)(2,1)S(1)} %dynamic-slice_bitcast_fusion.6), channel_id=1, source_target_pairs={{0,2},{1,3},{2,0},{3,1},{4,6},{5,7},{6,4},{7,5},{8,10},{9,11},{10,... | collective-permute-start | bytes 442376 | tf_op jit(solution)/shard_map/ppermute | solution.py:560
  108.2 5.0 %pad_maximum_fusion = bf16[8,4,96,768]{3,2,1,0:T(8,128)(2,1)} fusion(bf16[8,2,96,768]{3,2,1,0:T(8,128)(2,1)} %get-tuple-element.87, bf16[8,2,96,768]{3,2,1,0:T(8,128)(2,1)} %get-tuple-element.86), kind=kLoop, calls=%fused_computation.2 | loop fusion | flops 2359296 | bytes 9437184 | tf_op jit(solution)/shard_map/concatenate | solution.py:803
  113.3 1.8 collective-permute-done.16.refs_2_
  116.5 1.5 collective-permute-start.20
  118.3 1.7 collective-permute-start.18
  120.1 21.6 %attend.1 = (bf16[4,256,384]{2,1,0:T(8,128)(2,1)}, bf16[4,256,384]{2,1,0:T(8,128)(2,1)}, bf16[4,256,384]{2,1,0:T(8,128)(2,1)}, bf16[4,256,384]{2,1,0:T(8,128)(2,1)}) custom-call(s32[1]{0:T(128)} %bitcast.me, bf16[4,256,384]{2,1,0:T(8,128)(2,1)} %get-tuple-element.88.refs_0_, bf16[4,256,384]{2,1,0:T(8,128)(2,1)} %copy-done.35, ...), custom_call_target="tpu_custom_call" | custom-call | flops 120795955200 | bytes 6291456 | tf_op jit(solution)/shard_map/attend/pallas_call | solution.py:315
  142.9 1.6 collective-permute-done.22.refs_6_
  145.2 1.4 collective-permute-start.27
  146.5 1.5 collective-permute-start.28
  149.6 5.5 %assemble.1.refs_3_.refs_5_ = bf16[8,4,96,768]{3,2,1,0:T(8,128)(2,1)} custom-call(s32[2]{0:T(128)} %pad_add_fusion.1.me.at, bf16[4,96,768]{2,1,0:T(8,128)(2,1)} %copy-done, bf16[4,96,768]{2,1,0:T(8,128)(2,1)} %copy-done.12, bf16[3,96,768]{2,1,0:T(8,128)(2,1)} %copy-done.3, bf16[3,96,768]{2,1,0:T(8,128)(2,1)} %copy-done.18, bf16[3,96,768]{2,1,0:T(8,128)(2,1)} %copy-done.17, ...), custom_call_target="tpu_custom_call" | custom-call | tf_op jit(solution)/shard_map/assemble/pallas_call | solution.py:655
  155.1 17.7 %mlp.3 = (f32[512,768]{1,0:T(8,128)}, f32[512,768]{1,0:T(8,128)}, bf16[8,2,96,768]{3,2,1,0:T(8,128)(2,1)}, bf16[8,2,96,768]{3,2,1,0:T(8,128)(2,1)}, f32[1,1536]{1,0:T(1,128)}, /*index=5*/f32[8,768]{1,0:T(8,128)}) custom-call(bf16[512,768]{1,0:T(8,128)(2,1)} %bitcast.113, bf16[512,768]{1,0:T(8,128)(2,1)} %bitcast.117, ...), custom_call_target="tpu_custom_call" | custom-call | flops 7247757312 | bytes 14155776 | tf_op jit(solution)/shard_map/mlp/pallas_call | solution.py:402
  172.8 5.0 %pad_maximum_fusion.1 = bf16[8,4,96,768]{3,2,1,0:T(8,128)(2,1)} fusion(bf16[8,2,96,768]{3,2,1,0:T(8,128)(2,1)} %get-tuple-element.108, bf16[8,2,96,768]{3,2,1,0:T(8,128)(2,1)} %get-tuple-element.107), kind=kLoop, calls=%fused_computation.3 | loop fusion | flops 2359296 | bytes 9437184 | tf_op jit(solution)/shard_map/concatenate | solution.py:820
  177.8 4.0 %collective-permute-done.27.refs_2_ = bf16[4,256,384]{2,1,0:T(8,128)(2,1)S(1)} collective-permute-done((bf16[4,256,384]{2,1,0:T(8,128)(2,1)}, bf16[4,256,384]{2,1,0:T(8,128)(2,1)S(1)}, u32[]{:S(2)}, u32[]{:S(2)}) %collective-permute-start.27) | collective-permute-done | bytes 786464 | tf_op jit(solution)/shard_map/ppermute | solution.py:556
  184.1 14.3 %finish.1 = (bf16[512,768]{1,0:T(8,128)(2,1)}, bf16[512,768]{1,0:T(8,128)(2,1)}, bf16[4,4,96,768]{3,2,1,0:T(8,128)(2,1)}, bf16[4,4,96,768]{3,2,1,0:T(8,128)(2,1)...) custom-call(s32[2]{0:T(128)} %pad_add_fusion.at, bf16[4,256,384]{2,1,0:T(8,128)(2,1)} %get-tuple-element.109.refs_0_, ...), custom_call_target="tpu_custom_call" | custom-call | flops 4831838208 | bytes 15728640 | tf_op jit(solution)/shard_map/finish/pallas_call | solution.py:510
  199.1 4.5 %collective-permute-done.30 = f32[4,8,768]{2,1,0:T(8,128)S(1)} collective-permute-done((f32[4,8,768]{2,1,0:T(8,128)}, f32[4,8,768]{2,1,0:T(8,128)S(1)}, u32[]{:S(2)}, u32[]{:S(2)}) %collective-permute-start.30) | collective-permute-done | bytes 98336 | tf_op jit(solution)/shard_map/ppermute | solution.py:560
  204.5 2.4 add_convert_fusion
  207.1 1.3 dynamic-slice_bitcast_fusion.2
  208.4 1.0 collective-permute-start.31
  209.4 1.4 collective-permute-start.33
  210.8 1.1 collective-permute-start.32
  211.9 3.9 %copy_bitcast_fusion = (bf16[256,2,768]{2,1,0:T(2,128)(2,1)}, bf16[256,2,768]{2,1,0:T(2,128)(2,1)}) fusion(bf16[2,256,768]{2,1,0:T(8,128)(2,1)} %bitcast.120, bf16[2,256,768]{2,1,0:T(8,128)(2,1)S(1)} %bitcast.119), kind=kLoop, calls=%fused_computation.13 | loop fusion | bytes 3145728 | tf_op jit(solution)/shard_map/transpose | solution.py:830
  215.8 10.1 %collective-permute-done.31 = bf16[4,104,768]{2,1,0:T(8,128)(2,1)} collective-permute-done((bf16[4,104,768]{2,1,0:T(8,128)(2,1)}, bf16[4,104,768]{2,1,0:T(8,128)(2,1)}, u32[]{:S(2)}, u32[]{:S(2)}) %collective-permute-start.31) | collective-permute-done | bytes 639008 | tf_op jit(solution)/shard_map/ppermute | solution.py:556
  225.9 13.4 %collective-permute-done.33 = bf16[4,104,768]{2,1,0:T(8,128)(2,1)} collective-permute-done((bf16[4,104,768]{2,1,0:T(8,128)(2,1)}, bf16[4,104,768]{2,1,0:T(8,128)(2,1)}, u32[]{:S(2)}, u32[]{:S(2)}) %collective-permute-start.33) | collective-permute-done | bytes 639008 | tf_op jit(solution)/shard_map/ppermute | solution.py:556
  239.3 1.4 collective-permute-done.32
  240.6 1.8 fusion.4
  242.6 2.1 collective-permute-start.36
  244.7 1.4 collective-permute-start.35
  246.1 1.1 fusion.10
  247.2 1.3 collective-permute-start.42
  249.4 1.2 collective-permute-start.46
  250.6 1.4 collective-permute-done.36
  252.0 1.0 collective-permute-start.44
  253.0 4.9 %collective-permute-done.35 = bf16[104,768]{1,0:T(8,128)(2,1)S(1)} collective-permute-done((bf16[104,768]{1,0:T(8,128)(2,1)S(1)}, bf16[104,768]{1,0:T(8,128)(2,1)S(1)}, u32[]{:S(2)}, u32[]{:S(2)}) %collective-permute-start.35) | collective-permute-done | bytes 159776 | tf_op jit(solution)/shard_map/ppermute | solution.py:560
  258.0 1.6 collective-permute-start.39
  260.5 1.2 collective-permute-start.37
  262.8 1.2 collective-permute-start.41
  264.2 1.9 collective-permute-done.39
  266.7 1.5 collective-permute-done.38
  268.2 1.6 collective-permute-start.45
  272.8 1.0 pad_maximum_fusion.2
  273.8 2.6 collective-permute-done.43.refs_3_
  276.4 4.4 %collective-permute-done.47.refs_7_ = bf16[2,96,768]{2,1,0:T(8,128)(2,1)S(1)} collective-permute-done((bf16[2,96,768]{2,1,0:T(8,128)(2,1)S(1)}, bf16[2,96,768]{2,1,0:T(8,128)(2,1)S(1)}, u32[]{:S(2)}, u32[]{:S(2)}) %collective-permute-start.47) | collective-permute-done | bytes 294944 | tf_op jit(solution)/shard_map/ppermute | solution.py:556
  282.2 3.3 %lay.1 = (f32[96,3072]{1,0:T(8,128)}, f32[384,768]{1,0:T(8,128)}) custom-call(bf16[2,96,768]{2,1,0:T(8,128)(2,1)} %copy-done.5, bf16[2,96,768]{2,1,0:T(8,128)(2,1)} %copy-done.25, bf16[2,96,768]{2,1,0:T(8,128)(2,1)} %copy-done.4, bf16[2,96,768]{2,1,0:T(8,128)(2,1)} %copy-done.24, bf16[2,96,768]{2,1,0:T(8,128)(2,1)} %copy-done.7, ...), custom_call_target="tpu_custom_call" | custom-call | tf_op jit(solution)/shard_map/lay/pallas_call | solution.py:711
  (191 shorter events, 33.2 us)
Async XLA Ops:
  7.2 13.4 %copy-start.13 = (bf16[384,768]{1,0:T(8,128)(2,1)S(1)}, bf16[384,768]{1,0:T(8,128)(2,1)}, u32[]{:S(2)}) copy-start(bf16[384,768]{1,0:T(8,128)(2,1)} %param.28) | copy-start | bytes 1769476
  7.2 13.4 %copy-start.14 = (bf16[96,3072]{1,0:T(8,128)(2,1)S(1)}, bf16[96,3072]{1,0:T(8,128)(2,1)}, u32[]{:S(2)}) copy-start(bf16[96,3072]{1,0:T(8,128)(2,1)} %param.26) | copy-start | bytes 1769476
  7.2 82.5 %all-gather.3.cloned.1.call-start = ((), (), s32[]{:S(2)}) async-start(), calls=%async_computation.4 | async-start | bytes 5308416 | tf_op jit(solution)/shard_map/all_gather | solution.py:775
  11.9 26.1 %copy-start.8 = (bf16[4,96,768]{2,1,0:T(8,128)(2,1)}, bf16[4,96,768]{2,1,0:T(8,128)(2,1)S(1)}, u32[]{:S(2)}) copy-start(bf16[4,96,768]{2,1,0:T(8,128)(2,1)S(1)} %pad_maximum_fusion.6.rest_0_) | copy-start | bytes 1769476
  15.0 11.9 %collective-permute-start.2 = (bf16[112,768]{1,0:T(8,128)(2,1)}, bf16[112,768]{1,0:T(8,128)(2,1)S(1)}, u32[]{:S(2)}, u32[]{:S(2)}) collective-permute-start(bf16[112,768]{1,0:T(8,128)(2,1)} %pad_maximum_fusion.9), channel_id=1, source_target_pairs={{0,6},{1,7},{2,4},{3,5},{4,2},{5,3},{6,0},{7,1},{8,14},{9,15},{10,... | collective-permute-start | bytes 516104 | tf_op jit(solution)/shard_map/ppermute | solution.py:560
  20.0 14.9 %collective-permute-start.1 = (bf16[112,768]{1,0:T(8,128)(2,1)}, bf16[112,768]{1,0:T(8,128)(2,1)}, u32[]{:S(2)}, u32[]{:S(2)}) collective-permute-start(bf16[112,768]{1,0:T(8,128)(2,1)} %pad_maximum_fusion.9), channel_id=1, source_target_pairs={{0,4},{1,5},{2,6},{3,7},{4,0},{5,1},{6,2},{7,3},{8,12},{9,13},{10,... | collective-permute-start | bytes 516104 | tf_op jit(solution)/shard_map/ppermute | solution.py:560
  20.0 15.8 %collective-permute-start = (bf16[112,768]{1,0:T(8,128)(2,1)}, bf16[112,768]{1,0:T(8,128)(2,1)}, u32[]{:S(2)}, u32[]{:S(2)}) collective-permute-start(bf16[112,768]{1,0:T(8,128)(2,1)} %pad_maximum_fusion.9), channel_id=1, source_target_pairs={{0,2},{1,3},{2,0},{3,1},{4,6},{5,7},{6,4},{7,5},{8,10},{9,11},{10,... | collective-permute-start | bytes 516104 | tf_op jit(solution)/shard_map/ppermute | solution.py:560
  25.4 116.3 %copy-start = (bf16[4,96,768]{2,1,0:T(8,128)(2,1)}, bf16[4,96,768]{2,1,0:T(8,128)(2,1)S(1)}, u32[]{:S(2)}) copy-start(bf16[4,96,768]{2,1,0:T(8,128)(2,1)S(1)} %pad_maximum_fusion.5.refs_0_) | copy-start | bytes 1769476
  26.3 16.9 %copy-start.28 = (bf16[16,768]{1,0:T(8,128)(2,1)S(1)}, bf16[16,768]{1,0:T(8,128)(2,1)}, u32[]{:S(2)}) copy-start(bf16[16,768]{1,0:T(8,128)(2,1)} %pack.1) | copy-start | bytes 73732
  26.9 35.4 %copy-start.9 = (bf16[256,2,768]{2,1,0:T(2,128)(2,1)S(1)}, bf16[256,2,768]{2,1,0:T(2,128)(2,1)}, u32[]{:S(2)}) copy-start(bf16[256,2,768]{2,1,0:T(2,128)(2,1)} %param.17) | copy-start | bytes 2359300
  36.8 26.4 %copy-start.10 = (bf16[256,2,768]{2,1,0:T(2,128)(2,1)S(1)}, bf16[256,2,768]{2,1,0:T(2,128)(2,1)}, u32[]{:S(2)}) copy-start(bf16[256,2,768]{2,1,0:T(2,128)(2,1)} %param.30) | copy-start | bytes 2359300
  36.8 27.3 %copy-start.15 = (bf16[3,96,768]{2,1,0:T(8,128)(2,1)}, bf16[3,96,768]{2,1,0:T(8,128)(2,1)S(1)}, u32[]{:S(2)}) copy-start(bf16[3,96,768]{2,1,0:T(8,128)(2,1)S(1)} %pad_maximum_fusion.7.rest_2_) | copy-start | bytes 1327108
  37.8 204.7 %reduce-scatter.3.cloned.1.call-start = ((), (), s32[]{:S(2)}) async-start(), calls=%async_computation.2 | async-start | bytes 5308416 | tf_op jit(solution)/shard_map/reduce_scatter | solution.py:789
  38.0 26.8 %collective-permute-start.7 = (bf16[4,96,768]{2,1,0:T(8,128)(2,1)S(1)}, bf16[4,96,768]{2,1,0:T(8,128)(2,1)}, u32[]{:S(2)}, u32[]{:S(2)}) collective-permute-start(bf16[4,96,768]{2,1,0:T(8,128)(2,1)S(1)} %pad_maximum_fusion.6.rest_0_), channel_id=1, source_target_pairs={{0,1},{1,0},{2,3},{3,2},{4,5},{5,4},{6,7},{7,6},{8,9},{9,8},{10,11... | collective-permute-start | bytes 1769480 | tf_op jit(solution)/shard_map/ppermute | solution.py:560
  38.1 14.1 %collective-permute-start.6 = (bf16[3,96,768]{2,1,0:T(8,128)(2,1)S(1)}, bf16[3,96,768]{2,1,0:T(8,128)(2,1)}, u32[]{:S(2)}, u32[]{:S(2)}) collective-permute-start(bf16[3,96,768]{2,1,0:T(8,128)(2,1)S(1)} %pad_maximum_fusion.7.rest_2_), channel_id=1, source_target_pairs={{0,24},{8,16},{16,8},{24,0},{1,25},{9,17},{17,9},{25,1},{2,26},{10... | collective-permute-start | bytes 1327112 | tf_op jit(solution)/shard_map/ppermute | solution.py:556
  40.6 20.6 %collective-permute-start.5 = (bf16[3,96,768]{2,1,0:T(8,128)(2,1)S(1)}, bf16[3,96,768]{2,1,0:T(8,128)(2,1)}, u32[]{:S(2)}, u32[]{:S(2)}) collective-permute-start(bf16[3,96,768]{2,1,0:T(8,128)(2,1)S(1)} %pad_maximum_fusion.7.rest_2_), channel_id=1, source_target_pairs={{0,16},{8,24},{16,0},{24,8},{1,17},{9,25},{17,1},{25,9},{2,18},{10... | collective-permute-start | bytes 1327112 | tf_op jit(solution)/shard_map/ppermute | solution.py:556
  41.1 20.1 %collective-permute-start.4 = (bf16[3,96,768]{2,1,0:T(8,128)(2,1)S(1)}, bf16[3,96,768]{2,1,0:T(8,128)(2,1)}, u32[]{:S(2)}, u32[]{:S(2)}) collective-permute-start(bf16[3,96,768]{2,1,0:T(8,128)(2,1)S(1)} %pad_maximum_fusion.7.rest_2_), channel_id=1, source_target_pairs={{0,8},{8,0},{16,24},{24,16},{1,9},{9,1},{17,25},{25,17},{2,10},{10... | collective-permute-start | bytes 1327112 | tf_op jit(solution)/shard_map/ppermute | solution.py:556
  43.1 1.4 collective-permute-start.3
  61.2 3.5 %collective-permute-start.8 = (bf16[3,96,768]{2,1,0:T(8,128)(2,1)S(1)}, bf16[3,96,768]{2,1,0:T(8,128)(2,1)S(1)}, u32[]{:S(2)}, u32[]{:S(2)}) collective-permute-start(bf16[3,96,768]{2,1,0:T(8,128)(2,1)S(1)} %pad_maximum_fusion.7.rest_2_), channel_id=1, source_target_pairs={{0,1},{1,0},{2,3},{3,2},{4,5},{5,4},{6,7},{7,6},{8,9},{9,8},{10,11... | collective-permute-start | bytes 1327112 | tf_op jit(solution)/shard_map/ppermute | solution.py:560
  61.2 3.5 %collective-permute-start.9 = (bf16[3,96,768]{2,1,0:T(8,128)(2,1)}, bf16[3,96,768]{2,1,0:T(8,128)(2,1)S(1)}, u32[]{:S(2)}, u32[]{:S(2)}) collective-permute-start(bf16[3,96,768]{2,1,0:T(8,128)(2,1)} %collective-permute-done.4.rest_3_), channel_id=1, source_target_pairs={{0,1},{1,0},{2,3},{3,2},{4,5},{5,4},{6,7},{7,6},{8,9},{9,8},{10,11... | collective-permute-start | bytes 1327112 | tf_op jit(solution)/shard_map/ppermute | solution.py:560
  61.7 3.1 %collective-permute-start.10 = (bf16[3,96,768]{2,1,0:T(8,128)(2,1)}, bf16[3,96,768]{2,1,0:T(8,128)(2,1)S(1)}, u32[]{:S(2)}, u32[]{:S(2)}) collective-permute-start(bf16[3,96,768]{2,1,0:T(8,128)(2,1)} %collective-permute-done.5.rest_4_), channel_id=1, source_target_pairs={{0,1},{1,0},{2,3},{3,2},{4,5},{5,4},{6,7},{7,6},{8,9},{9,8},{10,11... | collective-permute-start | bytes 1327112 | tf_op jit(solution)/shard_map/ppermute | solution.py:560
  61.8 3.6 %collective-permute-start.11 = (bf16[3,96,768]{2,1,0:T(8,128)(2,1)}, bf16[3,96,768]{2,1,0:T(8,128)(2,1)S(1)}, u32[]{:S(2)}, u32[]{:S(2)}) collective-permute-start(bf16[3,96,768]{2,1,0:T(8,128)(2,1)} %collective-permute-done.6.rest_5_), channel_id=1, source_target_pairs={{0,1},{1,0},{2,3},{3,2},{4,5},{5,4},{6,7},{7,6},{8,9},{9,8},{10,11... | collective-permute-start | bytes 1327112 | tf_op jit(solution)/shard_map/ppermute | solution.py:560
  77.3 27.9 %collective-permute-start.15 = (bf16[4,256,384]{2,1,0:T(8,128)(2,1)}, bf16[4,256,384]{2,1,0:T(8,128)(2,1)S(1)}, u32[]{:S(2)}, u32[]{:S(2)}) collective-permute-start(bf16[4,256,384]{2,1,0:T(8,128)(2,1)} %get-tuple-element.80), channel_id=1, source_target_pairs={{0,8},{8,0},{16,24},{24,16},{1,9},{9,1},{17,25},{25,17},{2,10},{10... | collective-permute-start | bytes 2359304 | tf_op jit(solution)/shard_map/ppermute | solution.py:556
  78.8 36.3 %collective-permute-start.16 = (bf16[4,256,384]{2,1,0:T(8,128)(2,1)}, bf16[4,256,384]{2,1,0:T(8,128)(2,1)S(1)}, u32[]{:S(2)}, u32[]{:S(2)}) collective-permute-start(bf16[4,256,384]{2,1,0:T(8,128)(2,1)} %get-tuple-element.81), channel_id=1, source_target_pairs={{0,16},{8,24},{16,0},{24,8},{1,17},{9,25},{17,1},{25,9},{2,18},{10... | collective-permute-start | bytes 2359304 | tf_op jit(solution)/shard_map/ppermute | solution.py:556
  79.5 35.5 %collective-permute-start.17 = (bf16[4,256,384]{2,1,0:T(8,128)(2,1)}, bf16[4,256,384]{2,1,0:T(8,128)(2,1)S(1)}, u32[]{:S(2)}, u32[]{:S(2)}) collective-permute-start(bf16[4,256,384]{2,1,0:T(8,128)(2,1)} %get-tuple-element.82), channel_id=1, source_target_pairs={{0,24},{8,16},{16,8},{24,0},{1,25},{9,17},{17,9},{25,1},{2,26},{10... | collective-permute-start | bytes 2359304 | tf_op jit(solution)/shard_map/ppermute | solution.py:556
  89.8 26.7 %collective-permute-start.14 = (bf16[96,768]{1,0:T(8,128)(2,1)S(1)}, bf16[96,768]{1,0:T(8,128)(2,1)S(1)}, u32[]{:S(2)}, u32[]{:S(2)}) collective-permute-start(bf16[96,768]{1,0:T(8,128)(2,1)S(1)} %dynamic-slice_bitcast_fusion.6), channel_id=1, source_target_pairs={{0,6},{1,7},{2,4},{3,5},{4,2},{5,3},{6,0},{7,1},{8,14},{9,15},{10,... | collective-permute-start | bytes 442376 | tf_op jit(solution)/shard_map/ppermute | solution.py:560
  90.7 25.7 %collective-permute-start.13 = (bf16[96,768]{1,0:T(8,128)(2,1)S(1)}, bf16[96,768]{1,0:T(8,128)(2,1)S(1)}, u32[]{:S(2)}, u32[]{:S(2)}) collective-permute-start(bf16[96,768]{1,0:T(8,128)(2,1)S(1)} %dynamic-slice_bitcast_fusion.6), channel_id=1, source_target_pairs={{0,4},{1,5},{2,6},{3,7},{4,0},{5,1},{6,2},{7,3},{8,12},{9,13},{10,... | collective-permute-start | bytes 442376 | tf_op jit(solution)/shard_map/ppermute | solution.py:560
  105.2 11.2 %collective-permute-start.12 = (bf16[96,768]{1,0:T(8,128)(2,1)S(1)}, bf16[96,768]{1,0:T(8,128)(2,1)S(1)}, u32[]{:S(2)}, u32[]{:S(2)}) collective-permute-start(bf16[96,768]{1,0:T(8,128)(2,1)S(1)} %dynamic-slice_bitcast_fusion.6), channel_id=1, source_target_pairs={{0,2},{1,3},{2,0},{3,1},{4,6},{5,7},{6,4},{7,5},{8,10},{9,11},{10,... | collective-permute-start | bytes 442376 | tf_op jit(solution)/shard_map/ppermute | solution.py:560
  116.2 126.2 %reduce-scatter.5.cloned.1.call-start = ((), (), s32[]{:S(2)}) async-start(), calls=%async_computation.3 | async-start | bytes 5308416 | tf_op jit(solution)/shard_map/reduce_scatter | solution.py:789
  116.5 25.3 %copy-start.3 = (bf16[3,96,768]{2,1,0:T(8,128)(2,1)}, bf16[3,96,768]{2,1,0:T(8,128)(2,1)S(1)}, u32[]{:S(2)}) copy-start(bf16[3,96,768]{2,1,0:T(8,128)(2,1)S(1)} %pad_maximum_fusion.8.refs_2_) | copy-start | bytes 1327108
  116.5 25.1 %collective-permute-start.20 = (bf16[3,96,768]{2,1,0:T(8,128)(2,1)S(1)}, bf16[3,96,768]{2,1,0:T(8,128)(2,1)S(1)}, u32[]{:S(2)}, u32[]{:S(2)}) collective-permute-start(bf16[3,96,768]{2,1,0:T(8,128)(2,1)S(1)} %pad_maximum_fusion.8.refs_2_), channel_id=1, source_target_pairs={{0,24},{8,16},{16,8},{24,0},{1,25},{9,17},{17,9},{25,1},{2,26},{10... | collective-permute-start | bytes 1327112 | tf_op jit(solution)/shard_map/ppermute | solution.py:556
  118.0 23.7 %collective-permute-start.19 = (bf16[3,96,768]{2,1,0:T(8,128)(2,1)S(1)}, bf16[3,96,768]{2,1,0:T(8,128)(2,1)S(1)}, u32[]{:S(2)}, u32[]{:S(2)}) collective-permute-start(bf16[3,96,768]{2,1,0:T(8,128)(2,1)S(1)} %pad_maximum_fusion.8.refs_2_), channel_id=1, source_target_pairs={{0,16},{8,24},{16,0},{24,8},{1,17},{9,25},{17,1},{25,9},{2,18},{10... | collective-permute-start | bytes 1327112 | tf_op jit(solution)/shard_map/ppermute | solution.py:556
  118.3 23.3 %collective-permute-start.18 = (bf16[3,96,768]{2,1,0:T(8,128)(2,1)S(1)}, bf16[3,96,768]{2,1,0:T(8,128)(2,1)S(1)}, u32[]{:S(2)}, u32[]{:S(2)}) collective-permute-start(bf16[3,96,768]{2,1,0:T(8,128)(2,1)S(1)} %pad_maximum_fusion.8.refs_2_), channel_id=1, source_target_pairs={{0,8},{8,0},{16,24},{24,16},{1,9},{9,1},{17,25},{25,17},{2,10},{10... | collective-permute-start | bytes 1327112 | tf_op jit(solution)/shard_map/ppermute | solution.py:556
  141.7 6.3 %collective-permute-start.21 = (bf16[4,96,768]{2,1,0:T(8,128)(2,1)S(1)}, bf16[4,96,768]{2,1,0:T(8,128)(2,1)S(1)}, u32[]{:S(2)}, u32[]{:S(2)}) collective-permute-start(bf16[4,96,768]{2,1,0:T(8,128)(2,1)S(1)} %pad_maximum_fusion.5.refs_0_), channel_id=1, source_target_pairs={{0,1},{1,0},{2,3},{3,2},{4,5},{5,4},{6,7},{7,6},{8,9},{9,8},{10,11... | collective-permute-start | bytes 1769480 | tf_op jit(solution)/shard_map/ppermute | solution.py:560
  141.8 2.7 collective-permute-start.22
  142.3 2.9 collective-permute-start.23
  142.4 4.1 %collective-permute-start.24 = (bf16[3,96,768]{2,1,0:T(8,128)(2,1)S(1)}, bf16[3,96,768]{2,1,0:T(8,128)(2,1)S(1)}, u32[]{:S(2)}, u32[]{:S(2)}) collective-permute-start(bf16[3,96,768]{2,1,0:T(8,128)(2,1)S(1)} %collective-permute-done.19.refs_4_), channel_id=1, source_target_pairs={{0,1},{1,0},{2,3},{3,2},{4,5},{5,4},{6,7},{7,6},{8,9},{9,8},{10,11... | collective-permute-start | bytes 1327112 | tf_op jit(solution)/shard_map/ppermute | solution.py:560
  142.8 5.2 %collective-permute-start.25 = (bf16[3,96,768]{2,1,0:T(8,128)(2,1)S(1)}, bf16[3,96,768]{2,1,0:T(8,128)(2,1)S(1)}, u32[]{:S(2)}, u32[]{:S(2)}) collective-permute-start(bf16[3,96,768]{2,1,0:T(8,128)(2,1)S(1)} %collective-permute-done.20.refs_5_), channel_id=1, source_target_pairs={{0,1},{1,0},{2,3},{3,2},{4,5},{5,4},{6,7},{7,6},{8,9},{9,8},{10,11... | collective-permute-start | bytes 1327112 | tf_op jit(solution)/shard_map/ppermute | solution.py:560
  144.5 33.3 %collective-permute-start.26 = (bf16[4,256,384]{2,1,0:T(8,128)(2,1)}, bf16[4,256,384]{2,1,0:T(8,128)(2,1)S(1)}, u32[]{:S(2)}, u32[]{:S(2)}) collective-permute-start(bf16[4,256,384]{2,1,0:T(8,128)(2,1)} %get-tuple-element.96), channel_id=1, source_target_pairs={{0,8},{8,0},{16,24},{24,16},{1,9},{9,1},{17,25},{25,17},{2,10},{10... | collective-permute-start | bytes 2359304 | tf_op jit(solution)/shard_map/ppermute | solution.py:556
  145.2 36.6 %collective-permute-start.27 = (bf16[4,256,384]{2,1,0:T(8,128)(2,1)}, bf16[4,256,384]{2,1,0:T(8,128)(2,1)S(1)}, u32[]{:S(2)}, u32[]{:S(2)}) collective-permute-start(bf16[4,256,384]{2,1,0:T(8,128)(2,1)} %get-tuple-element.97), channel_id=1, source_target_pairs={{0,16},{8,24},{16,0},{24,8},{1,17},{9,25},{17,1},{25,9},{2,18},{10... | collective-permute-start | bytes 2359304 | tf_op jit(solution)/shard_map/ppermute | solution.py:556
  146.5 35.3 %collective-permute-start.28 = (bf16[4,256,384]{2,1,0:T(8,128)(2,1)}, bf16[4,256,384]{2,1,0:T(8,128)(2,1)S(1)}, u32[]{:S(2)}, u32[]{:S(2)}) collective-permute-start(bf16[4,256,384]{2,1,0:T(8,128)(2,1)} %get-tuple-element.98), channel_id=1, source_target_pairs={{0,24},{8,16},{16,8},{24,0},{1,25},{9,17},{17,9},{25,1},{2,26},{10... | collective-permute-start | bytes 2359304 | tf_op jit(solution)/shard_map/ppermute | solution.py:556
  198.5 6.0 %collective-permute-start.29 = (bf16[4,4,96,768]{3,2,1,0:T(8,128)(2,1)}, bf16[4,4,96,768]{3,2,1,0:T(8,128)(2,1)S(1)}, u32[]{:S(2)}, u32[]{:S(2)}) collective-permute-start(bf16[4,4,96,768]{3,2,1,0:T(8,128)(2,1)} %get-tuple-element.122), channel_id=1, source_target_pairs={{0,1},{1,0},{2,3},{3,2},{4,5},{5,4},{6,7},{7,6},{8,9},{9,8},{10,11... | collective-permute-start | bytes 7077896 | tf_op jit(solution)/shard_map/ppermute | solution.py:560
  198.6 5.0 %collective-permute-start.30 = (f32[4,8,768]{2,1,0:T(8,128)}, f32[4,8,768]{2,1,0:T(8,128)S(1)}, u32[]{:S(2)}, u32[]{:S(2)}) collective-permute-start(f32[4,8,768]{2,1,0:T(8,128)} %get-tuple-element.124), channel_id=1, source_target_pairs={{0,1},{1,0},{2,3},{3,2},{4,5},{5,4},{6,7},{7,6},{8,9},{9,8},{10,11... | collective-permute-start | bytes 294920 | tf_op jit(solution)/shard_map/ppermute | solution.py:560
  208.4 17.5 %collective-permute-start.31 = (bf16[4,104,768]{2,1,0:T(8,128)(2,1)}, bf16[4,104,768]{2,1,0:T(8,128)(2,1)}, u32[]{:S(2)}, u32[]{:S(2)}) collective-permute-start(bf16[4,104,768]{2,1,0:T(8,128)(2,1)} %get-tuple-element.134), channel_id=1, source_target_pairs={{0,8},{8,0},{16,24},{24,16},{1,9},{9,1},{17,25},{25,17},{2,10},{10... | collective-permute-start | bytes 1916936 | tf_op jit(solution)/shard_map/ppermute | solution.py:556
  209.4 29.9 %collective-permute-start.33 = (bf16[4,104,768]{2,1,0:T(8,128)(2,1)}, bf16[4,104,768]{2,1,0:T(8,128)(2,1)}, u32[]{:S(2)}, u32[]{:S(2)}) collective-permute-start(bf16[4,104,768]{2,1,0:T(8,128)(2,1)} %get-tuple-element.135), channel_id=1, source_target_pairs={{0,24},{8,16},{16,8},{24,0},{1,25},{9,17},{17,9},{25,1},{2,26},{10... | collective-permute-start | bytes 1916936 | tf_op jit(solution)/shard_map/ppermute | solution.py:556
  210.8 29.9 %collective-permute-start.32 = (bf16[4,104,768]{2,1,0:T(8,128)(2,1)}, bf16[4,104,768]{2,1,0:T(8,128)(2,1)}, u32[]{:S(2)}, u32[]{:S(2)}) collective-permute-start(bf16[4,104,768]{2,1,0:T(8,128)(2,1)} %get-tuple-element.136), channel_id=1, source_target_pairs={{0,16},{8,24},{16,0},{24,8},{1,17},{9,25},{17,1},{25,9},{2,18},{10... | collective-permute-start | bytes 1916936 | tf_op jit(solution)/shard_map/ppermute | solution.py:556
  242.4 19.3 %copy-start.1 = (bf16[1,4,96,768]{3,2,1,0:T(8,128)(2,1)S(1)}, bf16[1,4,96,768]{3,2,1,0:T(8,128)(2,1)}, u32[]{:S(2)}) copy-start(bf16[1,4,96,768]{3,2,1,0:T(8,128)(2,1)} %reduce-scatter.3.cloned.1.call-done) | copy-start | bytes 1769476
  242.5 6.9 %collective-permute-start.34 = (bf16[104,768]{1,0:T(8,128)(2,1)S(1)}, bf16[104,768]{1,0:T(8,128)(2,1)S(1)}, u32[]{:S(2)}, u32[]{:S(2)}) collective-permute-start(bf16[104,768]{1,0:T(8,128)(2,1)S(1)} %get-tuple-element.145), channel_id=1, source_target_pairs={{0,2},{1,3},{2,0},{3,1},{4,6},{5,7},{6,4},{7,5},{8,10},{9,11},{10,... | collective-permute-start | bytes 479240 | tf_op jit(solution)/shard_map/ppermute | solution.py:560
  242.6 9.4 %collective-permute-start.36 = (bf16[104,768]{1,0:T(8,128)(2,1)S(1)}, bf16[104,768]{1,0:T(8,128)(2,1)S(1)}, u32[]{:S(2)}, u32[]{:S(2)}) collective-permute-start(bf16[104,768]{1,0:T(8,128)(2,1)S(1)} %get-tuple-element.146), channel_id=1, source_target_pairs={{0,6},{1,7},{2,4},{3,5},{4,2},{5,3},{6,0},{7,1},{8,14},{9,15},{10,... | collective-permute-start | bytes 479240 | tf_op jit(solution)/shard_map/ppermute | solution.py:560
  244.7 13.3 %collective-permute-start.35 = (bf16[104,768]{1,0:T(8,128)(2,1)S(1)}, bf16[104,768]{1,0:T(8,128)(2,1)S(1)}, u32[]{:S(2)}, u32[]{:S(2)}) collective-permute-start(bf16[104,768]{1,0:T(8,128)(2,1)S(1)} %get-tuple-element.147), channel_id=1, source_target_pairs={{0,4},{1,5},{2,6},{3,7},{4,0},{5,1},{6,2},{7,3},{8,12},{9,13},{10,... | collective-permute-start | bytes 479240 | tf_op jit(solution)/shard_map/ppermute | solution.py:560
  247.2 12.5 %collective-permute-start.42 = (bf16[2,96,768]{2,1,0:T(8,128)(2,1)S(1)}, bf16[2,96,768]{2,1,0:T(8,128)(2,1)S(1)}, u32[]{:S(2)}, u32[]{:S(2)}) collective-permute-start(bf16[2,96,768]{2,1,0:T(8,128)(2,1)S(1)} %get-tuple-element.154), channel_id=1, source_target_pairs={{0,16},{8,24},{16,0},{24,8},{1,17},{9,25},{17,1},{25,9},{2,18},{10... | collective-permute-start | bytes 884744 | tf_op jit(solution)/shard_map/ppermute | solution.py:556
  248.4 12.1 %collective-permute-start.40 = (bf16[2,96,768]{2,1,0:T(8,128)(2,1)S(1)}, bf16[2,96,768]{2,1,0:T(8,128)(2,1)S(1)}, u32[]{:S(2)}, u32[]{:S(2)}) collective-permute-start(bf16[2,96,768]{2,1,0:T(8,128)(2,1)S(1)} %get-tuple-element.155), channel_id=1, source_target_pairs={{0,8},{8,0},{16,24},{24,16},{1,9},{9,1},{17,25},{25,17},{2,10},{10... | collective-permute-start | bytes 884744 | tf_op jit(solution)/shard_map/ppermute | solution.py:556
  249.4 12.5 %collective-permute-start.46 = (bf16[2,96,768]{2,1,0:T(8,128)(2,1)S(1)}, bf16[2,96,768]{2,1,0:T(8,128)(2,1)S(1)}, u32[]{:S(2)}, u32[]{:S(2)}) collective-permute-start(bf16[2,96,768]{2,1,0:T(8,128)(2,1)S(1)} %get-tuple-element.150), channel_id=1, source_target_pairs={{0,16},{8,24},{16,0},{24,8},{1,17},{9,25},{17,1},{25,9},{2,18},{10... | collective-permute-start | bytes 884744 | tf_op jit(solution)/shard_map/ppermute | solution.py:556
  252.0 10.8 %collective-permute-start.44 = (bf16[2,96,768]{2,1,0:T(8,128)(2,1)S(1)}, bf16[2,96,768]{2,1,0:T(8,128)(2,1)S(1)}, u32[]{:S(2)}, u32[]{:S(2)}) collective-permute-start(bf16[2,96,768]{2,1,0:T(8,128)(2,1)S(1)} %get-tuple-element.151), channel_id=1, source_target_pairs={{0,8},{8,0},{16,24},{24,16},{1,9},{9,1},{17,25},{25,17},{2,10},{10... | collective-permute-start | bytes 884744 | tf_op jit(solution)/shard_map/ppermute | solution.py:556
  258.0 8.0 %collective-permute-start.39 = (bf16[104,768]{1,0:T(8,128)(2,1)S(1)}, bf16[104,768]{1,0:T(8,128)(2,1)S(1)}, u32[]{:S(2)}, u32[]{:S(2)}) collective-permute-start(bf16[104,768]{1,0:T(8,128)(2,1)S(1)} %fusion.7), channel_id=1, source_target_pairs={{0,24},{8,16},{16,8},{24,0},{1,25},{9,17},{17,9},{25,1},{2,26},{10... | collective-permute-start | bytes 479240 | tf_op jit(solution)/shard_map/ppermute | solution.py:556
  259.6 8.5 %collective-permute-start.38 = (bf16[104,768]{1,0:T(8,128)(2,1)S(1)}, bf16[104,768]{1,0:T(8,128)(2,1)S(1)}, u32[]{:S(2)}, u32[]{:S(2)}) collective-permute-start(bf16[104,768]{1,0:T(8,128)(2,1)S(1)} %fusion.7), channel_id=1, source_target_pairs={{0,16},{8,24},{16,0},{24,8},{1,17},{9,25},{17,1},{25,9},{2,18},{10... | collective-permute-start | bytes 479240 | tf_op jit(solution)/shard_map/ppermute | solution.py:556
  260.5 9.6 %collective-permute-start.37 = (bf16[104,768]{1,0:T(8,128)(2,1)S(1)}, bf16[104,768]{1,0:T(8,128)(2,1)S(1)}, u32[]{:S(2)}, u32[]{:S(2)}) collective-permute-start(bf16[104,768]{1,0:T(8,128)(2,1)S(1)} %fusion.7), channel_id=1, source_target_pairs={{0,8},{8,0},{16,24},{24,16},{1,9},{9,1},{17,25},{25,17},{2,10},{10... | collective-permute-start | bytes 479240 | tf_op jit(solution)/shard_map/ppermute | solution.py:556
  261.9 8.4 %copy-start.4 = (bf16[2,96,768]{2,1,0:T(8,128)(2,1)}, bf16[2,96,768]{2,1,0:T(8,128)(2,1)S(1)}, u32[]{:S(2)}) copy-start(bf16[2,96,768]{2,1,0:T(8,128)(2,1)S(1)} %get-tuple-element.152.refs_2_) | copy-start | bytes 884740
  261.9 8.4 %copy-start.5 = (bf16[2,96,768]{2,1,0:T(8,128)(2,1)}, bf16[2,96,768]{2,1,0:T(8,128)(2,1)S(1)}, u32[]{:S(2)}) copy-start(bf16[2,96,768]{2,1,0:T(8,128)(2,1)S(1)} %get-tuple-element.153.refs_0_) | copy-start | bytes 884740
  261.9 14.5 %collective-permute-start.43 = (bf16[2,96,768]{2,1,0:T(8,128)(2,1)S(1)}, bf16[2,96,768]{2,1,0:T(8,128)(2,1)S(1)}, u32[]{:S(2)}, u32[]{:S(2)}) collective-permute-start(bf16[2,96,768]{2,1,0:T(8,128)(2,1)S(1)} %get-tuple-element.152.refs_2_), channel_id=1, source_target_pairs={{0,8},{8,0},{16,24},{24,16},{1,9},{9,1},{17,25},{25,17},{2,10},{10... | collective-permute-start | bytes 884744 | tf_op jit(solution)/shard_map/ppermute | solution.py:556
  262.8 13.6 %collective-permute-start.41 = (bf16[2,96,768]{2,1,0:T(8,128)(2,1)S(1)}, bf16[2,96,768]{2,1,0:T(8,128)(2,1)S(1)}, u32[]{:S(2)}, u32[]{:S(2)}) collective-permute-start(bf16[2,96,768]{2,1,0:T(8,128)(2,1)S(1)} %get-tuple-element.153.refs_0_), channel_id=1, source_target_pairs={{0,16},{8,24},{16,0},{24,8},{1,17},{9,25},{17,1},{25,9},{2,18},{10... | collective-permute-start | bytes 884744 | tf_op jit(solution)/shard_map/ppermute | solution.py:556
  266.0 14.8 %collective-permute-start.47 = (bf16[2,96,768]{2,1,0:T(8,128)(2,1)S(1)}, bf16[2,96,768]{2,1,0:T(8,128)(2,1)S(1)}, u32[]{:S(2)}, u32[]{:S(2)}) collective-permute-start(bf16[2,96,768]{2,1,0:T(8,128)(2,1)S(1)} %get-tuple-element.148.refs_6_), channel_id=1, source_target_pairs={{0,8},{8,0},{16,24},{24,16},{1,9},{9,1},{17,25},{25,17},{2,10},{10... | collective-permute-start | bytes 884744 | tf_op jit(solution)/shard_map/ppermute | solution.py:556
  268.2 12.7 %collective-permute-start.45 = (bf16[2,96,768]{2,1,0:T(8,128)(2,1)S(1)}, bf16[2,96,768]{2,1,0:T(8,128)(2,1)S(1)}, u32[]{:S(2)}, u32[]{:S(2)}) collective-permute-start(bf16[2,96,768]{2,1,0:T(8,128)(2,1)S(1)} %get-tuple-element.149.refs_4_), channel_id=1, source_target_pairs={{0,16},{8,24},{16,0},{24,8},{1,17},{9,25},{17,1},{25,9},{2,18},{10... | collective-permute-start | bytes 884744 | tf_op jit(solution)/shard_map/ppermute | solution.py:556
  271.4 14.2 %copy-start.32 = (f32[96]{0:T(128)}, f32[96]{0:T(128)S(1)}, u32[]{:S(2)}) copy-start(f32[96]{0:T(128)S(1)} %get-tuple-element.197) | copy-start | bytes 1156
  (30 other events, 100.0 us)
Sparse Core Ops, SparseCore 0:
  37.9 51.8 all-gather.2
  115.2 54.0 reduce-scatter.2
  182.0 54.0 reduce-scatter.4
